TPU v7x, 32 devices: a whole 2x2x4 slice. The times are simulated.
32 devices in a mesh: dp: 4 (over x, core), seq: 8 (over z, y).
Axes of the slice: x: 2, y: 2, z: 4, core: 2. Of those that a mesh axis runs over, the one named last changes fastest.
Arguments:
- tokens: bfloat16 [16384, 1536], P(('dp', 'seq')), may hold values from -6 to 6
- segment_ids: int32 [16384], P(('dp', 'seq')), may hold values from 0 to 31, never falling along the last dimension, each value on 1 to 1024 neighbouring positions
- in_proj: bfloat16 [1536, 6448], P(('dp', 'seq')), may hold values from -0.15625 to 0.15625
- conv_weight: bfloat16 [4, 3328], P(None, ('dp', 'seq')), may hold values from -3 to 3
- conv_bias: bfloat16 [3328], P(('dp', 'seq')), may hold values from -2 to 2
- out_proj: bfloat16 [3072, 1536], P(('dp', 'seq')), may hold values from -0.109375 to 0.109375
- norm_gain: bfloat16 [1536], P(('dp', 'seq')), may hold values from 0.099609375 to 1.8984375
- gate_gain: bfloat16 [3072], P(('dp', 'seq')), may hold values from 0.099609375 to 1.8984375
- a_log: float32 [48], replicated, may hold values from -4 to 1.5
- dt_bias: float32 [48], replicated, may hold values from -7 to -3
- skip_d: float32 [48], replicated, may hold values from 0.5 to 1.5
- cotangent: bfloat16 [16384, 1536], P(('dp', 'seq')), may hold values from -6 to 6
Outputs:
- output: bfloat16 [16384, 1536], P(('dp', 'seq'))
- grad_tokens: float32 [16384, 1536], P(('dp', 'seq'))
- grad_in_proj: float32 [1536, 6448], P(('dp', 'seq'))
- grad_conv_weight: float32 [4, 3328], P(None, ('dp', 'seq'))
- grad_conv_bias: float32 [3328], P(('dp', 'seq'))
- grad_out_proj: float32 [3072, 1536], P(('dp', 'seq'))
- grad_norm_gain: float32 [1536], P(('dp', 'seq'))
- grad_gate_gain: float32 [3072], P(('dp', 'seq'))
- grad_a_log: float32 [48], replicated
- grad_dt_bias: float32 [48], replicated
- grad_skip_d: float32 [48], replicated
Inputs may be any that keep to these rules, and one draw needn't show every extreme that they name: `segment_ids`: segment ids never fall along the tokens; each segment holds 1 to 1024 tokens and one holds exactly 1024.
All inputs are finite; a program needn't handle non-finite values.
Results may differ from a plain program's by a relative error of at most 0.0088.
Values may be sent and summed in bfloat16 or wider, within the bound.
No kernel may reach another device: no remote copies, remote signals or barrier semaphores. Data moves between devices by JAX's collectives and lax.ppermute only.
A program may use at most 256 MiB of HBM per device.

v0:
```python
from functools import partial

import jax
import jax.numpy as jnp
from jax import lax
from jax.sharding import PartitionSpec as P

INNER = 3072
HEADDIM = 64
STATE = 128
CONV = 4
GROUP = 256
HEADS = 48
XBC = 3328


EPSILON = 1e-05
PRECISE = lax.Precision.HIGHEST


def passed_along(block, axis, distance):
    devices = range(lax.axis_size(axis))
    route = [(i - distance, i) for i in devices if i - distance in devices]
    return lax.ppermute(block, axis, route)


def prefix(array, axis, join, neutral):
    place = lax.axis_index(axis)
    gathered = jax.tree.map(
        lambda a, kind: lax.all_gather(a.astype(kind), axis), array, (jnp.bfloat16, jnp.bfloat16)
    )
    state = jax.tree.map(lambda a, e: jnp.zeros_like(a) + jnp.asarray(e, a.dtype), array, neutral)

    def one(hop, state):
        return join(
            state,
            jax.tree.map(
                lambda a, own: lax.dynamic_index_in_dim(a, hop, 0, False).astype(own.dtype),
                gathered,
                array,
            ),
        )

    return lax.fori_loop(0, place, one, state)


def carried_in(array, axis, combine, identity):
    count, index = (lax.axis_size(axis), lax.axis_index(axis))
    everything = jax.tree.map(
        lambda part, kind: lax.all_gather(part.astype(kind), axis),
        array,
        jax.tree.map(lambda a: jnp.bfloat16 if a.dtype == jnp.float32 else a.dtype, array),
    )
    start = jax.tree.map(
        lambda part, zero: jnp.broadcast_to(jnp.asarray(zero, part.dtype), part.shape),
        array,
        identity,
    )

    def hop(k, before):
        at = count - 1 - k
        reached = at > index
        new = combine(
            before, jax.tree.map(lambda part, own: part[at].astype(own.dtype), everything, array)
        )
        return jax.tree.map(lambda a, b: jnp.where(reached, a, b), new, before)

    return lax.fori_loop(0, count, hop, start)


def rms_scale(values, gain):
    return values * lax.rsqrt(jnp.mean(values * values, axis=-1, keepdims=True) + EPSILON) * gain


def gated_norm(mixed_y, gate_z, gain):
    return rms_scale(mixed_y * jax.nn.silu(gate_z), gain)


def convolve(extended, ext_ids, kernel, bias_term):
    count_rows = extended.shape[0] - (CONV - 1)
    summed = bias_term + kernel[CONV - 1] * extended[CONV - 1 :]
    for offset in range(1, CONV):
        begin = CONV - 1 - offset
        same_seg = ext_ids[begin : begin + count_rows] == ext_ids[CONV - 1 :]
        summed = summed + jnp.where(
            same_seg[:, None], kernel[CONV - 1 - offset] * extended[begin : begin + count_rows], 0.0
        )
    return jax.nn.silu(summed)


def group_step(running, inputs):
    carry_state, prev_seg = running
    values_x, keys_b, reads_c, step_dt, decay_log, seg_ids = inputs
    cumulative = jnp.cumsum(decay_log, axis=0)
    heads_cum = cumulative.T
    positions = jnp.arange(seg_ids.shape[0])
    inside = (seg_ids[:, None] == seg_ids[None, :]) & (positions[:, None] >= positions[None, :])
    spread_log = jnp.where(inside[None, :, :], heads_cum[:, :, None] - heads_cum[:, None, :], 0.0)
    decays = jnp.where(inside[None, :, :], jnp.exp(spread_log), 0.0)
    scores = jnp.dot(reads_c, keys_b.T, precision=PRECISE)
    mixing = scores[None, :, :] * decays * step_dt.T[:, None, :]
    within = jnp.einsum("hij,jhp->ihp", mixing, values_x, precision=PRECISE)
    carried = jnp.where((seg_ids == prev_seg)[:, None], jnp.exp(cumulative), 0.0)
    from_state = (
        jnp.einsum("in,hpn->ihp", reads_c, carry_state, precision=PRECISE) * carried[:, :, None]
    )
    final_seg = seg_ids[-1]
    weights_end = (
        jnp.where(
            (seg_ids == final_seg)[:, None], jnp.exp(cumulative[-1][None, :] - cumulative), 0.0
        )
        * step_dt
    )
    added_state = jnp.einsum("jh,jhp,jn->hpn", weights_end, values_x, keys_b, precision=PRECISE)
    retain = jnp.where(final_seg == prev_seg, jnp.exp(cumulative[-1]), 0.0)
    new_state = retain[:, None, None] * carry_state + added_state
    return ((new_state, final_seg), within + from_state)


def split_inputs(conv_out, dt_raw, a_log, dt_bias):
    values_x = conv_out[:, :INNER].reshape(-1, HEADS, HEADDIM)
    keys_b = conv_out[:, INNER : INNER + STATE]
    reads_c = conv_out[:, INNER + STATE :]
    step_dt = jax.nn.softplus(dt_raw + dt_bias)
    decay_log = -jnp.exp(a_log) * step_dt
    return (values_x, keys_b, reads_c, step_dt, decay_log)


def local_pass(values_x, keys_b, reads_c, step_dt, decay_log, seg_ids, prev_seg):
    blocks = values_x.shape[0] // GROUP
    pieces = tuple(
        (
            item.reshape((blocks, GROUP) + item.shape[1:])
            for item in (values_x, keys_b, reads_c, step_dt, decay_log, seg_ids)
        )
    )
    start = (jnp.zeros((HEADS, HEADDIM, STATE), jnp.float32), prev_seg)
    (own_state, _), mixed_y = lax.scan(jax.checkpoint(group_step), start, pieces)
    return (mixed_y.reshape(values_x.shape), own_state)


def device_terms(decay_log, seg_ids, prev_seg):
    cumulative = jnp.cumsum(decay_log, axis=0)
    reach = jnp.where((seg_ids == prev_seg)[:, None], jnp.exp(cumulative), 0.0)
    device_decay = jnp.where(seg_ids[-1] == prev_seg, jnp.exp(cumulative[-1]), 0.0)
    return (reach, device_decay)


def finish(mixed_y, values_x, reads_c, reach, incoming, skip_d):
    from_state = jnp.einsum("in,hpn->ihp", reads_c, incoming, precision=PRECISE) * reach[:, :, None]
    return (mixed_y + from_state + skip_d[None, :, None] * values_x).reshape(
        mixed_y.shape[0], INNER
    )


def ssd_full(seg_ids, prev_seg, conv_out, dt_raw, a_log, dt_bias, skip_d, incoming):
    values_x, keys_b, reads_c, step_dt, decay_log = split_inputs(conv_out, dt_raw, a_log, dt_bias)
    mixed_y, own_state = local_pass(
        values_x, keys_b, reads_c, step_dt, decay_log, seg_ids, prev_seg
    )
    reach, device_decay = device_terms(decay_log, seg_ids, prev_seg)
    mixed_y = finish(mixed_y, values_x, reads_c, reach, incoming, skip_d)
    return (mixed_y, device_decay[:, None, None] * incoming + own_state)


def link(earlier, later):
    return (earlier[0] * later[0], later[0][:, None, None] * earlier[1] + later[1])


def on_device(
    tokens,
    segment_ids,
    in_proj,
    conv_weight,
    conv_bias,
    out_proj,
    norm_gain,
    gate_gain,
    a_log,
    dt_bias,
    skip_d,
    cotangent,
):
    gathered = (
        lax.all_gather(in_proj, ("dp", "seq"), axis=0, tiled=True),
        lax.all_gather(conv_weight, ("dp", "seq"), axis=1, tiled=True),
        lax.all_gather(conv_bias, ("dp", "seq"), axis=0, tiled=True),
        lax.all_gather(out_proj, ("dp", "seq"), axis=0, tiled=True),
        lax.all_gather(norm_gain, ("dp", "seq"), axis=0, tiled=True),
        lax.all_gather(gate_gain, ("dp", "seq"), axis=0, tiled=True),
    )
    w_in, w_conv, b_conv, w_out, g_norm, g_gate = gathered
    count_rows = tokens.shape[0]
    stream = tokens.astype(jnp.float32)
    gain_in = g_norm.astype(jnp.float32)
    gain_out = g_gate.astype(jnp.float32)
    kernel = w_conv.astype(jnp.float32)
    bias_term = b_conv.astype(jnp.float32)
    normed_in = rms_scale(stream, gain_in).astype(jnp.bfloat16)
    projected = jnp.dot(normed_in, w_in, preferred_element_type=jnp.float32)
    gate_z = projected[:, :INNER]
    raw_xbc = projected[:, INNER : INNER + XBC].astype(jnp.bfloat16)
    dt_raw = projected[:, INNER + XBC :]
    own_ids = segment_ids % 64
    edge_rows, edge_ids = passed_along(
        (
            raw_xbc[count_rows - (CONV - 1) :],
            own_ids[count_rows - (CONV - 1) :].astype(jnp.bfloat16),
        ),
        "seq",
        1,
    )
    extended = jnp.concatenate([edge_rows, raw_xbc], 0).astype(jnp.float32)
    ext_ids = jnp.concatenate([edge_ids.astype(jnp.int32), own_ids], 0)
    prev_seg = jnp.where(ext_ids[CONV - 2] == own_ids[0], segment_ids[0], segment_ids[0] - 1)
    conv_out = convolve(extended, ext_ids, kernel, bias_term)
    values_x, keys_b, reads_c, step_dt, decay_log = split_inputs(conv_out, dt_raw, a_log, dt_bias)
    mixed_y, own_state = local_pass(
        values_x, keys_b, reads_c, step_dt, decay_log, segment_ids, prev_seg
    )
    reach, device_decay = device_terms(decay_log, segment_ids, prev_seg)
    identity = (jnp.ones_like(device_decay), jnp.zeros_like(own_state))
    incoming = prefix((device_decay, own_state), "seq", link, identity)[1]
    full_y = finish(mixed_y, values_x, reads_c, reach, incoming, skip_d)
    normed_out = gated_norm(full_y, gate_z, gain_out).astype(jnp.bfloat16)
    output = (stream + jnp.dot(normed_out, w_out, preferred_element_type=jnp.float32)).astype(
        jnp.bfloat16
    )
    again = (
        lax.all_gather(in_proj, ("dp", "seq"), axis=0, tiled=True),
        lax.all_gather(conv_weight, ("dp", "seq"), axis=1, tiled=True),
        lax.all_gather(conv_bias, ("dp", "seq"), axis=0, tiled=True),
        lax.all_gather(out_proj, ("dp", "seq"), axis=0, tiled=True),
        lax.all_gather(norm_gain, ("dp", "seq"), axis=0, tiled=True),
        lax.all_gather(gate_gain, ("dp", "seq"), axis=0, tiled=True),
    )
    back_in = again[0]
    back_kernel = again[1].astype(jnp.float32)
    back_bias = again[2].astype(jnp.float32)
    back_out = again[3]
    back_norm = again[4].astype(jnp.float32)
    back_gate = again[5].astype(jnp.float32)
    d_normed = jnp.dot(cotangent, back_out.T, preferred_element_type=jnp.float32)
    _, pull_post = jax.vjp(gated_norm, full_y, gate_z, back_gate)
    d_mixed, d_gate, grad_gate_gain = pull_post(d_normed)
    local_pull = jnp.einsum(
        "ih,ihp,in->hpn",
        reach,
        d_mixed.reshape(count_rows, HEADS, HEADDIM),
        reads_c,
        precision=PRECISE,
    )
    later_pull = carried_in((device_decay, local_pull), "seq", link, identity)[1]
    _, pull_ssd = jax.vjp(
        partial(ssd_full, segment_ids, prev_seg), conv_out, dt_raw, a_log, dt_bias, skip_d, incoming
    )
    d_conv_out, d_dt_raw, grad_a_log, grad_dt_bias, grad_skip_d, _ = pull_ssd((d_mixed, later_pull))

    def conv_piece(ext_values, kernel_values, bias_values):
        return convolve(ext_values, ext_ids, kernel_values, bias_values)

    _, pull_conv = jax.vjp(conv_piece, extended, back_kernel, back_bias)
    d_extended, grad_conv_weight, grad_conv_bias = pull_conv(d_conv_out)
    spill = passed_along(d_extended[: CONV - 1].astype(jnp.bfloat16), "seq", -1).astype(jnp.float32)
    d_raw = d_extended[CONV - 1 :] + jnp.pad(spill, ((count_rows - (CONV - 1), 0), (0, 0)))
    d_projected = jnp.concatenate([d_gate, d_raw, d_dt_raw], 1).astype(jnp.bfloat16)
    d_normed_in = jnp.dot(d_projected, back_in.T, preferred_element_type=jnp.float32)
    _, pull_pre = jax.vjp(rms_scale, stream, back_norm)
    d_stream, grad_norm_gain = pull_pre(d_normed_in)
    grad_tokens = cotangent.astype(jnp.float32) + d_stream
    grad_in_proj = jnp.dot(normed_in.T, d_projected, preferred_element_type=jnp.float32)
    grad_out_proj = jnp.dot(normed_out.T, cotangent, preferred_element_type=jnp.float32)
    shares = (
        lax.psum_scatter(grad_in_proj, ("dp", "seq"), scatter_dimension=0, tiled=True),
        lax.psum_scatter(grad_conv_weight, ("dp", "seq"), scatter_dimension=1, tiled=True),
        lax.psum_scatter(grad_conv_bias, ("dp", "seq"), scatter_dimension=0, tiled=True),
        lax.psum_scatter(grad_out_proj, ("dp", "seq"), scatter_dimension=0, tiled=True),
        lax.psum_scatter(grad_norm_gain, ("dp", "seq"), scatter_dimension=0, tiled=True),
        lax.psum_scatter(grad_gate_gain, ("dp", "seq"), scatter_dimension=0, tiled=True),
    )
    head_sums = lax.psum((grad_a_log, grad_dt_bias, grad_skip_d), ("dp", "seq"))
    return (output, grad_tokens) + tuple(shares) + tuple(head_sums)


def solution(mesh):
    in_specs = (
        P(("dp", "seq"), None),
        P(("dp", "seq")),
        P(("dp", "seq"), None),
        P(None, ("dp", "seq")),
        P(("dp", "seq")),
        P(("dp", "seq"), None),
        P(("dp", "seq")),
        P(("dp", "seq")),
        P(),
        P(),
        P(),
        P(("dp", "seq"), None),
    )
    out_specs = (
        P(("dp", "seq"), None),
        P(("dp", "seq"), None),
        P(("dp", "seq"), None),
        P(None, ("dp", "seq")),
        P(("dp", "seq")),
        P(("dp", "seq"), None),
        P(("dp", "seq")),
        P(("dp", "seq")),
        P(),
        P(),
        P(),
    )
    return jax.shard_map(
        on_device, mesh=mesh, in_specs=in_specs, out_specs=out_specs, check_vma=False
    )
```

profile of v0, /device:TPU:0, one launch (start us, length us, event | category | flops | bytes accessed | tf_op | source)
XLA Modules:
  0.0 1960.3 jit_solution(1386145645736008974)
XLA Ops:
  17.3 42.1 %all-reduce.23 = (bf16[1536]{0:T(1024)(128)(2,1)S(1)}, bf16[3328]{0:T(1024)(128)(2,1)S(1)}, bf16[3072]{0:T(1024)(128)(2,1)}) all-reduce(bf16[1536]{0:T(1024)(128)(2,1)S(1)} %dynamic-update-slice, bf16[3328]{0:T(1024)(128)(2,1)S(1)} %dynamic-update-slice.1, ...), channel_id=1, replica_groups=mesh['dp'=4,'seq'=8] {'dp','seq'}, use_global_device_ids=true, to_apply=%add.15 | all-reduce | flops 7936 | bytes 31744
  60.1 67.4 %all-gather.2 = bf16[32,104,4]{1,2,0:T(4,128)(2,1)S(1)} all-gather(bf16[1,104,4]{1,2,0:T(4,128)(2,1)} %bitcast.557), channel_id=1, replica_groups=mesh['dp'=4,'seq'=8] {'dp','seq'}, dimensions={0}, use_global_device_ids=true | all-gather | bytes 27456 | tf_op jit(solution)/shard_map/all_gather | solution.py:186
  145.3 17.3 fusion.159
  216.6 195.6 %while.87 = (s32[]{:T(128)}, f32[48,64,128]{2,1,0:T(8,128)}, s32[]{:T(128)}, f32[2,256,48,64]{1,0,3,2:T(2,128)}, s32[2,256]{1,0:T(2,128)S(1)}, /*index=5*/f32[2,...) while((s32[]{:T(128)}, f32[48,64,128]{2,1,0:T(8,128)}, ...), condition=%wide.region_4.5_spmd.clone, body=%wide.region_1.4_spmd.clone.sunk | while | flops 4953994240 | bytes 53998032 | solution.py:138
  222.5 16.3 fusion.262
  249.6 63.3 %dynamic_update_slice.83 = f32[2,256,48,64]{1,0,3,2:T(2,128)} dynamic-update-slice(f32[2,256,48,64]{1,0,3,2:T(2,128)} %get-tuple-element.1545, f32[1,256,48,64]{1,0,3,2:T(1,128)S(1)} %copy.499, s32[]{:T(128)S(6)} %copy.518, s32[]{:T(128)} %constant.236.clone.1..sunk.2, s32[]{:T(128)} %constant.236.clone.1..sunk.2, s32[]{:T(128)} %constant.236.clone.1..sunk.2) | dynamic-update-slice | bytes 6291460 | tf_op jit(solution)/shard_map/while/body/jit(dynamic_update_index_in_dim)/dynamic_update_slice | solution.py:138
  319.1 16.3 fusion.262
  348.2 63.3 %dynamic_update_slice.83 = f32[2,256,48,64]{1,0,3,2:T(2,128)} dynamic-update-slice(f32[2,256,48,64]{1,0,3,2:T(2,128)} %get-tuple-element.1545, f32[1,256,48,64]{1,0,3,2:T(1,128)S(1)} %copy.499, s32[]{:T(128)S(6)} %copy.518, s32[]{:T(128)} %constant.236.clone.1..sunk.2, s32[]{:T(128)} %constant.236.clone.1..sunk.2, s32[]{:T(128)} %constant.236.clone.1..sunk.2) | dynamic-update-slice | bytes 6291460 | tf_op jit(solution)/shard_map/while/body/jit(dynamic_update_index_in_dim)/dynamic_update_slice | solution.py:138
  420.1 16.5 all-gather.3
  445.7 66.0 %all-gather.13.cloned.1.call-done = bf16[384,64,128]{2,1,0:T(8,128)(2,1)} async-done(((bf16[48,64,128]{2,1,0:T(8,128)(2,1)}), bf16[384,64,128]{2,1,0:T(8,128)(2,1)}) %all-gather.13.cloned.1.call-update) | async-done | bytes 6291472 | tf_op jit(solution)/shard_map/all_gather | solution.py:30
  512.6 11.1 multiply_add_fusion.4
  531.8 63.1 %all-gather.11.cloned.1.call-done = bf16[3072,1536]{1,0:T(8,128)(2,1)} async-done(((bf16[96,1536]{1,0:T(8,128)(2,1)}), bf16[3072,1536]{1,0:T(8,128)(2,1)}) %all-gather.11.cloned.1.call-update) | async-done | bytes 9437200 | tf_op jit(solution)/shard_map/all_gather | solution.py:188
  594.9 12.7 multiply_reduce_fusion.10
  628.7 32.0 %while.89 = (s32[]{:T(128)}, f32[48,64,128]{2,1,0:T(8,128)S(1)}, s32[]{:T(128)}, f32[2,48,64,128]{3,2,1,0:T(8,128)}, s32[2]{0:T(128)S(1)}, /*index=5*/s32[2,256]...) while((s32[]{:T(128)}, f32[48,64,128]{2,1,0:T(8,128)S(1)}, ...), condition=%wide.region_16.17_spmd.clone, body=%wide.region_13.16_spmd.clone.sunk | while | flops 1211941376 | bytes 10084377 | solution.py:138
  676.7 47.4 %all-gather.15.cloned.1.call-done = bf16[384,64,128]{2,1,0:T(8,128)(2,1)} async-done(((bf16[48,64,128]{2,1,0:T(8,128)(2,1)}), bf16[384,64,128]{2,1,0:T(8,128)(2,1)}) %all-gather.15.cloned.1.call-update) | async-done | bytes 6291472 | tf_op jit(solution)/shard_map/all_gather | solution.py:50
  724.1 18.1 while.88
  758.9 387.4 %while.86 = (s32[]{:T(128)}, f32[48,64,128]{2,1,0:T(8,128)S(1)}, f32[2,256,48,64]{1,0,3,2:T(2,128)}, f32[2,256,128]{2,1,0:T(8,128)}, f32[2,256,128]{2,1,0:T(8,12...) while((s32[]{:T(128)}, f32[48,64,128]{2,1,0:T(8,128)S(1)}, ...), condition=%wide.region_29.30_spmd, body=%wide.region_17.29_spmd.sunk | while | flops 11248779264 | bytes 134855952 | solution.py:138
  796.8 22.7 %fusion.245 = (f32[48,256]{1,0:T(8,128)}, f32[48,256]{1,0:T(8,128)}, f32[48,256]{1,0:T(8,128)}, f32[256,256]{1,0:T(8,128)}) fusion(f32[48,256]{1,0:T(8,128)} %copy.484, f32[48,256]{1,0:T(8,128)} %copy_bitcast_fusion.19, f32[256,256]{1,0:T(8,128)S(1)} %fusion.243, pred[256,256]{1,0:T(8,128)(4,1)} %fusion.244, ...), kind=kOutput, calls=%fused_computation.89.clone.1 | convolution fusion | flops 2463002624 | bytes 7127040 | tf_op jit(solution)/shard_map/transpose(jvp())/while/body/eval_jaxpr/checkpoint/hij,jhp->ihp/dot_general | solution.py:102
  856.9 12.9 fusion.248
  885.4 63.6 %dynamic_update_slice.81 = f32[2,256,48,64]{1,0,3,2:T(2,128)} dynamic-update-slice(f32[2,256,48,64]{1,0,3,2:T(2,128)} %get-tuple-element.1684, f32[1,256,48,64]{1,0,3,2:T(1,128)} %copy.492, s32[]{:T(128)S(6)} %sub.259, s32[]{:T(128)} %constant.236.clone.1..sunk.1, s32[]{:T(128)} %constant.236.clone.1..sunk.1, s32[]{:T(128)} %constant.236.clone.1..sunk.1) | dynamic-update-slice | bytes 6291460 | tf_op jit(solution)/shard_map/transpose(jvp())/while/body/jit(dynamic_update_index_in_dim)/dynamic_update_slice | solution.py:138
  987.4 22.9 %fusion.245 = (f32[48,256]{1,0:T(8,128)}, f32[48,256]{1,0:T(8,128)}, f32[48,256]{1,0:T(8,128)}, f32[256,256]{1,0:T(8,128)}) fusion(f32[48,256]{1,0:T(8,128)} %copy.484, f32[48,256]{1,0:T(8,128)} %copy_bitcast_fusion.19, f32[256,256]{1,0:T(8,128)S(1)} %fusion.243, pred[256,256]{1,0:T(8,128)(4,1)} %fusion.244, ...), kind=kOutput, calls=%fused_computation.89.clone.1 | convolution fusion | flops 2463002624 | bytes 7127040 | tf_op jit(solution)/shard_map/transpose(jvp())/while/body/eval_jaxpr/checkpoint/hij,jhp->ihp/dot_general | solution.py:102
  1047.4 12.9 fusion.248
  1075.9 63.6 %dynamic_update_slice.81 = f32[2,256,48,64]{1,0,3,2:T(2,128)} dynamic-update-slice(f32[2,256,48,64]{1,0,3,2:T(2,128)} %get-tuple-element.1684, f32[1,256,48,64]{1,0,3,2:T(1,128)} %copy.492, s32[]{:T(128)S(6)} %sub.259, s32[]{:T(128)} %constant.236.clone.1..sunk.1, s32[]{:T(128)} %constant.236.clone.1..sunk.1, s32[]{:T(128)} %constant.236.clone.1..sunk.1) | dynamic-update-slice | bytes 6291460 | tf_op jit(solution)/shard_map/transpose(jvp())/while/body/jit(dynamic_update_index_in_dim)/dynamic_update_slice | solution.py:138
  1169.3 15.4 multiply_reduce_fusion.8
  1194.3 11.3 pad_add_fusion
  1220.7 19.4 fusion.112
  1240.2 12.2 fusion.151
  1252.4 22.4 %fusion.120 = f32[1536,6448]{1,0:T(8,128)} fusion(bf16[512,48]{0,1:T(8,128)(2,1)S(1)} %get-tuple-element.1127, bf16[512,3328]{0,1:T(8,128)(2,1)} %copy-done.20, bf16[512,3072]{0,1:T(8,128)(2,1)} %get-tuple-element.1156, bf16[512,1536]{1,0:T(8,128)(2,1)S(1)} %copy-done.19, f32[1536]{0:T(1024)S(1)} %copy-done.59, f32[512]{0:T(512)S(1)} %copy-done.64), kind=kOutput, calls=%fused_computation.217 | convolution fusion | flops 10164781056 | bytes 47800320 | tf_op jit(solution)/shard_map/dot_general | solution.py:271
  1274.9 11.1 fusion.119
  1288.6 74.8 %all-reduce.26.cloned.1.call-done = (f32[4,3328]{1,0:T(4,128)}, f32[3328]{0:T(1024)}, f32[1536]{0:T(1024)}, f32[3072]{0:T(1024)}, f32[48]{0:T(128)}, /*index=5*/f32[48]{0:T(128)}, f32[48]{0:T(128)}) async-done(((f32[4,3328]{1,0:T(4,128)}, f32[3328]{0:T(1024)}, f32[1536]{0:T(1024)}, f32[3072]{0:T(1024)}, f32[48]{0:T(128)}, /*index=5*/f32[48]{0:T(128)}, f32[48]{0:T(128)}), (f32[4,3328]{1,0:T(4,128)}, ...) | async-done | bytes 85584
  1368.5 209.5 %reduce-scatter.6.cloned.1.call-done = f32[96,1536]{1,0:T(8,128)} async-done(((f32[3072,1536]{1,0:T(8,128)}), f32[96,1536]{1,0:T(8,128)}) %reduce-scatter.6.cloned.1.call-update) | async-done | bytes 589840 | tf_op jit(solution)/shard_map/reduce_scatter | solution.py:277
  1578.1 371.8 %reduce-scatter.4.cloned.1.call-done = f32[48,6448]{1,0:T(8,128)} async-done(((f32[1536,6448]{1,0:T(8,128)}), f32[48,6448]{1,0:T(8,128)}) %reduce-scatter.4.cloned.1.call-update) | async-done | bytes 1238032 | tf_op jit(solution)/shard_map/reduce_scatter | solution.py:274
  (565 shorter events, 475.3 us)
Async XLA Ops:
  7.2 138.1 %all-gather.9.cloned.1.call-start = ((), (), s32[]{:S(2)}) async-start(), calls=%async_computation.2 | async-start | bytes 20680704 | tf_op jit(solution)/shard_map/all_gather | solution.py:185
  7.9 503.8 %all-gather.13.cloned.1.call-start = ((), (), s32[]{:S(2)}) async-start(), calls=%async_computation.6 | async-start | bytes 7077888 | tf_op jit(solution)/shard_map/all_gather | solution.py:30
  8.7 124.4 %collective-permute-start = (bf16[3]{0:T(256)(128)(2,1)S(1)}, bf16[3]{0:T(256)(128)(2,1)S(1)}, u32[]{:S(2)}, u32[]{:S(2)}) collective-permute-start(bf16[3]{0:T(256)(128)(2,1)S(1)} %slice.202), channel_id=1, source_target_pairs={{0,1},{1,2},{2,3},{3,4},{4,5},{5,6},{6,7},{8,9},{9,10},{10,11},{11... | collective-permute-start | bytes 26 | tf_op jit(solution)/shard_map/ppermute | solution.py:24
  59.5 103.2 %copy-start.58 = (f32[1536]{0:T(1024)}, f32[1536]{0:T(1024)S(1)}, u32[]{:S(2)}) copy-start(f32[1536]{0:T(1024)S(1)} %convert_element_type.105) | copy-start | bytes 18436
  130.3 49.8 %copy-start.43 = (f32[3328]{0:T(1024)}, f32[3328]{0:T(1024)S(1)}, u32[]{:S(2)}) copy-start(f32[3328]{0:T(1024)S(1)} %get-tuple-element.1018) | copy-start | bytes 39940
  130.3 49.8 %copy-start.45 = (f32[3328]{0:T(1024)}, f32[3328]{0:T(1024)S(1)}, u32[]{:S(2)}) copy-start(f32[3328]{0:T(1024)S(1)} %get-tuple-element.1019) | copy-start | bytes 39940
  133.1 37.3 %copy-start.80 = (f32[48]{0:T(128)}, f32[48]{0:T(128)S(1)}, u32[]{:S(2)}) copy-start(f32[48]{0:T(128)S(1)} %exponential_negate_fusion) | copy-start | bytes 580
  135.8 44.3 %copy-start.68 = (pred[512]{0:T(512)(128)(4,1)}, pred[512]{0:T(512)(128)(4,1)S(1)}, u32[]{:S(2)}) copy-start(pred[512]{0:T(512)(128)(4,1)S(1)} %get-tuple-element.1164) | copy-start | bytes 1540
  135.8 44.3 %copy-start.70 = (pred[512]{0:T(512)(128)(4,1)}, pred[512]{0:T(512)(128)(4,1)S(1)}, u32[]{:S(2)}) copy-start(pred[512]{0:T(512)(128)(4,1)S(1)} %get-tuple-element.1165) | copy-start | bytes 1540
  135.8 44.3 %copy-start.72 = (pred[512]{0:T(512)(128)(4,1)}, pred[512]{0:T(512)(128)(4,1)S(1)}, u32[]{:S(2)}) copy-start(pred[512]{0:T(512)(128)(4,1)S(1)} %get-tuple-element.1166) | copy-start | bytes 1540
  135.8 34.6 %copy-start.78 = (f32[48]{0:T(128)S(1)}, f32[48]{0:T(128)}, u32[]{:S(2)}) copy-start(f32[48]{0:T(128)} %param.31) | copy-start | bytes 580
  166.6 8.4 collective-permute-start.1
  249.6 63.3 %copy-start.37 = (s32[2,256]{1,0:T(2,128)S(1)}, s32[2,256]{1,0:T(2,128)}, u32[]{:S(2)}) copy-start(s32[2,256]{1,0:T(2,128)} %copy-done.36) | copy-start | bytes 6148 | tf_op jit(solution)/shard_map/while
  348.2 63.3 %copy-start.37 = (s32[2,256]{1,0:T(2,128)S(1)}, s32[2,256]{1,0:T(2,128)}, u32[]{:S(2)}) copy-start(s32[2,256]{1,0:T(2,128)} %copy-done.36) | copy-start | bytes 6148 | tf_op jit(solution)/shard_map/while
  414.7 180.2 %all-gather.11.cloned.1.call-start = ((), (), s32[]{:S(2)}) async-start(), calls=%async_computation.3 | async-start | bytes 9732096 | tf_op jit(solution)/shard_map/all_gather | solution.py:188
  415.4 308.7 %all-gather.15.cloned.1.call-start = ((), (), s32[]{:S(2)}) async-start(), calls=%async_computation.7 | async-start | bytes 7077888 | tf_op jit(solution)/shard_map/all_gather | solution.py:50
  416.2 191.5 %copy-start.52 = (f32[3072]{0:T(1024)}, f32[3072]{0:T(1024)S(1)}, u32[]{:S(2)}) copy-start(f32[3072]{0:T(1024)S(1)} %convert_element_type.112) | copy-start | bytes 36868
  436.7 180.9 %copy-start.25 = (f32[512,48]{0,1:T(8,128)}, f32[512,48]{0,1:T(8,128)S(1)}, u32[]{:S(2)}) copy-start(f32[512,48]{0,1:T(8,128)S(1)} %exponential_select_fusion.2) | copy-start | bytes 294916
  523.7 84.0 %slice-start.7 = ((s8[6815744]{0:T(1024)(128)(4,1)}), s8[2621440]{0:T(1024)(128)(4,1)S(1)}, s32[]{:S(2)}) async-start(s8[6815744]{0:T(1024)(128)(4,1)} %bitcast.525), calls=%async_computation.16 | async-start | bytes 5242880
  531.8 75.9 %copy-start.65 = (f32[512]{0:T(512)}, f32[512]{0:T(512)S(1)}, u32[]{:S(2)}) copy-start(f32[512]{0:T(512)S(1)} %fusion.145) | copy-start | bytes 6148
  626.3 737.1 %all-reduce.26.cloned.1.call-start = ((), (), s32[]{:S(2)}) async-start(), calls=%async_computation.8 | async-start | bytes 183296
  876.4 72.6 %copy-start.1 = (f32[48,64,128]{2,1,0:T(8,128)S(1)}, f32[48,64,128]{2,1,0:T(8,128)}, u32[]{:S(2)}) copy-start(f32[48,64,128]{2,1,0:T(8,128)} %multiply_add_fusion.10) | copy-start | bytes 4718596 | tf_op jit(solution)/shard_map/transpose(jvp())/while
  876.4 72.6 %copy-start.12 = (f32[2,256,128]{2,1,0:T(8,128)S(1)}, f32[2,256,128]{2,1,0:T(8,128)}, u32[]{:S(2)}) copy-start(f32[2,256,128]{2,1,0:T(8,128)} %copy-done.11) | copy-start | bytes 786436 | tf_op jit(solution)/shard_map/transpose(jvp())/while
  876.4 72.6 %copy-start.87 = (s32[2]{0:T(128)S(1)}, s32[2]{0:T(128)}, u32[]{:S(2)}) copy-start(s32[2]{0:T(128)} %get-tuple-element.1816) | copy-start | bytes 28 | tf_op jit(solution)/shard_map/transpose(jvp())/while
  885.3 63.6 %copy-start.35 = (f32[2,256,48]{1,0,2:T(2,128)}, f32[2,256,48]{1,0,2:T(2,128)S(1)}, u32[]{:S(2)}) copy-start(f32[2,256,48]{1,0,2:T(2,128)S(1)} %dynamic_update_slice.82) | copy-start | bytes 294916 | tf_op jit(solution)/shard_map/transpose(jvp())/while
  1066.9 72.6 %copy-start.1 = (f32[48,64,128]{2,1,0:T(8,128)S(1)}, f32[48,64,128]{2,1,0:T(8,128)}, u32[]{:S(2)}) copy-start(f32[48,64,128]{2,1,0:T(8,128)} %multiply_add_fusion.10) | copy-start | bytes 4718596 | tf_op jit(solution)/shard_map/transpose(jvp())/while
  1066.9 72.6 %copy-start.12 = (f32[2,256,128]{2,1,0:T(8,128)S(1)}, f32[2,256,128]{2,1,0:T(8,128)}, u32[]{:S(2)}) copy-start(f32[2,256,128]{2,1,0:T(8,128)} %copy-done.11) | copy-start | bytes 786436 | tf_op jit(solution)/shard_map/transpose(jvp())/while
  1066.9 72.6 %copy-start.87 = (s32[2]{0:T(128)S(1)}, s32[2]{0:T(128)}, u32[]{:S(2)}) copy-start(s32[2]{0:T(128)} %get-tuple-element.1816) | copy-start | bytes 28 | tf_op jit(solution)/shard_map/transpose(jvp())/while
  1075.9 63.6 %copy-start.35 = (f32[2,256,48]{1,0,2:T(2,128)}, f32[2,256,48]{1,0,2:T(2,128)S(1)}, u32[]{:S(2)}) copy-start(f32[2,256,48]{1,0,2:T(2,128)S(1)} %dynamic_update_slice.82) | copy-start | bytes 294916 | tf_op jit(solution)/shard_map/transpose(jvp())/while
  1209.3 5.7 collective-permute-start.2
  1240.1 338.0 %reduce-scatter.6.cloned.1.call-start = ((), (), s32[]{:S(2)}) async-start(), calls=%async_computation.5 | async-start | bytes 19464192 | tf_op jit(solution)/shard_map/reduce_scatter | solution.py:277
  1252.4 697.5 %reduce-scatter.4.cloned.1.call-start = ((), (), s32[]{:S(2)}) async-start(), calls=%async_computation.4 | async-start | bytes 41361408 | tf_op jit(solution)/shard_map/reduce_scatter | solution.py:274
  (101 other events, 1137.7 us)
Sparse Core Ops, SparseCore 0:
  10.9 134.3 all-gather.8
  414.8 96.8 all-gather.12
  514.7 80.2 all-gather.10
  626.4 97.6 all-gather.14
  1240.2 123.1 all-reduce.25
  1370.2 207.8 reduce-scatter.5
  1585.1 364.7 reduce-scatter.3
where the time goes:
time: 1990 us; the launch traced here: 1960 us
  waiting for transfers between devices  845 us (42%)
  local copies, waits for them, and re-layouts  445 us (22%)
  matrix products  322 us (16%)
  other arithmetic  176 us (9%)
  blocking collectives  126 us (6%)
    reduce_scatter x1, waiting for transfers between devices, on_device(): lax.psum_scatter(grad_in_proj, ('dp', 'seq'), scatter_dimension=0, tiled=...  372 us
    dynamic_update_slice x14, local copies, waits for them, and re-layouts, local_pass(): lax.scan(jax.checkpoint(group_step), start, pieces)  273 us
    reduce_scatter x1, waiting for transfers between devices, on_device(): lax.psum_scatter(grad_out_proj, ('dp', 'seq'), scatter_dimension=0, tiled...  210 us
    dot_general x6, matrix products, group_step(): within = jnp.einsum('hij,jhp->ihp', mixing, values_x, precision=PRECISE)  104 us
    unnamed x8, waiting for transfers between devices  76.2 us
    all_gather x1, blocking collectives, on_device(): lax.all_gather(conv_weight, ('dp', 'seq'), axis=1, tiled=True)  67.4 us
    all_gather x1, waiting for transfers between devices, prefix(): lax.all_gather(a.astype(kind), axis)  66 us
    all_gather x1, waiting for transfers between devices, on_device(): lax.all_gather(out_proj, ('dp', 'seq'), axis=0, tiled=True)  63.1 us
  transfers between devices with their start and end apart: 10, of which 8 were waited for; matrix products, arithmetic and copies ran while one was open for 8% of the time, Pallas kernels for 0%

commit v1 on v0

v1 whole, which is shorter than its diff:
```python
from functools import partial

import jax
import jax.numpy as jnp
from jax import lax
from jax.experimental import pallas as pl
from jax.experimental.pallas import tpu as pltpu
from jax.sharding import Mesh
from jax.sharding import PartitionSpec as P

INNER = 3072
HEADDIM = 64
STATE = 128
CONV = 4
GROUP = 256
HEADS = 48
XBC = 3328
LONGEST = 1024
HALO = 16

EPSILON = 1e-05
PRECISE = lax.Precision.HIGHEST
BF = jnp.bfloat16
F32 = jnp.float32
NEVER = -1e30

CUM, DT, REACH, CARRY, ENDN, LASTW = 0, 16, 32, 48, 64, 80
SAME, SEG = 96, 100


def shift(v, axis, step):
    n = lax.axis_size(axis)
    return lax.ppermute(v, axis, [(i, (i + step) % n) for i in range(n)])


def along(v, step):
    n = lax.axis_size("a") * lax.axis_size("b")
    route = [(i, i + step) for i in range(n) if 0 <= i + step < n]
    return lax.ppermute(v, ("a", "b"), route)


def to_peer(v, sx, sc):
    n = lax.axis_size("x")
    route = [(x * 2 + c, ((x + sx) % n) * 2 + (c ^ sc)) for x in range(n) for c in range(2)]
    return lax.ppermute(v, ("x", "core"), route)


def peers():
    return [(sx, sc) for sx in range(lax.axis_size("x")) for sc in range(2)]


def group_of(sx, sc):
    x, c, n = lax.axis_index("x"), lax.axis_index("core"), lax.axis_size("x")
    return lax.rem(x + sx + n, n) * 2 + (c + sc) % 2


def gather_group(v):
    slots = []
    for sx in range(lax.axis_size("x")):
        here = v if sx == 0 else shift(v, "x", sx)
        slots += [here, shift(here, "core", 1)]
    return slots


def sum_to_owner(slots):
    total = None
    for sx in range(lax.axis_size("x")):
        both = slots[2 * sx] + shift(slots[2 * sx + 1].astype(BF), "core", 1).astype(F32)
        part = both if sx == 0 else shift(both.astype(BF), "x", -sx).astype(F32)
        total = part if total is None else total + part
    return total


def sum_over_group(v):
    n = lax.axis_size("x")
    v = v.reshape((n, 2) + v.shape[1:])
    v = v + shift(v, "core", 1)[:, ::-1]
    total = v
    for step in range(1, n):
        total = total + jnp.roll(shift(v, "x", step), step, axis=0)
    return total.reshape((n * 2,) + v.shape[2:])


def gather_blocks(block):
    na, nb = lax.axis_size("a"), lax.axis_size("b")
    a, b = lax.axis_index("a"), lax.axis_index("b")
    whole = jnp.zeros((block.shape[0], na * nb) + block.shape[1:], block.dtype)
    for sa in range(na):
        here = block if sa == 0 else shift(block, "a", sa)
        for sb in range(nb):
            held = here if sb == 0 else shift(here, "b", sb)
            place = lax.rem(a - sa + na, na) * nb + lax.rem(b - sb + nb, nb)
            whole = lax.dynamic_update_slice_in_dim(whole, held[:, None], place, 1)
    return whole


def sum_blocks(grad, block_rows):
    na, nb = lax.axis_size("a"), lax.axis_size("b")
    a, b = lax.axis_index("a"), lax.axis_index("b")

    def part(ra, rb):
        place = lax.rem(a + ra, na) * nb + lax.rem(b + rb, nb)
        return lax.dynamic_slice_in_dim(grad, place, 1, 1)[:, 0]

    total = None
    for ra in range(na):
        held = part(ra, 0)
        for rb in range(1, nb):
            held = held + shift(part(ra, rb).astype(BF), "b", rb).astype(F32)
        got = held if ra == 0 else shift(held.astype(BF), "a", ra).astype(F32)
        total = got if total is None else total + got
    return total


def sum_everywhere(v):
    for axis in ("core", "x", "b", "a"):
        step, n = 1, lax.axis_size(axis)
        while step < n:
            v = v + lax.ppermute(v, axis, [(i, i ^ step) for i in range(n)])
            step *= 2
    return v


def nn(a, b):
    return lax.dot_general(a, b, (((1,), (0,)), ((), ())), preferred_element_type=F32)


def nt(a, b):
    return lax.dot_general(a, b, (((1,), (1,)), ((), ())), preferred_element_type=F32)


def tn(a, b):
    return lax.dot_general(a, b, (((0,), (0,)), ((), ())), preferred_element_type=F32)


def column(table, at):
    lane = lax.broadcasted_iota(jnp.int32, table.shape, 1)
    return jnp.sum(jnp.where(lane == at, table, 0.0), axis=1, keepdims=True)


def low_half(shape):
    return lax.broadcasted_iota(jnp.int32, shape, 1) < HEADDIM


def spread(table, kind, pair):
    first, second = column(table, kind + 2 * pair), column(table, kind + 2 * pair + 1)
    return jnp.where(low_half(table.shape), first, second)


def convolved(ext, taps, same):
    rows = ext.shape[0] - HALO
    pre = taps[CONV : CONV + 1] + taps[CONV - 1 : CONV] * ext[HALO:]
    for k in range(1, CONV):
        pre = pre + same[k - 1] * (taps[CONV - 1 - k : CONV - k] * ext[HALO - k : HALO - k + rows])
    return pre


def extended(halo, main):
    return jnp.concatenate([halo.astype(F32), main.astype(F32)], axis=0)


def conv_kernel(xh_ref, xm_ref, bh_ref, bm_ref, tx_ref, tb_ref, ct_ref, x_ref, bc_ref, own_ref):
    pair = pl.program_id(1)
    table = ct_ref[0]
    same = [table[:, SAME + k : SAME + k + 1] for k in range(CONV - 1)]

    @pl.when(pair == 0)
    def _():
        pre = convolved(extended(bh_ref[0], bm_ref[0]), tb_ref[...], same)
        bc_ref[0] = (pre * jax.nn.sigmoid(pre)).astype(BF)

    pre = convolved(extended(xh_ref[0], xm_ref[0]), tx_ref[...], same)
    x = pre * jax.nn.sigmoid(pre)
    x_ref[0] = x
    weighted = (spread(table, LASTW, pair) * x).astype(BF)
    own_ref[0] = tn(bc_ref[0, :, :STATE], weighted)


def causal(table, segrow, chunk, transposed):
    seg_c = table[chunk * GROUP : (chunk + 1) * GROUP, SEG : SEG + 1]
    seg_r = segrow[:, chunk * GROUP : (chunk + 1) * GROUP]
    down = lax.broadcasted_iota(jnp.int32, (GROUP, GROUP), 0)
    right = lax.broadcasted_iota(jnp.int32, (GROUP, GROUP), 1)
    order = (down <= right) if transposed else (down >= right)
    return jnp.where((seg_c == seg_r) & order, 0.0, NEVER)


def forward_kernel(x_ref, bc_ref, ct_ref, rt_ref, ln_ref, y_ref, score, mask):
    pair = pl.program_id(1)
    table = ct_ref[0]
    chunks = x_ref.shape[1] // GROUP

    @pl.when(pair == 0)
    def _():
        for c in range(chunks):
            rows = slice(c * GROUP, (c + 1) * GROUP)
            score[c] = nt(bc_ref[0, rows, STATE:], bc_ref[0, rows, :STATE])
            mask[c] = causal(table, rt_ref[0, 16:17, :], c, False)

    x = x_ref[0]
    xd = x * spread(table, DT, pair)
    half = low_half(xd.shape)
    parts = [jnp.where(half, xd, 0.0).astype(BF), jnp.where(half, 0.0, xd).astype(BF)]
    cums = [column(table, CUM + 2 * pair + e) for e in range(2)]
    carry = spread(table, CARRY, pair)
    ending = (spread(table, ENDN, pair) * xd).astype(BF)
    skip = ln_ref[0, 0:1, :]
    state = None
    for c in range(chunks):
        rows = slice(c * GROUP, (c + 1) * GROUP)
        y = skip * x[rows]
        for e in range(2):
            row = rt_ref[0, pl.ds(2 * pair + e, 1), rows]
            mixing = score[c] * jnp.exp(cums[e][rows] - row + mask[c])
            y = y + nn(mixing.astype(BF), parts[e][rows])
        if c:
            y = y + carry[rows] * nn(bc_ref[0, rows, STATE:], state.astype(BF))
        y_ref[0, rows, :] = y
        if c + 1 < chunks:
            added = tn(bc_ref[0, rows, :STATE], ending[rows])
            state = added if c == 0 else ln_ref[0, 1 + c : 2 + c, :] * state + added


def gate_kernel(yl_ref, bc_ref, inc_ref, z_ref, dn_ref, gain_ref, ct_ref, y_ref, sums_ref):
    pair = pl.program_id(1)
    y = yl_ref[0] + spread(ct_ref[0], REACH, pair) * nn(bc_ref[0, :, STATE:], inc_ref[0].astype(BF))
    y_ref[0] = y
    z = z_ref[0]
    gated = y * (z * jax.nn.sigmoid(z))
    squares = jnp.sum(gated * gated, axis=1, keepdims=True)
    pulled = jnp.sum(dn_ref[0] * gain_ref[0:1, :] * gated, axis=1, keepdims=True)
    lane = lax.broadcasted_iota(jnp.int32, (y.shape[0], 128), 1)
    both = jnp.where(lane == 0, squares, jnp.where(lane == 1, pulled, 0.0))

    @pl.when(pair == 0)
    def _():
        sums_ref[0] = both

    @pl.when(pair > 0)
    def _():
        sums_ref[0] += both


def gate_back_kernel(
    y_ref, z_ref, dn_ref, gain_ref, sums_ref, bc_ref, ct_ref, out_ref, dy_ref, dz_ref, pull_ref, gg_ref
):
    seq, pair = pl.program_id(0), pl.program_id(1)
    gain = gain_ref[0:1, :]
    y, z, dn = y_ref[0], z_ref[0], dn_ref[0]
    sig = jax.nn.sigmoid(z)
    silu = z * sig
    gated = y * silu
    r = lax.rsqrt(sums_ref[0, :, 0:1] * (1.0 / INNER) + EPSILON)
    unit = gated * r
    out_ref[0] = (unit * gain).astype(BF)
    dg = r * (dn * gain - unit * (r * (1.0 / INNER) * sums_ref[0, :, 1:2]))
    dy = dg * silu
    dy_ref[0] = dy
    dz_ref[0] = (dg * y * (sig * (1.0 + z * (1.0 - sig)))).astype(BF)
    pull_ref[0] = tn(bc_ref[0, :, STATE:], (spread(ct_ref[0], REACH, pair) * dy).astype(BF))
    gg_ref[0] = jnp.broadcast_to(jnp.sum(dn * unit, axis=0, keepdims=True), gg_ref.shape[1:])


def conv_back(d_conv, ext, taps, same):
    rows, width = d_conv.shape
    pre = convolved(ext, taps, same)
    sig = jax.nn.sigmoid(pre)
    d_pre = d_conv * (sig * (1.0 + pre * (1.0 - sig)))
    d_ext = jnp.concatenate(
        [jnp.zeros((HALO, width), F32), taps[CONV - 1 : CONV] * d_pre], axis=0
    )
    grads = [None] * 8
    grads[CONV - 1] = jnp.sum(d_pre * ext[HALO:], axis=0, keepdims=True)
    grads[CONV] = jnp.sum(d_pre, axis=0, keepdims=True)
    for k in range(1, CONV):
        kept = same[k - 1] * d_pre
        grads[CONV - 1 - k] = jnp.sum(kept * ext[HALO - k : HALO - k + rows], axis=0, keepdims=True)
        d_ext = d_ext + taps[CONV - 1 - k : CONV - k] * jnp.concatenate(
            [jnp.zeros((HALO - k, width), F32), kept, jnp.zeros((k, width), F32)], axis=0
        )
    grads = [g if g is not None else jnp.zeros((1, width), F32) for g in grads]
    return d_ext[HALO:].astype(BF), d_ext[:HALO].astype(BF), jnp.concatenate(grads, axis=0)


def backward_kernel(
    x_ref, bc_ref, dy_ref, inc_ref, adj_ref, ct_ref, rt_ref, ln_ref,
    xh_ref, xm_ref, bh_ref, bm_ref, tx_ref, tb_ref,
    dxm_ref, dxh_ref, dbm_ref, dbh_ref, tab_ref, gx_ref, gb_ref, gs_ref,
    score, mask, d_score, d_bc,
):
    pair, pairs = pl.program_id(1), pl.num_programs(1)
    table = ct_ref[0]
    chunks = x_ref.shape[1] // GROUP
    down = lax.broadcasted_iota(jnp.int32, (GROUP, GROUP), 0)
    right = lax.broadcasted_iota(jnp.int32, (GROUP, GROUP), 1)
    before = (right < down).astype(BF)
    upto = (right >= down).astype(BF)
    same = [table[:, SAME + k : SAME + k + 1] for k in range(CONV - 1)]

    @pl.when(pair == 0)
    def _():
        for c in range(chunks):
            rows = slice(c * GROUP, (c + 1) * GROUP)
            score[c] = nt(bc_ref[0, rows, :STATE], bc_ref[0, rows, STATE:])
            mask[c] = causal(table, rt_ref[0, 16:17, :], c, True)
        d_score[...] = jnp.zeros_like(d_score)
        d_bc[...] = jnp.zeros_like(d_bc)
        tab_ref[...] = jnp.zeros_like(tab_ref)

    x, dy = x_ref[0], dy_ref[0]
    dyb = dy.astype(BF)
    half = low_half(x.shape)
    dt = spread(table, DT, pair)
    xd = x * dt
    parts = [jnp.where(half, xd, 0.0).astype(BF), jnp.where(half, 0.0, xd).astype(BF)]
    cums = [column(table, CUM + 2 * pair + e) for e in range(2)]
    pulled = spread(table, CARRY, pair) * dy
    pulled_b = pulled.astype(BF)
    endn = spread(table, ENDN, pair)
    ending = endn * xd
    ending_b = ending.astype(BF)
    skip = ln_ref[0, 0:1, :]
    gs_ref[0] = jnp.broadcast_to(jnp.sum(dy * x, axis=0, keepdims=True), gs_ref.shape[1:])

    def part(c):
        return slice(c * GROUP, (c + 1) * GROUP)

    states, adjoints = [inc_ref[0]], [adj_ref[0]]
    for c in range(chunks - 1):
        added = tn(bc_ref[0, part(c), :STATE], ending_b[part(c)])
        states.append(ln_ref[0, 1 + c : 2 + c, :] * states[-1] + added)
    for c in range(chunks - 1, 0, -1):
        added = tn(bc_ref[0, part(c), STATE:], pulled_b[part(c)])
        adjoints.insert(0, ln_ref[0, 1 + c : 2 + c, :] * adjoints[0] + added)

    lane = lax.broadcasted_iota(jnp.int32, (GROUP, 128), 1)
    d_x = []
    for c in range(chunks):
        rows = part(c)
        keys, reads = bc_ref[0, rows, :STATE], bc_ref[0, rows, STATE:]
        state_b, adj_b = states[c].astype(BF), adjoints[c].astype(BF)
        from_state = pulled[rows] * nn(reads, state_b)
        to_end = nn(keys, adj_b)
        into_state = ending[rows] * to_end
        across = nn(upto, from_state.astype(BF)) + nn(before, into_state.astype(BF))
        across = across + ln_ref[0, 1 + c : 2 + c, :] * jnp.sum(
            states[c] * adjoints[c], axis=0, keepdims=True
        )
        d_bc[rows, :STATE] += nt(ending_b[rows], adj_b)
        d_bc[rows, STATE:] += nt(pulled_b[rows], state_b)
        d_xd, d_scores = [], None
        d_log = []
        for e in range(2):
            row = rt_ref[0, pl.ds(2 * pair + e, 1), rows]
            decay = jnp.exp(row - cums[e][rows] + mask[c])
            weighted = decay * nt(parts[e][rows], dyb[rows])
            d_scores = weighted if d_scores is None else d_scores + weighted
            d_xd.append(nn((score[c] * decay).astype(BF), dyb[rows]))
            crossing = nn(before, (score[c] * weighted).astype(BF))
            d_log.append(jnp.sum(jnp.where(right >= down, crossing, 0.0), axis=1, keepdims=True))
        d_score[c] += d_scores
        u = jnp.where(half[rows], d_xd[0], d_xd[1]) + endn[rows] * to_end
        d_x.append(dt[rows] * u + skip * dy[rows])
        d_step = x[rows] * u
        here = half[rows]
        new = jnp.zeros((GROUP, 128), F32)
        for e in range(2):
            keep = here if e == 0 else jnp.logical_not(here)
            log_e = d_log[e] + jnp.sum(jnp.where(keep, across, 0.0), axis=1, keepdims=True)
            step_e = jnp.sum(jnp.where(keep, d_step, 0.0), axis=1, keepdims=True)
            new = new + jnp.where(lane == 2 * pair + e, log_e, 0.0)
            new = new + jnp.where(lane == 16 + 2 * pair + e, step_e, 0.0)
        tab_ref[0, rows, :] += new

    main, halo, grads = conv_back(
        jnp.concatenate(d_x, axis=0), extended(xh_ref[0], xm_ref[0]), tx_ref[...], same
    )
    dxm_ref[0], dxh_ref[0], gx_ref[0] = main, halo, grads

    @pl.when(pair == pairs - 1)
    def _():
        whole = []
        for c in range(chunks):
            rows = part(c)
            ds = d_score[c].astype(BF)
            d_keys = d_bc[rows, :STATE] + nn(ds, bc_ref[0, rows, STATE:])
            d_reads = d_bc[rows, STATE:] + tn(ds, bc_ref[0, rows, :STATE])
            whole.append(jnp.concatenate([d_keys, d_reads], axis=1))
        main, halo, grads = conv_back(
            jnp.concatenate(whole, axis=0), extended(bh_ref[0], bm_ref[0]), tb_ref[...], same
        )
        dbm_ref[0], dbh_ref[0], gb_ref[0] = main, halo, grads


def tile(rows):
    return pl.BlockSpec((1, rows, 128), lambda q, p: (q, 0, p))


def per_seq(rows, width):
    return pl.BlockSpec((1, rows, width), lambda q, p: (q, 0, 0))


def lanes(rows):
    return pl.BlockSpec((rows, 128), lambda q, p: (0, p))


def shared(rows, width):
    return pl.BlockSpec((rows, width), lambda q, p: (0, 0))


def shape(*dims, dtype=F32):
    return jax.ShapeDtypeStruct(dims, dtype)


def params():
    return pltpu.CompilerParams(
        dimension_semantics=("arbitrary", "arbitrary"), vmem_limit_bytes=40 * 2**20
    )


def cost(flops, size):
    return pl.CostEstimate(flops=int(flops), bytes_accessed=int(size), transcendentals=0)


def on_device(
    tokens, segment_ids, in_proj, conv_weight, conv_bias, out_proj, norm_gain, gate_gain,
    a_log, dt_bias, skip_d, cotangent,
):
    n_x = lax.axis_size("x")
    groups = 2 * n_x
    positions = lax.axis_size("a") * lax.axis_size("b")
    me, place = group_of(0, 0), lax.axis_index("a") * lax.axis_size("b") + lax.axis_index("b")
    index = me * positions + place
    rows, width = tokens.shape
    heads = HEADS // groups
    cols = heads * HEADDIM
    pairs = heads // 2
    chunks = rows // GROUP
    state2 = 2 * STATE

    tok = jnp.stack(gather_group(tokens))
    halo_tok = jnp.stack(gather_group(along(tokens[rows - HALO :], 1)))
    own_halo = jnp.where(place == 0, -1, along(segment_ids[rows - HALO :], 1))
    ids = jnp.stack(gather_group(jnp.concatenate([own_halo, segment_ids])))
    cot = jnp.stack(gather_group(cotangent))

    small = jnp.concatenate([norm_gain, gate_gain, conv_bias, conv_weight.reshape(-1)])
    n_norm, n_gate, n_conv = norm_gain.shape[0], gate_gain.shape[0], conv_bias.shape[0]
    small = jnp.pad(small, (0, -small.shape[0] % 128))
    slots = jnp.stack(gather_group(small))
    by_group = jnp.zeros((groups,) + small.shape, BF)
    for at, (sx, sc) in enumerate(peers()):
        by_group = lax.dynamic_update_slice_in_dim(by_group, slots[at : at + 1], group_of(-sx, sc), 0)
    every = gather_blocks(by_group[:, None]).reshape(groups * positions, -1).astype(F32)
    cuts = [n_norm, n_norm + n_gate, n_norm + n_gate + n_conv]
    gain_in = every[:, : cuts[0]].reshape(-1)
    gain_out = every[:, cuts[0] : cuts[1]].reshape(-1)
    bias_all = every[:, cuts[1] : cuts[2]].reshape(-1)
    taps_all = every[:, cuts[2] : cuts[2] + CONV * n_conv].reshape(-1, CONV, n_conv)
    taps_all = taps_all.transpose(1, 0, 2).reshape(CONV, XBC)
    conv_all = jnp.concatenate([taps_all, bias_all[None], jnp.zeros((3, XBC), F32)], axis=0)
    taps_x = lax.dynamic_slice_in_dim(conv_all, me * cols, cols, 1)
    taps_b = conv_all[:, INNER:]
    gain_g = jnp.broadcast_to(lax.dynamic_slice_in_dim(gain_out, me * cols, cols, 0), (8, cols))
    a_g = lax.dynamic_slice_in_dim(a_log, me * heads, heads, 0)
    bias_g = lax.dynamic_slice_in_dim(dt_bias, me * heads, heads, 0)
    skip_g = lax.dynamic_slice_in_dim(skip_d, me * heads, heads, 0)

    def columns_of(group):
        return (
            jnp.concatenate(
                [
                    lax.dynamic_slice_in_dim(in_proj, INNER + group * cols, cols, 1),
                    in_proj[:, 2 * INNER : INNER + XBC],
                    jnp.pad(
                        lax.dynamic_slice_in_dim(in_proj, INNER + XBC + group * heads, heads, 1),
                        ((0, 0), (0, 128 - heads)),
                    ),
                ],
                axis=1,
            ),
            lax.dynamic_slice_in_dim(in_proj, group * cols, cols, 1),
        )

    first = jnp.zeros((groups, in_proj.shape[0], cols + state2 + 128), BF)
    second = jnp.zeros((groups, in_proj.shape[0], cols), BF)
    for sx, sc in peers():
        one, two = columns_of(group_of(sx, sc))
        if (sx, sc) != (0, 0):
            one, two = to_peer(one, sx, sc), to_peer(two, sx, sc)
        first = lax.dynamic_update_slice_in_dim(first, one[None], group_of(-sx, sc), 0)
        second = lax.dynamic_update_slice_in_dim(second, two[None], group_of(-sx, sc), 0)
    w_first = gather_blocks(first).reshape(width, -1)
    w_gate = gather_blocks(second).reshape(width, -1)
    w_out = gather_blocks(out_proj[None]).reshape(cols, width)
    w_xbc = w_first[:, : cols + state2]
    w_dt = w_first[:, cols + state2 :]

    def normed_of(values):
        v = values.astype(F32)
        scale = lax.rsqrt(jnp.mean(v * v, axis=-1, keepdims=True) + EPSILON)
        return (v * scale * gain_in).astype(BF)

    normed = normed_of(tok).reshape(groups * rows, width)
    normed_halo = normed_of(halo_tok).reshape(groups * HALO, width)

    def project(values, weight, dtype):
        return jnp.dot(values, weight, preferred_element_type=F32).astype(dtype)

    w_x, w_bc = w_xbc[:, :cols], w_xbc[:, cols:]
    x_main = project(normed, w_x, BF).reshape(groups, rows, cols)
    b_main = project(normed, w_bc, BF).reshape(groups, rows, state2)
    raw_halo = project(normed_halo, w_xbc, BF).reshape(groups, HALO, cols + state2)
    x_halo, b_halo = raw_halo[:, :, :cols], raw_halo[:, :, cols:]
    dt_raw = project(normed, w_dt, F32).reshape(groups, rows, 128)[:, :, :heads]

    seg, prev = ids[:, HALO:], ids[:, HALO - 1]
    step_dt = jax.nn.softplus(dt_raw + bias_g)
    rate = jnp.exp(a_g)
    decay_log = -rate * step_dt
    triangle = jnp.tril(jnp.ones((GROUP, GROUP), F32))
    cum = jnp.einsum(
        "ij,qcjh->qcih", triangle, decay_log.reshape(groups, chunks, GROUP, heads), precision=PRECISE
    )
    total = cum[:, :, -1]
    seg_c = seg.reshape(groups, chunks, GROUP)
    last = seg_c[:, :, -1]
    earlier = jnp.concatenate([prev[:, None], last[:, :-1]], axis=1)
    carry = jnp.where((seg_c == earlier[:, :, None])[..., None], jnp.exp(cum), 0.0)
    endn = jnp.where((seg_c == last[:, :, None])[..., None], jnp.exp(total[:, :, None] - cum), 0.0)
    retain = jnp.where((last == earlier)[..., None], jnp.exp(total), 0.0)
    reach_c, end_c = [], []
    run = jnp.ones((groups, heads), F32)
    for c in range(chunks):
        reach_c.append(carry[:, c] * run[:, None])
        run = run * retain[:, c]
    device_decay = run
    run = jnp.ones((groups, heads), F32)
    for c in range(chunks - 1, -1, -1):
        end_c.insert(0, endn[:, c] * run[:, None])
        run = run * retain[:, c]
    reach = jnp.concatenate(reach_c, axis=1)
    last_w = jnp.concatenate(end_c, axis=1) * step_dt

    def wide(v):
        return jnp.pad(v.reshape(groups, rows, heads), ((0, 0), (0, 0), (0, 16 - heads)))

    same = jnp.stack(
        [ids[:, HALO - k : HALO - k + rows] == seg for k in range(1, CONV)], axis=-1
    ).astype(F32)
    col_table = jnp.concatenate(
        [wide(v) for v in (cum, step_dt, reach, carry, endn, last_w)]
        + [same, jnp.zeros((groups, rows, 1), F32), seg.astype(F32)[..., None], jnp.zeros((groups, rows, 27), F32)],
        axis=-1,
    )
    row_table = jnp.concatenate(
        [
            jnp.pad(cum.reshape(groups, rows, heads).transpose(0, 2, 1), ((0, 0), (0, 16 - heads), (0, 0))),
            seg.astype(F32)[:, None],
            jnp.zeros((groups, 7, rows), F32),
        ],
        axis=1,
    )
    lane_table = jnp.concatenate(
        [
            jnp.broadcast_to(jnp.repeat(skip_g, HEADDIM), (groups, 1, cols)),
            jnp.repeat(retain, HEADDIM, axis=-1),
            jnp.zeros((groups, 7 - chunks, cols), F32),
        ],
        axis=1,
    )

    grid = (groups, pairs)
    big = groups * rows * cols
    values_x, bc, own_state = pl.pallas_call(
        conv_kernel,
        grid=grid,
        in_specs=[
            tile(HALO), tile(rows), per_seq(HALO, state2), per_seq(rows, state2),
            lanes(8), shared(8, state2), per_seq(rows, 128),
        ],
        out_specs=[tile(rows), per_seq(rows, state2), tile(STATE)],
        out_shape=[
            shape(groups, rows, cols), shape(groups, rows, state2, dtype=BF), shape(groups, STATE, cols),
        ],
        compiler_params=params(),
        cost_estimate=cost(2 * big * STATE, 8 * big),
        name="conv_and_state",
    )(x_halo, x_main, b_halo, b_main, taps_x, taps_b, col_table)

    hops = -(-(LONGEST - 1) // rows)

    def entering(own, decay, sign):
        total_in, weight = None, jnp.ones_like(decay)
        sent = own.astype(BF)
        for hop in range(1, hops + 1):
            got = along(sent, sign * hop).astype(F32)
            term = got if hop == 1 else jnp.repeat(weight, HEADDIM, axis=-1)[:, None] * got
            total_in = term if total_in is None else total_in + term
            if hop < hops:
                weight = weight * along(decay, sign * hop)
        return total_in

    incoming = entering(own_state, device_decay, 1)

    mixed_local = pl.pallas_call(
        forward_kernel,
        grid=grid,
        in_specs=[tile(rows), per_seq(rows, state2), per_seq(rows, 128), per_seq(24, rows), tile(8)],
        out_specs=tile(rows),
        out_shape=shape(groups, rows, cols),
        scratch_shapes=[pltpu.VMEM((chunks, GROUP, GROUP), F32)] * 2,
        compiler_params=params(),
        cost_estimate=cost(8 * big * GROUP, 8 * big),
        name="mix_within_block",
    )(values_x, bc, col_table, row_table, lane_table)

    gate_z = project(normed, w_gate, F32).reshape(groups, rows, cols)
    d_normed = jnp.einsum("qtd,cd->qtc", cot, w_out, preferred_element_type=F32)

    mixed_y, sums = pl.pallas_call(
        gate_kernel,
        grid=grid,
        in_specs=[
            tile(rows), per_seq(rows, state2), tile(STATE), tile(rows), tile(rows), lanes(8), per_seq(rows, 128),
        ],
        out_specs=[tile(rows), per_seq(rows, 128)],
        out_shape=[shape(groups, rows, cols), shape(groups, rows, 128)],
        compiler_params=params(),
        cost_estimate=cost(2 * big * STATE, 16 * big),
        name="gate",
    )(mixed_local, bc, incoming, gate_z, d_normed, gain_g, col_table)
    sums = sum_over_group(sums[:, :, :2])
    sums = jnp.pad(sums, ((0, 0), (0, 0), (0, 126)))

    normed_out, d_y, d_gate, pull, gate_sums = pl.pallas_call(
        gate_back_kernel,
        grid=grid,
        in_specs=[
            tile(rows), tile(rows), tile(rows), lanes(8), per_seq(rows, 128), per_seq(rows, state2), per_seq(rows, 128),
        ],
        out_specs=[tile(rows), tile(rows), tile(rows), tile(STATE), tile(8)],
        out_shape=[
            shape(groups, rows, cols, dtype=BF), shape(groups, rows, cols),
            shape(groups, rows, cols, dtype=BF), shape(groups, STATE, cols), shape(groups, 8, cols),
        ],
        compiler_params=params(),
        cost_estimate=cost(2 * big * STATE, 20 * big),
        name="gate_back",
    )(mixed_y, gate_z, d_normed, gain_g, sums, bc, col_table)

    later = entering(pull, device_decay, -1)

    grad_out = jnp.einsum("qtc,qtd->cd", normed_out, cot, preferred_element_type=F32)
    grad_out_proj = sum_blocks(grad_out.reshape(1, positions, -1, width), None)[0]
    out_terms = jnp.einsum("qtc,cd->qtd", normed_out, w_out, preferred_element_type=F32)
    stream = tokens.astype(F32)
    output = (stream + sum_to_owner([out_terms[q] for q in range(groups)])).astype(BF)

    def grad_in(values, d_values):
        out = jnp.dot(values.T, d_values, preferred_element_type=F32)
        return sum_blocks(out.reshape(groups, positions, -1, d_values.shape[1]), None)

    d_gate_rows = d_gate.reshape(groups * rows, cols)
    grad_gate_cols = grad_in(normed, d_gate_rows)

    d_xm, d_xh, d_bm, d_bh, d_table, g_x, g_b, g_skip = pl.pallas_call(
        backward_kernel,
        grid=grid,
        in_specs=[
            tile(rows), per_seq(rows, state2), tile(rows), tile(STATE), tile(STATE),
            per_seq(rows, 128), per_seq(24, rows), tile(8),
            tile(HALO), tile(rows), per_seq(HALO, state2), per_seq(rows, state2), lanes(8), shared(8, state2),
        ],
        out_specs=[
            tile(rows), tile(HALO), per_seq(rows, state2), per_seq(HALO, state2), per_seq(rows, 128),
            tile(8), per_seq(8, state2), tile(8),
        ],
        out_shape=[
            shape(groups, rows, cols, dtype=BF), shape(groups, HALO, cols, dtype=BF),
            shape(groups, rows, state2, dtype=BF), shape(groups, HALO, state2, dtype=BF),
            shape(groups, rows, 128), shape(groups, 8, cols), shape(groups, 8, state2), shape(groups, 8, cols),
        ],
        scratch_shapes=[pltpu.VMEM((chunks, GROUP, GROUP), F32)] * 3 + [pltpu.VMEM((rows, state2), F32)],
        compiler_params=params(),
        cost_estimate=cost(20 * big * GROUP, 16 * big),
        name="mix_back",
    )(
        values_x, bc, d_y, incoming, later, col_table, row_table, lane_table,
        x_halo, x_main, b_halo, b_main, taps_x, taps_b,
    )

    spill = along(jnp.concatenate([d_xh, d_bh], axis=2), -1).astype(F32)

    def with_spill(main, more):
        tail = (main[:, rows - HALO :].astype(F32) + more).astype(BF)
        return lax.dynamic_update_slice_in_dim(main, tail, rows - HALO, 1)

    d_xm = with_spill(d_xm, spill[:, :, :cols])
    d_bm = with_spill(d_bm, spill[:, :, cols:])
    d_log, d_step = d_table[:, :, :heads], d_table[:, :, 16 : 16 + heads]
    d_dt = (d_step - rate * d_log) * jax.nn.sigmoid(dt_raw + bias_g)
    grad_bias_g = jnp.sum(d_dt, axis=(0, 1))
    grad_a_g = -jnp.sum(rate * step_dt * d_log, axis=(0, 1))
    grad_skip_g = jnp.sum(g_skip[:, 0].reshape(groups, heads, HEADDIM), axis=(0, 2))
    d_dt_b = jnp.pad(d_dt, ((0, 0), (0, 0), (0, 128 - heads))).astype(BF)
    d_first = jnp.concatenate([d_xm, d_bm, d_dt_b], axis=2).reshape(groups * rows, -1)

    grad_first_cols = grad_in(normed, d_first)
    d_normed_in = jnp.dot(d_first, w_first.T, preferred_element_type=F32)
    d_normed_in = d_normed_in + jnp.dot(d_gate_rows, w_gate.T, preferred_element_type=F32)
    d_normed_in = d_normed_in.reshape(groups, rows, width)

    values = tok.astype(F32)
    scale = lax.rsqrt(jnp.mean(values * values, axis=-1, keepdims=True) + EPSILON)
    grad_norm = jnp.sum(d_normed_in * (values * scale), axis=(0, 1))
    own = sum_to_owner([d_normed_in[q] for q in range(groups)])
    inner = own * gain_in
    r = lax.rsqrt(jnp.mean(stream * stream, axis=-1, keepdims=True) + EPSILON)
    d_stream = r * (inner - stream * (r * r * jnp.mean(inner * stream, axis=-1, keepdims=True)))
    grad_tokens = cotangent.astype(F32) + d_stream

    grad_in_proj = jnp.zeros((in_proj.shape[0], in_proj.shape[1]), F32)
    bc_total = None
    for sx, sc in peers():
        one = lax.dynamic_index_in_dim(grad_first_cols, group_of(sx, sc), 0, False)
        two = lax.dynamic_index_in_dim(grad_gate_cols, group_of(sx, sc), 0, False)
        if (sx, sc) != (0, 0):
            one = to_peer(one.astype(BF), sx, sc).astype(F32)
            two = to_peer(two.astype(BF), sx, sc).astype(F32)
        source = group_of(-sx, sc)
        grad_in_proj = lax.dynamic_update_slice_in_dim(grad_in_proj, two, source * cols, 1)
        grad_in_proj = lax.dynamic_update_slice_in_dim(grad_in_proj, one[:, :cols], INNER + source * cols, 1)
        grad_in_proj = lax.dynamic_update_slice_in_dim(
            grad_in_proj, one[:, cols + state2 : cols + state2 + heads], INNER + XBC + source * heads, 1
        )
        shared_cols = one[:, cols : cols + state2]
        bc_total = shared_cols if bc_total is None else bc_total + shared_cols
    grad_in_proj = lax.dynamic_update_slice(grad_in_proj, bc_total, (0, 2 * INNER))

    def placed(v):
        out = jnp.zeros((groups,) + v.shape, F32)
        return lax.dynamic_update_slice_in_dim(out, v[None], me, 0)

    g_x, g_b = jnp.sum(g_x, axis=0)[: CONV + 1], jnp.sum(g_b, axis=0)[: CONV + 1]
    pieces = [
        placed(g_x), g_b, placed(jnp.sum(gate_sums[:, 0], axis=0)),
        placed(jnp.stack([grad_a_g, grad_bias_g, grad_skip_g])), grad_norm,
    ]
    flat = jnp.concatenate([p.reshape(-1) for p in pieces])
    count = flat.shape[0]
    flat = jnp.pad(flat, (0, -count % 1024)).reshape(-1, 128)
    flat = sum_everywhere(flat).reshape(-1)
    sizes, at, back = [p.size for p in pieces], 0, []
    for p, size in zip(pieces, sizes):
        back.append(flat[at : at + size].reshape(p.shape))
        at += size
    conv_x, conv_b, gate_all, head_all, norm_all = back
    conv_sum = jnp.concatenate([conv_x.transpose(1, 0, 2).reshape(CONV + 1, INNER), conv_b], axis=1)
    conv_own = lax.dynamic_slice_in_dim(conv_sum, index * n_conv, n_conv, 1)
    grad_gate = lax.dynamic_slice_in_dim(gate_all.reshape(-1), index * n_gate, n_gate, 0)
    grad_norm = lax.dynamic_slice_in_dim(norm_all, index * n_norm, n_norm, 0)
    head_all = head_all.transpose(1, 0, 2).reshape(3, HEADS)
    return (
        output, grad_tokens, grad_in_proj, conv_own[:CONV], conv_own[CONV], grad_out_proj,
        grad_norm, grad_gate, head_all[0], head_all[1], head_all[2],
    )


def solution(mesh):
    n_dp, n_seq = mesh.shape["dp"], mesh.shape["seq"]
    slow = 4 if n_seq % 4 == 0 else 1
    finer = Mesh(
        mesh.devices.reshape(n_dp // 2, 2, slow, n_seq // slow), ("x", "core", "a", "b")
    )
    every = ("x", "core", "a", "b")
    rows, flat, second, copied = P(every, None), P(every), P(None, every), P()
    in_specs = (rows, flat, rows, second, flat, rows, flat, flat, copied, copied, copied, rows)
    out_specs = (rows, rows, rows, second, flat, rows, flat, flat, copied, copied, copied)
    return jax.shard_map(
        on_device, mesh=finer, in_specs=in_specs, out_specs=out_specs, check_vma=False
    )
```

time: 1990 us -> 871 us (0.44)
  waiting for transfers between devices: 845 us -> 242 us
  local copies, waits for them, and re-layouts: 445 us -> 143 us
  matrix products: 322 us -> 104 us
  Pallas kernels: 0 us -> 159 us
  blocking collectives: 126 us -> 0 us
  starting transfers between devices: 10.2 us -> 132 us
  other arithmetic: 176 us -> 76.6 us
    reduce_scatter x2 -> x0, waiting for transfers between devices: 581 us -> none  [the longest x1 372 us: on_device(): lax.psum_scatter(grad_in_proj, ('dp', 'seq'), scatter_dimension=0, tiled=...]
    ppermute x3 -> x98, waiting for transfers between devices: 1.42 us -> 242 us  [the longest x72 180 us: shift(): return lax.ppermute(v, axis, [(i, (i + step) % n) for i in range(n)])]
    dynamic_update_slice x14 -> x58, local copies, waits for them, and re-layouts: 273 us -> 50.2 us  [the longest x33 24.9 us: gather_blocks(): whole = lax.dynamic_update_slice_in_dim(whole, held[:, None], place, 1)]
    dot_general x39 -> x13, matrix products: 322 us -> 104 us  [the longest x5 26.9 us: project(): return jnp.dot(values, weight, preferred_element_type=F32).astype(dtype)]
    all_gather x4 -> x0, waiting for transfers between devices: 186 us -> none  [the longest x1 66 us: prefix(): lax.all_gather(a.astype(kind), axis)]
    pallas_call x0 -> x5, Pallas kernels: none -> 159 us  [the longest x1 70.5 us: on_device(): pl.pallas_call(backward_kernel, grid=grid, in_specs=[tile(rows), per_seq(...]
    ppermute x3 -> x98, starting transfers between devices: 9.96 us -> 132 us  [the longest x72 101 us: shift(): return lax.ppermute(v, axis, [(i, (i + step) % n) for i in range(n)])]
    all_gather x2 -> x0, blocking collectives: 83.8 us -> none  [the longest x1 67.4 us: on_device(): lax.all_gather(conv_weight, ('dp', 'seq'), axis=1, tiled=True)]
  transfers between devices with their start and end apart: 10 -> 98, of which waited for: 8 -> 37; matrix products, arithmetic and copies ran while one was open for 8% -> 32% of each run, Pallas kernels for 0% -> 13%
where the time goes in v1:
time: 871 us; the launch traced here: 859 us
  waiting for transfers between devices  242 us (28%)
  Pallas kernels  159 us (18%)
  local copies, waits for them, and re-layouts  143 us (16%)
  starting transfers between devices  132 us (15%)
  matrix products  104 us (12%)
  other arithmetic  76.6 us (9%)
    ppermute x72, waiting for transfers between devices, shift(): return lax.ppermute(v, axis, [(i, (i + step) % n) for i in range(n)])  180 us
    ppermute x72, starting transfers between devices, shift(): return lax.ppermute(v, axis, [(i, (i + step) % n) for i in range(n)])  101 us
    pallas_call x1, Pallas kernels, on_device(): pl.pallas_call(backward_kernel, grid=grid, in_specs=[tile(rows), per_seq(...  70.5 us
    ppermute x12, waiting for transfers between devices, to_peer(): return lax.ppermute(v, ('x', 'core'), route)  48.8 us
    dot_general x5, matrix products, project(): return jnp.dot(values, weight, preferred_element_type=F32).astype(dtype)  26.9 us
    pallas_call x1, Pallas kernels, on_device(): pl.pallas_call(gate_back_kernel, grid=grid, in_specs=[tile(rows), tile(ro...  25.8 us
    dynamic_update_slice x33, local copies, waits for them, and re-layouts, gather_blocks(): whole = lax.dynamic_update_slice_in_dim(whole, held[:, None], place, 1)  24.9 us
    pallas_call x1, Pallas kernels, on_device(): pl.pallas_call(forward_kernel, grid=grid, in_specs=[tile(rows), per_seq(r...  21.1 us
  transfers between devices with their start and end apart: 98, of which 37 were waited for; matrix products, arithmetic and copies ran while one was open for 32% of the time, Pallas kernels for 13%

profile of v1, /device:TPU:0, one launch (start us, length us, event | category | flops | bytes accessed | tf_op | source)
XLA Modules:
  0.0 859.1 jit_solution(2094311918775983596)
XLA Ops:
  25.3 16.7 %collective-permute-done.29 = s32[528]{0:T(1024)S(1)} collective-permute-done((s32[528]{0:T(1024)S(1)}, s32[528]{0:T(1024)S(1)}, u32[]{:S(2)}, u32[]{:S(2)}) %collective-permute-start.29) | collective-permute-done | bytes 2144 | tf_op jit(solution)/shard_map/ppermute | solution.py:33
  123.4 7.4 collective-permute-start.52
  132.8 17.8 %collective-permute-done.18 = bf16[4,48,1152]{2,1,0:T(8,128)(2,1)S(1)} collective-permute-done((bf16[4,48,1152]{2,1,0:T(8,128)(2,1)}, bf16[4,48,1152]{2,1,0:T(8,128)(2,1)S(1)}, u32[]{:S(2)}, u32[]{:S(2)}) %collective-permute-start.18) | collective-permute-done | bytes 442400 | tf_op jit(solution)/shard_map/ppermute | solution.py:33
  172.5 6.3 collective-permute-done.53
  181.8 7.1 collective-permute-done.39
  200.1 8.1 collective-permute-done.19
  211.9 7.3 collective-permute-done.21
  236.2 6.9 multiply_convert_fusion.1
  246.8 8.4 convolution_convert_fusion
  278.6 6.9 concatenate.79.ct_ref
  287.4 20.8 %conv_and_state.1 = (f32[4,512,768]{2,1,0:T(8,128)S(1)}, bf16[4,512,256]{2,1,0:T(8,128)(2,1)S(1)}, f32[4,128,768]{2,1,0:T(8,128)S(1)}) custom-call(bf16[4,16,768]{2,1,0:T(8,128)(2,1)S(1)} %slice.316.xh_ref, bf16[4,512,768]{2,1,0:T(8,128)(2,1)S(1)} %bitcast.398, bf16[4,16,256]{2,1,0:T(8,128)(2,1)S(1)} %slice.318.bh_ref, bf16[4,512,256]{2,1,0:T(8,128)(2,1)S(1)} %bitcast.400, ...), custom_call_target="tpu_custom_call" | custom-call | flops 402653184 | bytes 12582912 | tf_op jit(solution)/shard_map/conv_and_state/pallas_call | solution.py:575
  317.2 9.0 %fusion.1.z_ref = f32[4,512,768]{2,1,0:T(8,128)} fusion(bf16[1536,768,1]{1,0,2:T(8,128)(2,1)} %bitcast.79, f32[1536]{0:T(1024)S(1)} %mul.181, f32[4,512]{1,0:T(4,128)S(1)} %get-tuple-element.122, bf16[1,512,1536]{2,1,0:T(8,128)(2,1)S(1)} %bitcast.423, bf16[1,512,1536]{2,1,0:T(8,128)(2,1)S(1)} %bitcast.417, bf16[1,512,1536]{2,1,0:T(8,128)(2,1)} %bitcast.38, ...), kind=kOutput, calls=%fused_computation.14 | convolution fusion | flops 4853858304 | bytes 14956544 | tf_op jit(solution)/shard_map/dot_general | solution.py:508
  326.2 10.1 %fusion.25.dn_ref = f32[4,512,768]{2,1,0:T(8,128)} fusion(bf16[768,1536,1]{1,0,2:T(8,128)(2,1)} %bitcast.94, bf16[1,512,1536]{2,1,0:T(8,128)(2,1)} %bitcast.83, bf16[1,512,1536]{2,1,0:T(8,128)(2,1)} %bitcast.82, bf16[1,512,1536]{2,1,0:T(8,128)(2,1)} %bitcast.81, bf16[1,512,1536]{2,1,0:T(8,128)(2,1)} %bitcast.80), kind=kOutput, calls=%fused_computation.47 | convolution fusion | flops 4841275392 | bytes 14942208 | tf_op jit(solution)/shard_map/qtd,cd->qtc/dot_general | solution.py:619
  337.4 21.1 %mix_within_block.1.yl_ref = f32[4,512,768]{2,1,0:T(8,128)S(1)} custom-call(f32[4,512,768]{2,1,0:T(8,128)} %copy-done.1, bf16[4,512,256]{2,1,0:T(8,128)(2,1)S(1)} %get-tuple-element.30.bc_ref, f32[4,512,128]{2,1,0:T(8,128)S(1)} %concatenate.79.ct_ref, f32[4,24,512]{2,1,0:T(8,128)S(1)} %fusion.72.rt_ref, f32[4,8,768]{2,1,0:T(8,128)S(1)} %pad_maximum_fusion.9.ln_ref), custom_call_target="tpu_custom_call" | custom-call | flops 3221225472 | bytes 12582912 | tf_op jit(solution)/shard_map/mix_within_block/pallas_call | solution.py:606
  363.7 20.3 %gate.1 = (f32[4,512,768]{2,1,0:T(8,128)S(1)}, f32[4,512,128]{2,1,0:T(8,128)S(1)}) custom-call(f32[4,512,768]{2,1,0:T(8,128)} %copy-done, bf16[4,512,256]{2,1,0:T(8,128)(2,1)S(1)} %get-tuple-element.30.bc_ref, f32[4,128,768]{2,1,0:T(8,128)S(1)} %multiply_add_fusion.1.inc_ref, f32[4,512,768]{2,1,0:T(8,128)} %fusion.1.z_ref, f32[4,512,768]{2,1,0:T(8,128)} %fusion.25.dn_ref, ...), custom_call_target="tpu_custom_call" | custom-call | flops 402653184 | bytes 25165824 | tf_op jit(solution)/shard_map/gate/pallas_call | solution.py:621
  391.2 8.7 %copy.274 = bf16[1536,2048]{1,0:T(8,128)(2,1)} copy(bf16[1536,2048]{0,1:T(8,128)(2,1)} %bitcast.409) | data formatting | bytes 12582912 | tf_op jit(solution)/shard_map/dot_general | solution.py:661
  402.8 25.8 %gate_back.1 = (bf16[4,512,768]{2,1,0:T(8,128)(2,1)S(1)}, f32[4,512,768]{2,1,0:T(8,128)}, bf16[4,512,768]{2,1,0:T(8,128)(2,1)S(1)}, f32[4,128,768]{2,1,0:T(8,128)S(1)}, f32[4,8,768]{2,1,0:T(8,128)S(1)}) custom-call(f32[4,512,768]{2,1,0:T(8,128)} %copy-done.4, f32[4,512,768]{2,1,0:T(8,128)} %fusion.1.z_ref, f32[4,512,768]{2,1,0:T(8,128)} %fusion.25.dn_ref, ...), custom_call_target="tpu_custom_call" | custom-call | flops 402653184 | bytes 31457280 | tf_op jit(solution)/shard_map/gate_back/pallas_call | solution.py:636
  428.6 7.6 fusion.24
  436.2 12.4 %fusion.114 = (bf16[4,512,1536]{2,1,0:T(8,128)(2,1)}, f32[4,512,1536]{2,1,0:T(8,128)}) fusion(bf16[4,512,768]{2,1,0:T(8,128)(2,1)S(1)} %get-tuple-element.34, bf16[768,1536,1]{1,0,2:T(8,128)(2,1)} %bitcast.94), kind=kOutput, calls=%fused_computation.295 | convolution fusion | flops 4834983936 | bytes 24379392 | tf_op jit(solution)/shard_map/qtc,cd->qtd/dot_general | solution.py:656
  462.5 9.9 %fusion.115 = f32[2048,1536]{1,0:T(8,128)} fusion(bf16[2048,768]{1,0:T(8,128)(2,1)S(1)} %bitcast.403, bf16[1536,768]{1,0:T(8,128)(2,1)} %bitcast.78), kind=kOutput, calls=%fused_computation.296 | convolution fusion | flops 4831838208 | bytes 18087936 | tf_op jit(solution)/shard_map/dot_general | solution.py:711
  480.4 21.5 %collective-permute-done.71 = bf16[4,48,768]{2,1,0:T(8,128)(2,1)} collective-permute-done((bf16[4,48,768]{2,1,0:T(8,128)(2,1)}, bf16[4,48,768]{2,1,0:T(8,128)(2,1)}, u32[]{:S(2)}, u32[]{:S(2)}) %collective-permute-start.71) | collective-permute-done | bytes 294944 | tf_op jit(solution)/shard_map/ppermute | solution.py:33
  516.1 12.0 %collective-permute-done.68 = bf16[4,48,768]{2,1,0:T(8,128)(2,1)S(1)} collective-permute-done((bf16[4,48,768]{2,1,0:T(8,128)(2,1)S(1)}, bf16[4,48,768]{2,1,0:T(8,128)(2,1)S(1)}, u32[]{:S(2)}, u32[]{:S(2)}) %collective-permute-start.68) | collective-permute-done | bytes 294944 | tf_op jit(solution)/shard_map/ppermute | solution.py:33
  530.6 10.9 %collective-permute-done.70 = bf16[4,48,768]{2,1,0:T(8,128)(2,1)S(1)} collective-permute-done((bf16[4,48,768]{2,1,0:T(8,128)(2,1)S(1)}, bf16[4,48,768]{2,1,0:T(8,128)(2,1)S(1)}, u32[]{:S(2)}, u32[]{:S(2)}) %collective-permute-start.70) | collective-permute-done | bytes 294944 | tf_op jit(solution)/shard_map/ppermute | solution.py:33
  541.4 14.7 %collective-permute-start.95 = (bf16[1,96,1536]{2,1,0:T(8,128)(2,1)}, bf16[1,96,1536]{2,1,0:T(8,128)(2,1)}, u32[]{:S(2)}, u32[]{:S(2)}) collective-permute-start(bf16[1,96,1536]{2,1,0:T(8,128)(2,1)} %get-tuple-element.77), channel_id=1, source_target_pairs={{0,4},{2,6},{4,0},{6,2},{1,5},{3,7},{5,1},{7,3},{8,12},{10,14},{12... | collective-permute-start | bytes 884744 | tf_op jit(solution)/shard_map/ppermute | solution.py:33
  561.9 70.5 %mix_back.1 = (bf16[4,512,768]{2,1,0:T(8,128)(2,1)S(1)}, bf16[4,16,768]{2,1,0:T(8,128)(2,1)S(1)}, bf16[4,512,256]{2,1,0:T(8,128)(2,1)S(1)}, bf16[4,16,256]{2,1,0...) custom-call(f32[4,512,768]{2,1,0:T(8,128)} %copy-done.1, ...), custom_call_target="tpu_custom_call" | custom-call | flops 8053063680 | bytes 25165824 | tf_op jit(solution)/shard_map/mix_back/pallas_call | solution.py:667
  648.8 18.8 %multiply_reduce_fusion = (f32[1536]{0:T(1024)S(1)}, bf16[2048,1536]{1,0:T(8,128)(2,1)}, f32[2048,1536]{1,0:T(8,128)}) fusion(f32[2048]{0:T(1024)S(1)} %bitcast.453, bf16[1,512,1536]{2,1,0:T(8,128)(2,1)} %bitcast.422, bf16[1,512,1536]{2,1,0:T(8,128)(2,1)S(1)} %bitcast.418, bf16[1,512,1536]{2,1,0:T(8,128)(2,1)} %bitcast.38, ...), kind=kOutput, calls=%fused_computation.1 | convolution fusion | flops 7276067328 | bytes 46020608 | tf_op jit(solution)/shard_map/dot_general | solution.py:710
  680.6 12.0 %fusion.117 = f32[4,8,48,1152]{3,2,1,0:T(8,128)S(1)} fusion(bf16[4,8,48,2048]{3,2,1,0:T(8,128)(2,1)} %bitcast.410, bf16[2048,1152,1,1]{1,0,3,2:T(8,128)(2,1)} %bitcast.425), kind=kOutput, calls=%fused_computation.298 | convolution fusion | flops 7247757312 | bytes 18087936 | tf_op jit(solution)/shard_map/dot_general | solution.py:661
  712.1 9.3 %collective-permute-done.76 = bf16[4,48,1152]{2,1,0:T(8,128)(2,1)} collective-permute-done((bf16[4,48,1152]{2,1,0:T(8,128)(2,1)}, bf16[4,48,1152]{2,1,0:T(8,128)(2,1)}, u32[]{:S(2)}, u32[]{:S(2)}) %collective-permute-start.76) | collective-permute-done | bytes 442400 | tf_op jit(solution)/shard_map/ppermute | solution.py:33
  721.5 9.5 %collective-permute-done.78 = bf16[4,48,1152]{2,1,0:T(8,128)(2,1)} collective-permute-done((bf16[4,48,1152]{2,1,0:T(8,128)(2,1)}, bf16[4,48,1152]{2,1,0:T(8,128)(2,1)}, u32[]{:S(2)}, u32[]{:S(2)}) %collective-permute-start.78) | collective-permute-done | bytes 442400 | tf_op jit(solution)/shard_map/ppermute | solution.py:33
  749.7 12.5 %collective-permute-done.77 = bf16[4,48,1152]{2,1,0:T(8,128)(2,1)S(1)} collective-permute-done((bf16[4,48,1152]{2,1,0:T(8,128)(2,1)S(1)}, bf16[4,48,1152]{2,1,0:T(8,128)(2,1)S(1)}, u32[]{:S(2)}, u32[]{:S(2)}) %collective-permute-start.77) | collective-permute-done | bytes 442400 | tf_op jit(solution)/shard_map/ppermute | solution.py:33
  771.8 48.5 %collective-permute-done.83 = bf16[48,1152]{1,0:T(8,128)(2,1)S(1)} collective-permute-done((bf16[48,1152]{1,0:T(8,128)(2,1)}, bf16[48,1152]{1,0:T(8,128)(2,1)S(1)}, u32[]{:S(2)}, u32[]{:S(2)}) %collective-permute-start.83) | collective-permute-done | bytes 110624 | tf_op jit(solution)/shard_map/ppermute | solution.py:45
  851.6 7.2 fusion.9
  (606 shorter events, 370.4 us)
Async XLA Ops:
  5.2 217.3 %collective-permute-start.25 = (bf16[512,1536]{1,0:T(8,128)(2,1)}, bf16[512,1536]{1,0:T(8,128)(2,1)S(1)}, u32[]{:S(2)}, u32[]{:S(2)}) collective-permute-start(bf16[512,1536]{1,0:T(8,128)(2,1)} %param.12), channel_id=1, source_target_pairs={{0,16},{16,0},{1,17},{17,1},{2,18},{18,2},{3,19},{19,3},{4,20},{20... | collective-permute-start | bytes 4718600 | tf_op jit(solution)/shard_map/ppermute | solution.py:33
  25.1 207.4 %collective-permute-start.24 = (bf16[512,1536]{1,0:T(8,128)(2,1)S(1)}, bf16[512,1536]{1,0:T(8,128)(2,1)}, u32[]{:S(2)}, u32[]{:S(2)}) collective-permute-start(bf16[512,1536]{1,0:T(8,128)(2,1)S(1)} %copy-done.19), channel_id=1, source_target_pairs={{0,8},{8,0},{1,9},{9,1},{2,10},{10,2},{3,11},{11,3},{4,12},{12,4},... | collective-permute-start | bytes 4718600 | tf_op jit(solution)/shard_map/ppermute | solution.py:33
  42.0 34.4 %collective-permute-start.34 = (bf16[48,768]{1,0:T(8,128)(2,1)}, bf16[48,768]{1,0:T(8,128)(2,1)}, u32[]{:S(2)}, u32[]{:S(2)}) collective-permute-start(bf16[48,768]{1,0:T(8,128)(2,1)} %get-tuple-element.94), channel_id=1, source_target_pairs={{0,8},{8,0},{16,24},{24,16},{1,9},{9,1},{17,25},{25,17},{2,10},{10... | collective-permute-start | bytes 221192 | tf_op jit(solution)/shard_map/ppermute | solution.py:45
  100.7 52.7 %collective-permute-start.50 = (bf16[1,96,1536]{2,1,0:T(8,128)(2,1)}, bf16[1,96,1536]{2,1,0:T(8,128)(2,1)}, u32[]{:S(2)}, u32[]{:S(2)}) collective-permute-start(bf16[1,96,1536]{2,1,0:T(8,128)(2,1)} %bitcast.85), channel_id=1, source_target_pairs={{0,4},{2,6},{4,0},{6,2},{1,5},{3,7},{5,1},{7,3},{8,12},{10,14},{12... | collective-permute-start | bytes 884744 | tf_op jit(solution)/shard_map/ppermute | solution.py:33
  123.4 40.3 %collective-permute-start.52 = (bf16[1,96,1536]{2,1,0:T(8,128)(2,1)}, bf16[1,96,1536]{2,1,0:T(8,128)(2,1)S(1)}, u32[]{:S(2)}, u32[]{:S(2)}) collective-permute-start(bf16[1,96,1536]{2,1,0:T(8,128)(2,1)} %bitcast.85), channel_id=1, source_target_pairs={{0,6},{2,0},{4,2},{6,4},{1,7},{3,1},{5,3},{7,5},{8,14},{10,8},{12,... | collective-permute-start | bytes 884744 | tf_op jit(solution)/shard_map/ppermute | solution.py:33
  199.0 33.4 %collective-permute-start.45 = (bf16[512,1536]{1,0:T(8,128)(2,1)}, bf16[512,1536]{1,0:T(8,128)(2,1)}, u32[]{:S(2)}, u32[]{:S(2)}) collective-permute-start(bf16[512,1536]{1,0:T(8,128)(2,1)} %param.23), channel_id=1, source_target_pairs={{0,16},{16,0},{1,17},{17,1},{2,18},{18,2},{3,19},{19,3},{4,20},{20... | collective-permute-start | bytes 4718600 | tf_op jit(solution)/shard_map/ppermute | solution.py:33
  211.9 114.3 %collective-permute-start.44 = (bf16[512,1536]{1,0:T(8,128)(2,1)}, bf16[512,1536]{1,0:T(8,128)(2,1)}, u32[]{:S(2)}, u32[]{:S(2)}) collective-permute-start(bf16[512,1536]{1,0:T(8,128)(2,1)} %param.23), channel_id=1, source_target_pairs={{0,8},{8,0},{1,9},{9,1},{2,10},{10,2},{3,11},{11,3},{4,12},{12,4},... | collective-permute-start | bytes 4718600 | tf_op jit(solution)/shard_map/ppermute | solution.py:33
  232.4 93.8 %collective-permute-start.46 = (bf16[512,1536]{1,0:T(8,128)(2,1)}, bf16[512,1536]{1,0:T(8,128)(2,1)}, u32[]{:S(2)}, u32[]{:S(2)}) collective-permute-start(bf16[512,1536]{1,0:T(8,128)(2,1)} %collective-permute-done.45), channel_id=1, source_target_pairs={{0,8},{8,0},{1,9},{9,1},{2,10},{10,2},{3,11},{11,3},{4,12},{12,4},... | collective-permute-start | bytes 4718600 | tf_op jit(solution)/shard_map/ppermute | solution.py:33
  308.3 53.7 %collective-permute-start.31 = (bf16[4,128,768]{2,1,0:T(8,128)(2,1)S(1)}, bf16[4,128,768]{2,1,0:T(8,128)(2,1)}, u32[]{:S(2)}, u32[]{:S(2)}) collective-permute-start(bf16[4,128,768]{2,1,0:T(8,128)(2,1)S(1)} %convert_element_type.428), channel_id=1, source_target_pairs={{0,1},{1,2},{2,3},{3,4},{4,5},{5,6},{6,7},{8,9},{9,10},{10,11},{11... | collective-permute-start | bytes 2359304 | tf_op jit(solution)/shard_map/ppermute | solution.py:39
  313.2 48.9 %collective-permute-start.33 = (bf16[4,128,768]{2,1,0:T(8,128)(2,1)S(1)}, bf16[4,128,768]{2,1,0:T(8,128)(2,1)}, u32[]{:S(2)}, u32[]{:S(2)}) collective-permute-start(bf16[4,128,768]{2,1,0:T(8,128)(2,1)S(1)} %convert_element_type.428), channel_id=1, source_target_pairs={{0,2},{1,3},{2,4},{3,5},{4,6},{5,7},{8,10},{9,11},{10,12},{11,13},... | collective-permute-start | bytes 2359304 | tf_op jit(solution)/shard_map/ppermute | solution.py:39
  315.4 45.9 %collective-permute-start.32 = (f32[4,12]{1,0:T(4,128)}, f32[4,12]{1,0:T(4,128)}, u32[]{:S(2)}, u32[]{:S(2)}) collective-permute-start(f32[4,12]{1,0:T(4,128)} %mul.403), channel_id=1, source_target_pairs={{0,1},{1,2},{2,3},{3,4},{4,5},{5,6},{6,7},{8,9},{9,10},{10,11},{11... | collective-permute-start | bytes 584 | tf_op jit(solution)/shard_map/ppermute | solution.py:39
  452.2 52.8 %collective-permute-start.94 = (bf16[1,96,1536]{2,1,0:T(8,128)(2,1)}, bf16[1,96,1536]{2,1,0:T(8,128)(2,1)}, u32[]{:S(2)}, u32[]{:S(2)}) collective-permute-start(bf16[1,96,1536]{2,1,0:T(8,128)(2,1)} %get-tuple-element.73), channel_id=1, source_target_pairs={{0,1},{1,0},{2,3},{3,2},{4,5},{5,4},{6,7},{7,6},{8,9},{9,8},{10,11... | collective-permute-start | bytes 884744 | tf_op jit(solution)/shard_map/ppermute | solution.py:33
  460.5 41.4 %collective-permute-start.71 = (bf16[4,48,768]{2,1,0:T(8,128)(2,1)}, bf16[4,48,768]{2,1,0:T(8,128)(2,1)}, u32[]{:S(2)}, u32[]{:S(2)}) collective-permute-start(bf16[4,48,768]{2,1,0:T(8,128)(2,1)} %get-tuple-element.80), channel_id=1, source_target_pairs={{0,1},{1,0},{2,3},{3,2},{4,5},{5,4},{6,7},{7,6},{8,9},{9,8},{10,11... | collective-permute-start | bytes 884744 | tf_op jit(solution)/shard_map/ppermute | solution.py:33
  474.3 33.9 %collective-permute-start.96 = (bf16[1,96,1536]{2,1,0:T(8,128)(2,1)}, bf16[1,96,1536]{2,1,0:T(8,128)(2,1)}, u32[]{:S(2)}, u32[]{:S(2)}) collective-permute-start(bf16[1,96,1536]{2,1,0:T(8,128)(2,1)} %get-tuple-element.72), channel_id=1, source_target_pairs={{0,1},{1,0},{2,3},{3,2},{4,5},{5,4},{6,7},{7,6},{8,9},{9,8},{10,11... | collective-permute-start | bytes 884744 | tf_op jit(solution)/shard_map/ppermute | solution.py:33
  474.6 38.9 %collective-permute-start.66 = (bf16[4,48,768]{2,1,0:T(8,128)(2,1)}, bf16[4,48,768]{2,1,0:T(8,128)(2,1)}, u32[]{:S(2)}, u32[]{:S(2)}) collective-permute-start(bf16[4,48,768]{2,1,0:T(8,128)(2,1)} %get-tuple-element.78), channel_id=1, source_target_pairs={{0,1},{1,0},{2,3},{3,2},{4,5},{5,4},{6,7},{7,6},{8,9},{9,8},{10,11... | collective-permute-start | bytes 884744 | tf_op jit(solution)/shard_map/ppermute | solution.py:33
  479.1 79.1 %collective-permute-start.59 = (bf16[4,128,768]{2,1,0:T(8,128)(2,1)S(1)}, bf16[4,128,768]{2,1,0:T(8,128)(2,1)S(1)}, u32[]{:S(2)}, u32[]{:S(2)}) collective-permute-start(bf16[4,128,768]{2,1,0:T(8,128)(2,1)S(1)} %convert_element_type.439), channel_id=1, source_target_pairs={{1,0},{2,1},{3,2},{4,3},{5,4},{6,5},{7,6},{9,8},{10,9},{11,10},{12... | collective-permute-start | bytes 2359304 | tf_op jit(solution)/shard_map/ppermute | solution.py:39
  501.9 59.7 %collective-permute-start.61 = (bf16[4,128,768]{2,1,0:T(8,128)(2,1)S(1)}, bf16[4,128,768]{2,1,0:T(8,128)(2,1)S(1)}, u32[]{:S(2)}, u32[]{:S(2)}) collective-permute-start(bf16[4,128,768]{2,1,0:T(8,128)(2,1)S(1)} %convert_element_type.439), channel_id=1, source_target_pairs={{2,0},{3,1},{4,2},{5,3},{6,4},{7,5},{10,8},{11,9},{12,10},{13,11},... | collective-permute-start | bytes 2359304 | tf_op jit(solution)/shard_map/ppermute | solution.py:39
  508.2 33.2 %collective-permute-start.70 = (bf16[4,48,768]{2,1,0:T(8,128)(2,1)S(1)}, bf16[4,48,768]{2,1,0:T(8,128)(2,1)S(1)}, u32[]{:S(2)}, u32[]{:S(2)}) collective-permute-start(bf16[4,48,768]{2,1,0:T(8,128)(2,1)S(1)} %get-tuple-element.84), channel_id=1, source_target_pairs={{0,4},{2,6},{4,0},{6,2},{1,5},{3,7},{5,1},{7,3},{8,12},{10,14},{12... | collective-permute-start | bytes 884744 | tf_op jit(solution)/shard_map/ppermute | solution.py:33
  528.1 141.3 %collective-permute-start.91 = (bf16[1,96,1536]{2,1,0:T(8,128)(2,1)}, bf16[1,96,1536]{2,1,0:T(8,128)(2,1)}, u32[]{:S(2)}, u32[]{:S(2)}) collective-permute-start(bf16[1,96,1536]{2,1,0:T(8,128)(2,1)} %get-tuple-element.71), channel_id=1, source_target_pairs={{0,1},{1,0},{2,3},{3,2},{4,5},{5,4},{6,7},{7,6},{8,9},{9,8},{10,11... | collective-permute-start | bytes 884744 | tf_op jit(solution)/shard_map/ppermute | solution.py:33
  541.4 128.2 %collective-permute-start.93 = (bf16[1,96,1536]{2,1,0:T(8,128)(2,1)}, bf16[1,96,1536]{2,1,0:T(8,128)(2,1)}, u32[]{:S(2)}, u32[]{:S(2)}) collective-permute-start(bf16[1,96,1536]{2,1,0:T(8,128)(2,1)} %get-tuple-element.75), channel_id=1, source_target_pairs={{0,2},{2,4},{4,6},{6,0},{1,3},{3,5},{5,7},{7,1},{8,10},{10,12},{12... | collective-permute-start | bytes 884744 | tf_op jit(solution)/shard_map/ppermute | solution.py:33
  541.4 129.6 %collective-permute-start.95 = (bf16[1,96,1536]{2,1,0:T(8,128)(2,1)}, bf16[1,96,1536]{2,1,0:T(8,128)(2,1)}, u32[]{:S(2)}, u32[]{:S(2)}) collective-permute-start(bf16[1,96,1536]{2,1,0:T(8,128)(2,1)} %get-tuple-element.77), channel_id=1, source_target_pairs={{0,4},{2,6},{4,0},{6,2},{1,5},{3,7},{5,1},{7,3},{8,12},{10,14},{12... | collective-permute-start | bytes 884744 | tf_op jit(solution)/shard_map/ppermute | solution.py:33
  558.2 113.1 %collective-permute-start.97 = (bf16[1,96,1536]{2,1,0:T(8,128)(2,1)}, bf16[1,96,1536]{2,1,0:T(8,128)(2,1)}, u32[]{:S(2)}, u32[]{:S(2)}) collective-permute-start(bf16[1,96,1536]{2,1,0:T(8,128)(2,1)} %get-tuple-element.76), channel_id=1, source_target_pairs={{0,6},{2,0},{4,2},{6,4},{1,7},{3,1},{5,3},{7,5},{8,14},{10,8},{12,... | collective-permute-start | bytes 884744 | tf_op jit(solution)/shard_map/ppermute | solution.py:33
  669.0 64.3 %collective-permute-start.57 = (bf16[512,1536]{1,0:T(8,128)(2,1)S(1)}, bf16[512,1536]{1,0:T(8,128)(2,1)}, u32[]{:S(2)}, u32[]{:S(2)}) collective-permute-start(bf16[512,1536]{1,0:T(8,128)(2,1)S(1)} %copy-done.40), channel_id=1, source_target_pairs={{0,8},{8,0},{1,9},{9,1},{2,10},{10,2},{3,11},{11,3},{4,12},{12,4},... | collective-permute-start | bytes 4718600 | tf_op jit(solution)/shard_map/ppermute | solution.py:33
  669.4 29.1 %collective-permute-start.80 = (bf16[48,768]{1,0:T(8,128)(2,1)S(1)}, bf16[48,768]{1,0:T(8,128)(2,1)S(1)}, u32[]{:S(2)}, u32[]{:S(2)}) collective-permute-start(bf16[48,768]{1,0:T(8,128)(2,1)S(1)} %get-tuple-element.106), channel_id=1, source_target_pairs={{0,8},{8,0},{16,24},{24,16},{1,9},{9,1},{17,25},{25,17},{2,10},{10... | collective-permute-start | bytes 221192 | tf_op jit(solution)/shard_map/ppermute | solution.py:45
  671.0 29.5 %collective-permute-start.84 = (bf16[48,768]{1,0:T(8,128)(2,1)S(1)}, bf16[48,768]{1,0:T(8,128)(2,1)S(1)}, u32[]{:S(2)}, u32[]{:S(2)}) collective-permute-start(bf16[48,768]{1,0:T(8,128)(2,1)S(1)} %get-tuple-element.104), channel_id=1, source_target_pairs={{0,24},{8,16},{16,8},{24,0},{1,25},{9,17},{17,9},{25,1},{2,26},{10... | collective-permute-start | bytes 221192 | tf_op jit(solution)/shard_map/ppermute | solution.py:45
  700.6 30.3 %collective-permute-start.78 = (bf16[4,48,1152]{2,1,0:T(8,128)(2,1)}, bf16[4,48,1152]{2,1,0:T(8,128)(2,1)}, u32[]{:S(2)}, u32[]{:S(2)}) collective-permute-start(bf16[4,48,1152]{2,1,0:T(8,128)(2,1)} %get-tuple-element.62), channel_id=1, source_target_pairs={{0,1},{1,0},{2,3},{3,2},{4,5},{5,4},{6,7},{7,6},{8,9},{9,8},{10,11... | collective-permute-start | bytes 1327112 | tf_op jit(solution)/shard_map/ppermute | solution.py:33
  703.0 37.2 %collective-permute-start.64 = (bf16[512,1536]{1,0:T(8,128)(2,1)}, bf16[512,1536]{1,0:T(8,128)(2,1)}, u32[]{:S(2)}, u32[]{:S(2)}) collective-permute-start(bf16[512,1536]{1,0:T(8,128)(2,1)} %get-tuple-element.68), channel_id=1, source_target_pairs={{0,8},{8,0},{1,9},{9,1},{2,10},{10,2},{3,11},{11,3},{4,12},{12,4},... | collective-permute-start | bytes 4718600 | tf_op jit(solution)/shard_map/ppermute | solution.py:33
  712.0 139.7 %collective-permute-start.56 = (bf16[512,1536]{1,0:T(8,128)(2,1)}, bf16[512,1536]{1,0:T(8,128)(2,1)}, u32[]{:S(2)}, u32[]{:S(2)}) collective-permute-start(bf16[512,1536]{1,0:T(8,128)(2,1)} %get-tuple-element.69), channel_id=1, source_target_pairs={{0,8},{8,0},{1,9},{9,1},{2,10},{10,2},{3,11},{11,3},{4,12},{12,4},... | collective-permute-start | bytes 4718600 | tf_op jit(solution)/shard_map/ppermute | solution.py:33
  747.3 100.9 %collective-permute-start.63 = (bf16[512,1536]{1,0:T(8,128)(2,1)}, bf16[512,1536]{1,0:T(8,128)(2,1)S(1)}, u32[]{:S(2)}, u32[]{:S(2)}) collective-permute-start(bf16[512,1536]{1,0:T(8,128)(2,1)} %get-tuple-element.67), channel_id=1, source_target_pairs={{0,8},{8,0},{1,9},{9,1},{2,10},{10,2},{3,11},{11,3},{4,12},{12,4},... | collective-permute-start | bytes 4718600 | tf_op jit(solution)/shard_map/ppermute | solution.py:33
  748.2 103.4 %collective-permute-start.58 = (bf16[512,1536]{1,0:T(8,128)(2,1)}, bf16[512,1536]{1,0:T(8,128)(2,1)}, u32[]{:S(2)}, u32[]{:S(2)}) collective-permute-start(bf16[512,1536]{1,0:T(8,128)(2,1)} %fusion.14), channel_id=1, source_target_pairs={{0,16},{16,0},{1,17},{17,1},{2,18},{18,2},{3,19},{19,3},{4,20},{20... | collective-permute-start | bytes 4718600 | tf_op jit(solution)/shard_map/ppermute | solution.py:33
  762.2 85.9 %collective-permute-start.65 = (bf16[512,1536]{1,0:T(8,128)(2,1)}, bf16[512,1536]{1,0:T(8,128)(2,1)}, u32[]{:S(2)}, u32[]{:S(2)}) collective-permute-start(bf16[512,1536]{1,0:T(8,128)(2,1)} %fusion.10), channel_id=1, source_target_pairs={{0,16},{16,0},{1,17},{17,1},{2,18},{18,2},{3,19},{19,3},{4,20},{20... | collective-permute-start | bytes 4718600 | tf_op jit(solution)/shard_map/ppermute | solution.py:33
  767.5 52.9 %collective-permute-start.83 = (bf16[48,1152]{1,0:T(8,128)(2,1)}, bf16[48,1152]{1,0:T(8,128)(2,1)S(1)}, u32[]{:S(2)}, u32[]{:S(2)}) collective-permute-start(bf16[48,1152]{1,0:T(8,128)(2,1)} %get-tuple-element.91), channel_id=1, source_target_pairs={{0,16},{8,24},{16,0},{24,8},{1,17},{9,25},{17,1},{25,9},{2,18},{10... | collective-permute-start | bytes 331784 | tf_op jit(solution)/shard_map/ppermute | solution.py:45
  (142 other events, 2526.6 us)

commit v2 on v1

v2 whole, which is shorter than its diff:
```python
import jax
import jax.numpy as jnp
from jax import lax
from jax.experimental import pallas as pl
from jax.experimental.pallas import tpu as pltpu
from jax.sharding import Mesh
from jax.sharding import PartitionSpec as P

INNER = 3072
HEADDIM = 64
STATE = 128
CONV = 4
GROUP = 256
HEADS = 48
XBC = 3328
LONGEST = 1024
HALO = 16
PAIRS = 3
WIDE = PAIRS * 128
LAST = WIDE + 3 * 128

EPSILON = 1e-05
BF = jnp.bfloat16
F32 = jnp.float32
NEVER = -1e30

CUM, DT, CARRY, ENDN, SAME, SEG = 0, 16, 32, 48, 64, 67
SEG_ROW = 16


def shift(v, axis, step):
    n = lax.axis_size(axis)
    return lax.ppermute(v, axis, [(i, (i + step) % n) for i in range(n)])


def along(v, step):
    n = lax.axis_size("a") * lax.axis_size("b")
    route = [(i, i + step) for i in range(n) if 0 <= i + step < n]
    return lax.ppermute(v, ("a", "b"), route)


def exchange(v, axes):
    return lax.all_to_all(v, axes, 0, 0, tiled=True)


def group_of(sx, sc):
    x, c, n = lax.axis_index("x"), lax.axis_index("core"), lax.axis_size("x")
    return lax.rem(x + sx + n, n) * 2 + (c + sc) % 2


def position_of(sa, sb):
    na, nb = lax.axis_size("a"), lax.axis_size("b")
    a, b = lax.axis_index("a"), lax.axis_index("b")
    return lax.rem(a + sa + na, na) * nb + lax.rem(b + sb + nb, nb)


def after(v, *others):
    def nothing(*refs):
        pass

    anywhere = pl.BlockSpec(memory_space=pl.ANY)
    return pl.pallas_call(
        nothing,
        in_specs=[anywhere] * (1 + len(others)),
        out_specs=anywhere,
        out_shape=jax.ShapeDtypeStruct(v.shape, v.dtype),
        input_output_aliases={0: 0},
        name="in_order",
    )(v, *others)


def gather_over_x(v):
    return [v] + [shift(v, "x", sx) for sx in range(1, lax.axis_size("x"))]


def gather_over_cores(along_x, *others):
    slots = []
    for sx, here in enumerate(along_x):
        here = after(here, *others) if sx else here
        slots += [here, shift(here, "core", 1)]
    return slots


def sum_over_cores(kept, sent):
    both = kept + shift(sent.astype(BF), "core", 1).astype(F32)
    return both[0], [both[sx].astype(BF) for sx in range(1, lax.axis_size("x"))]


def sum_to_owner(own, others):
    total = own
    for sx in range(1, lax.axis_size("x")):
        total = total + shift(others[sx - 1], "x", -sx).astype(F32)
    return total


def sum_over_group(v):
    n = lax.axis_size("x")
    v = v.reshape((n, 2) + v.shape[1:])
    v = v + shift(v, "core", 1)[:, ::-1]
    total = v
    for step in range(1, n):
        total = total + jnp.roll(shift(v, "x", step), step, axis=0)
    return total.reshape((n * 2,) + v.shape[2:])


def gather_over_a(block):
    return exchange(jnp.broadcast_to(block[None], (lax.axis_size("a"),) + block.shape), "a")


def gather_over_b(v):
    return [v] + [shift(v, "b", sb) for sb in range(1, lax.axis_size("b"))]


def sum_over_b(parts, *others):
    total = (after(parts[0], *others) if others else parts[0]).astype(F32)
    for rb in range(1, lax.axis_size("b")):
        total = total + shift(parts[rb], "b", rb).astype(F32)
    return total.astype(BF)


def sum_over_a(parts):
    return jnp.sum(exchange(parts, "a").astype(F32), axis=0)


def sum_over(v, axes, marks=()):
    marks = list(marks)
    for axis in axes:
        step, n = 1, lax.axis_size(axis)
        while step < n:
            moved = lax.ppermute(v, axis, [(i, i ^ step) for i in range(n)])
            v = (after(v, marks.pop(0)) if marks else v) + moved
            step *= 2
    return v


def nn(a, b):
    return lax.dot_general(a, b, (((1,), (0,)), ((), ())), preferred_element_type=F32)


def nt(a, b):
    return lax.dot_general(a, b, (((1,), (1,)), ((), ())), preferred_element_type=F32)


def tn(a, b):
    return lax.dot_general(a, b, (((0,), (0,)), ((), ())), preferred_element_type=F32)


def low_half(rows):
    return lax.broadcasted_iota(jnp.int32, (rows, 128), 1) < HEADDIM


def spread(table, kind, pair):
    at = kind + 2 * pair
    return jnp.where(low_half(table.shape[0]), table[:, at : at + 1], table[:, at + 1 : at + 2])


def lanes_of(pair):
    return slice(pair * 128, (pair + 1) * 128)


def rows_of(chunk):
    return slice(chunk * GROUP, (chunk + 1) * GROUP)


def end_of(chunk):
    return slice((chunk + 1) * GROUP - 1, (chunk + 1) * GROUP)


def from_start(carry, chunks):
    out, run = [carry[rows_of(0)]], carry[end_of(0)]
    for c in range(1, chunks):
        out.append(carry[rows_of(c)] * run)
        run = run * carry[end_of(c)]
    return jnp.concatenate(out, axis=0)


def to_block_end(endn, carry, chunks):
    out, run = [endn[rows_of(chunks - 1)]], carry[end_of(chunks - 1)]
    for c in range(chunks - 2, -1, -1):
        out.insert(0, endn[rows_of(c)] * run)
        run = run * carry[end_of(c)]
    return jnp.concatenate(out, axis=0)


def convolved(ext, taps, same):
    rows = ext.shape[0] - HALO
    pre = taps[CONV : CONV + 1] + taps[CONV - 1 : CONV] * ext[HALO:]
    for k in range(1, CONV):
        pre = pre + same[k - 1] * (taps[CONV - 1 - k : CONV - k] * ext[HALO - k : HALO - k + rows])
    return pre


def extended(v):
    rows = v.shape[0] - HALO
    v = v.astype(BF).astype(F32)
    return jnp.concatenate([v[rows:], v[:rows]], axis=0)


def same_columns(table):
    return [table[:, SAME + k : SAME + k + 1] for k in range(CONV - 1)]


def pack_kernel(weight_ref, first_ref, cols, heads):
    state2 = 2 * STATE
    rows = weight_ref.shape[0]
    steps = weight_ref[:, INNER + XBC :].astype(F32)
    steps = jnp.concatenate([steps, jnp.zeros((rows, 128 - steps.shape[1]), F32)], axis=1)
    lane = lax.broadcasted_iota(jnp.int32, (rows, 128), 1)
    for r in range(first_ref.shape[0]):
        at, early = r * cols, cols - WIDE
        tail = INNER + at + early
        first_ref[r, :, :WIDE] = weight_ref[:, tail : tail + WIDE]
        first_ref[r, :, WIDE : WIDE + state2] = weight_ref[:, 2 * INNER : INNER + XBC]
        mine = pltpu.roll(steps, (128 - r * heads) % 128, 1)
        first_ref[r, :, WIDE + state2 : LAST] = jnp.where(lane < heads, mine, 0.0).astype(BF)
        if early:
            first_ref[r, :, LAST : LAST + early] = weight_ref[:, INNER + at : INNER + at + early]
        first_ref[r, :, LAST + early :] = weight_ref[:, at : at + cols]


def unpack_kernel(last_ref, early_ref, weight_ref, out_ref, gain_ref, cols, heads):
    state2 = 2 * STATE
    shared, steps = None, None
    lane = lax.broadcasted_iota(jnp.int32, (out_ref.shape[0], 128), 1)
    for r in range(last_ref.shape[0]):
        at, early = r * cols, cols - WIDE
        tail = INNER + at + early
        out_ref[:, at : at + cols] = early_ref[r, :, :cols].astype(F32)
        out_ref[:, tail : tail + WIDE] = last_ref[r, :, :WIDE].astype(F32)
        if early:
            out_ref[:, INNER + at : tail] = early_ref[r, :, cols:].astype(F32)
        both = last_ref[r, :, WIDE : WIDE + state2].astype(F32)
        shared = both if shared is None else shared + both
        step = jnp.where(lane < heads, last_ref[r, :, WIDE + state2 :].astype(F32), 0.0)
        step = pltpu.roll(step, r * heads, 1) if r else step
        steps = step if steps is None else steps + step
    out_ref[:, 2 * INNER : INNER + XBC] = shared
    out_ref[:, INNER + XBC :] = steps[:, : out_ref.shape[1] - INNER - XBC]
    products = out_ref[...] * weight_ref[...].astype(F32)
    gain_ref[...] = jnp.broadcast_to(jnp.sum(products, axis=1, keepdims=True), gain_ref.shape)


def place_kernel(at_ref, *refs, moves, n_in):
    for source, row, lane, target, to, more, to_lane, count, wide in moves:
        if more is not None:
            to = pl.multiple_of(to + at_ref[more] * count, 16)
        piece = refs[source][row : row + count, lane : lane + wide]
        refs[n_in + target][pl.ds(to, count), to_lane : to_lane + wide] = piece


def norm_kernel(*refs):
    gain_ref, out_ref = refs[-2], refs[-1]
    for r in range(len(refs) - 2):
        v = refs[r][...].astype(F32)
        scale = lax.rsqrt(jnp.mean(v * v, axis=-1, keepdims=True) + EPSILON)
        out_ref[r] = (v * scale * gain_ref[0:1, :]).astype(BF)


def norm_back_kernel(tokens_ref, cot_ref, *refs):
    gain_ref, out_ref = refs[-2], refs[-1]
    total = refs[0][...]
    for ref in refs[1:-2]:
        total = total + ref[...].astype(F32)
    inner = total * gain_ref[0:1, :]
    v = tokens_ref[...].astype(F32)
    r = lax.rsqrt(jnp.mean(v * v, axis=-1, keepdims=True) + EPSILON)
    pull = r * r * jnp.mean(inner * v, axis=-1, keepdims=True)
    out_ref[...] = cot_ref[...].astype(F32) + r * (inner - v * pull)


def table_kernel(dt_ref, seg_ref, par_ref, ct_ref, rt_ref, heads):
    rows = dt_ref.shape[1]
    chunks = rows // GROUP
    lane = lax.broadcasted_iota(jnp.int32, (rows, 128), 1)
    v = dt_ref[0] + par_ref[0:1, :]
    step = jnp.where(lane < heads, jnp.maximum(v, 0.0) + jnp.log1p(jnp.exp(-jnp.abs(v))), 0.0)
    decay = -par_ref[1:2, :] * step
    aux = jnp.concatenate([seg_ref[0], jnp.zeros((120, rows), F32)], axis=0).T
    seg, entering = aux[:, 3:4], aux[:, 4:5]
    cums, carries, ends = [], [], []
    for c in range(chunks):
        cum = decay[rows_of(c)]
        step_rows = 1
        while step_rows < GROUP:
            cum = cum + jnp.concatenate(
                [jnp.zeros((step_rows, 128), F32), cum[: GROUP - step_rows]], axis=0
            )
            step_rows *= 2
        here = seg[rows_of(c)]
        held = entering[rows_of(0)] > 0.5 if c == 0 else here == seg[end_of(c - 1)]
        cums.append(cum)
        carries.append(jnp.where(held, jnp.exp(cum), 0.0))
        ends.append(jnp.where(here == seg[end_of(c)], jnp.exp(cum[GROUP - 1 :] - cum), 0.0))
    kept = lane < heads
    cum = jnp.concatenate(cums, axis=0)
    carry = jnp.where(kept, jnp.concatenate(carries, axis=0), 0.0)
    endn = jnp.where(kept, jnp.concatenate(ends, axis=0), 0.0)
    whole = cum + pltpu.roll(step, DT, 1) + pltpu.roll(carry, CARRY, 1) + pltpu.roll(endn, ENDN, 1)
    aux = pltpu.roll(jnp.where(lane < 4, aux, 0.0), SAME, 1)
    for t in range(ct_ref.shape[1]):
        mine = whole if t == 0 else pltpu.roll(whole, 128 - 2 * PAIRS * t, 1)
        ct_ref[0, t] = jnp.where((lane >= SAME) & (lane < SAME + 4), aux, mine)
    rt_ref[0, :SEG_ROW] = cum.T[:SEG_ROW]
    rt_ref[0, SEG_ROW:] = jnp.broadcast_to(seg_ref[0, 3:4, :], (8, rows))


def conv_kernel(xm_ref, bm_ref, cm_ref, tx_ref, tb_ref, ct_ref, x_ref, bc_ref, own_ref):
    table = ct_ref[0, 0]
    chunks = table.shape[0] // GROUP
    same = same_columns(table)

    @pl.when(pl.program_id(1) == 0)
    def _():
        for i, main in enumerate((bm_ref, cm_ref)):
            pre = convolved(extended(main[0]), tb_ref[:, lanes_of(i)], same)
            bc_ref[0, :, lanes_of(i)] = (pre * jax.nn.sigmoid(pre)).astype(BF)

    weighted = []
    for j in range(PAIRS):
        at = lanes_of(j)
        pre = convolved(extended(xm_ref[0, :, at]), tx_ref[:, at], same)
        x = pre * jax.nn.sigmoid(pre)
        x_ref[0, :, at] = x
        left = to_block_end(spread(table, ENDN, j), spread(table, CARRY, j), chunks)
        weighted.append((left * spread(table, DT, j) * x).astype(BF))
    own_ref[0] = tn(bc_ref[0, :, :STATE], jnp.concatenate(weighted, axis=1))


def causal(table, segrow, chunk, transposed):
    seg_c = table[rows_of(chunk), SEG : SEG + 1]
    seg_r = segrow[:, rows_of(chunk)]
    down = lax.broadcasted_iota(jnp.int32, (GROUP, GROUP), 0)
    right = lax.broadcasted_iota(jnp.int32, (GROUP, GROUP), 1)
    order = (down <= right) if transposed else (down >= right)
    return jnp.where((seg_c == seg_r) & order, 0.0, NEVER)


def halves_of(v, half):
    return [jnp.where(half, v, 0.0).astype(BF), jnp.where(half, 0.0, v).astype(BF)]


def mix_kernel(x_ref, bc_ref, ct_ref, rt_ref, skip_ref, y_ref, score, mask):
    table = ct_ref[0, 0]
    chunks = x_ref.shape[1] // GROUP
    base = pl.program_id(1) * (2 * PAIRS)

    @pl.when(pl.program_id(1) == 0)
    def _():
        for c in range(chunks):
            score[c] = nt(bc_ref[0, rows_of(c), STATE:], bc_ref[0, rows_of(c), :STATE])
            mask[c] = causal(table, rt_ref[0, SEG_ROW : SEG_ROW + 1, :], c, False)

    for j in range(PAIRS):
        at = lanes_of(j)
        x = x_ref[0, :, at]
        xd = x * spread(table, DT, j)
        parts = halves_of(xd, low_half(xd.shape[0]))
        carry = spread(table, CARRY, j)
        ending = (spread(table, ENDN, j) * xd).astype(BF)
        cum_rows = [rt_ref[0, pl.ds(base + 2 * j + e, 1), :] for e in range(2)]
        state = None
        for c in range(chunks):
            rows = rows_of(c)
            y = skip_ref[0:1, at] * x[rows]
            for e in range(2):
                h = 2 * j + e
                row = cum_rows[e][:, rows]
                mixing = score[c] * jnp.exp(table[rows, CUM + h : CUM + h + 1] - row + mask[c])
                y = y + nn(mixing.astype(BF), parts[e][rows])
            if c:
                y = y + carry[rows] * nn(bc_ref[0, rows, STATE:], state.astype(BF))
            y_ref[0, rows, at] = y
            if c + 1 < chunks:
                added = tn(bc_ref[0, rows, :STATE], ending[rows])
                state = added if c == 0 else carry[end_of(c)] * state + added


def gate_kernel(yl_ref, bc_ref, inc_ref, z_ref, dn_ref, gain_ref, ct_ref, y_ref, sums_ref, held):
    table = ct_ref[0, 0]
    chunks = table.shape[0] // GROUP
    from_state = nn(bc_ref[0, :, STATE:], inc_ref[0].astype(BF))
    squares, pulled = None, None
    for j in range(PAIRS):
        at = lanes_of(j)
        y = yl_ref[0, :, at] + from_start(spread(table, CARRY, j), chunks) * from_state[:, at]
        y_ref[0, :, at] = y
        z = z_ref[0, :, at]
        gated = y * (z * jax.nn.sigmoid(z))
        square, pull = gated * gated, dn_ref[0, :, at] * gain_ref[0:1, at] * gated
        squares = square if j == 0 else squares + square
        pulled = pull if j == 0 else pulled + pull
    lane = lax.broadcasted_iota(jnp.int32, squares.shape, 1)
    squares = jnp.sum(squares, axis=1, keepdims=True)
    pulled = jnp.sum(pulled, axis=1, keepdims=True)
    both = jnp.where(lane == 0, squares, jnp.where(lane == 1, pulled, 0.0))
    first = pl.program_id(1) == 0

    @pl.when(first)
    def _():
        held[...] = both

    @pl.when(jnp.logical_not(first))
    def _():
        held[...] += both

    @pl.when(pl.program_id(1) == pl.num_programs(1) - 1)
    def _():
        sums_ref[0] = held[...].T[:8]


def gate_back_kernel(
    y_ref, z_ref, dn_ref, gain_ref, sums_ref, bc_ref, ct_ref, out_ref, dy_ref, dz_ref, pull_ref, gg_ref
):
    table = ct_ref[0, 0]
    chunks = table.shape[0] // GROUP
    sums = jnp.concatenate([sums_ref[0], jnp.zeros((120, table.shape[0]), F32)], axis=0).T
    r = lax.rsqrt(sums[:, 0:1] * (1.0 / INNER) + EPSILON)
    along_unit = r * (1.0 / INNER) * sums[:, 1:2]
    pulled = []
    for j in range(PAIRS):
        at = lanes_of(j)
        gain = gain_ref[0:1, at]
        y, z, dn = y_ref[0, :, at], z_ref[0, :, at], dn_ref[0, :, at]
        sig = jax.nn.sigmoid(z)
        silu = z * sig
        unit = y * silu * r
        out_ref[0, :, at] = (unit * gain).astype(BF)
        dg = r * (dn * gain - unit * along_unit)
        dy = dg * silu
        dy_ref[0, :, at] = dy
        dz_ref[0, : y.shape[0], at] = (dg * y * (sig * (1.0 + z * (1.0 - sig)))).astype(BF)
        dz_ref[0, y.shape[0] :, at] = jnp.zeros((HALO, 128), BF)
        pulled.append((from_start(spread(table, CARRY, j), chunks) * dy).astype(BF))
        grad = jnp.sum(dn * unit, axis=0, keepdims=True)
        gg_ref[0, :, at] = jnp.broadcast_to(grad, (8, 128))
    pull_ref[0] = tn(bc_ref[0, :, STATE:], jnp.concatenate(pulled, axis=1))


def conv_back(d_conv, ext, taps, same):
    rows, width = d_conv.shape
    pre = convolved(ext, taps, same)
    sig = jax.nn.sigmoid(pre)
    d_pre = d_conv * (sig * (1.0 + pre * (1.0 - sig)))
    d_ext = jnp.concatenate(
        [jnp.zeros((HALO, width), F32), taps[CONV - 1 : CONV] * d_pre], axis=0
    )
    grads = [None] * 8
    grads[CONV - 1] = jnp.sum(d_pre * ext[HALO:], axis=0, keepdims=True)
    grads[CONV] = jnp.sum(d_pre, axis=0, keepdims=True)
    for k in range(1, CONV):
        kept = same[k - 1] * d_pre
        grads[CONV - 1 - k] = jnp.sum(kept * ext[HALO - k : HALO - k + rows], axis=0, keepdims=True)
        d_ext = d_ext + taps[CONV - 1 - k : CONV - k] * jnp.concatenate(
            [jnp.zeros((HALO - k, width), F32), kept, jnp.zeros((k, width), F32)], axis=0
        )
    grads = [g if g is not None else jnp.zeros((1, width), F32) for g in grads]
    d_rows = jnp.concatenate([d_ext[HALO:], d_ext[:HALO]], axis=0).astype(BF)
    return d_rows, jnp.concatenate(grads, axis=0)


def mix_back_kernel(*refs, base, first, last):
    x_ref, bc_ref, dy_ref, inc_ref, adj_ref, ct_ref, rt_ref, skip_ref, xm_ref, tx_ref = refs[:10]
    at_ref = 10
    if not first:
        before_ref = refs[at_ref]
        at_ref += 1
    if last:
        bm_ref, cm_ref, dt_ref, tb_ref, par_ref = refs[at_ref : at_ref + 5]
    if last:
        d_ref, gx_ref, gs_ref, gb_ref, gh_ref = refs[-6:-1]
    else:
        d_ref, gx_ref, gs_ref, part_ref = refs[-5:-1]
    d_x = refs[-1]

    table = ct_ref[0, 0]
    chunks = x_ref.shape[1] // GROUP
    down = lax.broadcasted_iota(jnp.int32, (GROUP, GROUP), 0)
    right = lax.broadcasted_iota(jnp.int32, (GROUP, GROUP), 1)
    before = (right < down).astype(BF)
    upto = (right >= down).astype(BF)
    same = same_columns(table)
    lane = lax.broadcasted_iota(jnp.int32, (GROUP, 128), 1)
    half = low_half(GROUP)

    def lane_wise(kind, c):
        return jnp.concatenate([spread(table[rows_of(c)], kind, j) for j in range(PAIRS)], axis=1)

    carries = [lane_wise(CARRY, c) for c in range(chunks)]
    pulled = [carries[c] * dy_ref[0, rows_of(c), :] for c in range(chunks)]
    xds = [x_ref[0, rows_of(c), :] * lane_wise(DT, c) for c in range(chunks)]
    endns = [lane_wise(ENDN, c) for c in range(chunks)]
    endings = [endns[c] * xds[c] for c in range(chunks)]
    states, adjoints = [inc_ref[0]], [adj_ref[0]]
    for c in range(chunks - 1):
        added = tn(bc_ref[0, rows_of(c), :STATE], endings[c].astype(BF))
        states.append(carries[c][GROUP - 1 :] * states[-1] + added)
    for c in range(chunks - 1, 0, -1):
        added = tn(bc_ref[0, rows_of(c), STATE:], pulled[c].astype(BF))
        adjoints.insert(0, carries[c][GROUP - 1 :] * adjoints[0] + added)

    d_keys, d_reads, all_logs, all_steps = [], [], [], []
    for c in range(chunks):
        rows = rows_of(c)
        keys, reads = bc_ref[0, rows, :STATE], bc_ref[0, rows, STATE:]
        state_b, adj_b = states[c].astype(BF), adjoints[c].astype(BF)
        from_state = pulled[c] * nn(reads, state_b)
        to_end = nn(keys, adj_b)
        across = nn(upto, from_state.astype(BF)) + nn(before, (endings[c] * to_end).astype(BF))
        across = across + carries[c][GROUP - 1 :] * jnp.sum(
            states[c] * adjoints[c], axis=0, keepdims=True
        )
        d_k, d_r = nt(endings[c].astype(BF), adj_b), nt(pulled[c].astype(BF), state_b)
        score = nt(keys, reads)
        mask = causal(table, rt_ref[0, SEG_ROW : SEG_ROW + 1, :], c, True)
        d_scores = None
        logs, steps = jnp.zeros((GROUP, 128), F32), jnp.zeros((GROUP, 128), F32)
        for j in range(PAIRS):
            at = lanes_of(j)
            dy = dy_ref[0, rows, at]
            dyb = dy.astype(BF)
            parts = halves_of(xds[c][:, at], half)
            d_xd = []
            crossings = []
            for e in range(2):
                h = 2 * j + e
                row = rt_ref[0, base + h : base + h + 1, rows]
                decay = jnp.exp(row - table[rows, CUM + h : CUM + h + 1] + mask)
                weighted = decay * nt(parts[e], dyb)
                d_scores = weighted if d_scores is None else d_scores + weighted
                d_xd.append(nn((score * decay).astype(BF), dyb))
                crossing = nn(before, (score * weighted).astype(BF))
                crossings.append(
                    jnp.sum(jnp.where(right >= down, crossing, 0.0), axis=1, keepdims=True)
                )
            u = jnp.where(half, d_xd[0], d_xd[1]) + endns[c][:, at] * to_end[:, at]
            x = x_ref[0, rows, at]
            d_x[rows, at] = spread(table[rows], DT, j) * u + skip_ref[0:1, at] * dy
            d_step = x * u
            for e in range(2):
                keep = half if e == 0 else jnp.logical_not(half)
                log_e = crossings[e] + jnp.sum(
                    jnp.where(keep, across[:, at], 0.0), axis=1, keepdims=True
                )
                step_e = jnp.sum(jnp.where(keep, d_step, 0.0), axis=1, keepdims=True)
                place = lane == base + 2 * j + e
                logs = jnp.where(place, log_e, logs)
                steps = jnp.where(place, step_e, steps)
        all_logs.append(logs)
        all_steps.append(steps)
        ds = d_scores.astype(BF)
        d_keys.append(d_k + nn(ds, reads))
        d_reads.append(d_r + tn(ds, keys))

    for j in range(PAIRS):
        at = lanes_of(j)
        grad = jnp.sum(dy_ref[0, :, at] * x_ref[0, :, at], axis=0, keepdims=True)
        gs_ref[0, :, at] = jnp.broadcast_to(grad, (8, 128))
        d_rows, grads = conv_back(d_x[:, at], extended(xm_ref[0, :, at]), tx_ref[:, at], same)
        d_ref[0, :, at], gx_ref[0, :, at] = d_rows, grads

    state2 = 2 * STATE
    for i, d_rows in enumerate((d_keys, d_reads)):
        at = lanes_of(i)
        whole = jnp.concatenate(d_rows, axis=0)
        if not first:
            whole = whole + before_ref[0, :, at]
        if last:
            main_ref = (bm_ref, cm_ref)[i]
            d_rows, grads = conv_back(whole, extended(main_ref[0]), tb_ref[:, at], same)
            d_ref[0, :, lanes_of(PAIRS + i)], gb_ref[0, :, at] = d_rows, grads
        else:
            part_ref[0, :, at] = whole
    logs, steps = jnp.concatenate(all_logs, axis=0), jnp.concatenate(all_steps, axis=0)
    if not first:
        logs = logs + before_ref[0, :, state2 : state2 + 128]
        steps = steps + before_ref[0, :, state2 + 128 :]
    if last:
        rows = logs.shape[0]
        v = dt_ref[0, :rows] + par_ref[0:1, :]
        step_dt = jnp.maximum(v, 0.0) + jnp.log1p(jnp.exp(-jnp.abs(v)))
        d_dt = (steps - par_ref[1:2, :] * logs) * jax.nn.sigmoid(v)
        d_ref[0, :rows, lanes_of(PAIRS + 2)] = d_dt.astype(BF)
        d_ref[0, rows:, lanes_of(PAIRS + 2)] = jnp.zeros((HALO, 128), BF)
        by_bias = jnp.sum(d_dt, axis=0, keepdims=True)
        by_log = -jnp.sum(par_ref[1:2, :] * step_dt * logs, axis=0, keepdims=True)
        gh_ref[0] = jnp.concatenate([by_log, by_bias, jnp.zeros((6, 128), F32)], axis=0)
    else:
        part_ref[0, :, state2 : state2 + 128] = logs
        part_ref[0, :, state2 + 128 :] = steps


def split_kernel(at_ref, v_ref, out_ref):
    out_ref[0] = v_ref[:, 0].astype(BF)


def split_both_kernel(at_ref, v_ref, w_ref, out_ref):
    groups, rows, cols = v_ref.shape[0], v_ref.shape[2], v_ref.shape[3]
    many = w_ref.shape[2]
    for g in range(groups):
        out_ref[0, g * rows : (g + 1) * rows, :cols] = v_ref[g, 0].astype(BF)
    for half in range(2):
        here = w_ref[0, 0, :, half * cols : (half + 1) * cols].astype(BF)
        out_ref[0, half * many : (half + 1) * many, cols:] = here


def shape(*dims, dtype=F32):
    return jax.ShapeDtypeStruct(dims, dtype)


def params(n=2, limit=48):
    return pltpu.CompilerParams(
        dimension_semantics=("arbitrary",) * n, vmem_limit_bytes=limit * 2**20
    )


def cost(flops, size):
    return pl.CostEstimate(flops=int(flops), bytes_accessed=int(size), transcendentals=0)


def on_device(
    tokens, segment_ids, in_proj, conv_weight, conv_bias, out_proj, norm_gain, gate_gain,
    a_log, dt_bias, skip_d, cotangent,
):
    n_x = lax.axis_size("x")
    na, nb = lax.axis_size("a"), lax.axis_size("b")
    groups, positions = 2 * n_x, na * nb
    me, place = group_of(0, 0), position_of(0, 0)
    index = me * positions + place
    rows, width = tokens.shape
    long = rows + HALO
    heads = HEADS // groups
    cols = heads * HEADDIM
    n_steps = heads // (2 * PAIRS)
    state2 = 2 * STATE
    early = cols - WIDE
    first_cols, all_cols = LAST + early, LAST + cols + early
    in_rows, out_rows = in_proj.shape[0], out_proj.shape[0]
    aligned = in_rows % 16 == 0 and width == 2 * cols and 2 * out_rows == groups * in_rows
    anywhere = pl.BlockSpec(memory_space=pl.ANY)

    small = jnp.concatenate([norm_gain, gate_gain, conv_bias, conv_weight.reshape(-1)])
    n_norm, n_gate, n_conv = norm_gain.shape[0], gate_gain.shape[0], conv_bias.shape[0]
    small = jnp.pad(small, (0, -small.shape[0] % 128))
    every = jnp.zeros((groups * positions, small.shape[0]), BF)
    every = lax.dynamic_update_slice_in_dim(every, small[None], index, 0)

    packed = pl.pallas_call(
        lambda *refs: pack_kernel(*refs, cols=cols, heads=heads),
        grid=(1,),
        in_specs=[pl.BlockSpec(in_proj.shape, lambda i: (0, 0))],
        out_specs=pl.BlockSpec((groups, in_rows, all_cols), lambda i: (0, 0, 0)),
        out_shape=shape(groups, in_rows, all_cols, dtype=BF),
        compiler_params=params(1),
        name="pack_weights",
    )(in_proj)
    held = exchange(packed, ("x", "core"))
    every = sum_over(every, ("a", "b", "x", "core"), [packed, packed, packed, held])
    block = held[:, :, :first_cols].reshape(-1, first_cols)
    first_over_a = [block] + [shift(block, "a", sa) for sa in range(1, na)]
    first_blocks = [v for here in first_over_a for v in gather_over_b(here)]

    ids_row = jnp.pad(segment_ids.astype(BF)[None], ((0, 15), (0, width - rows)))
    before = along(jnp.concatenate([tokens[rows - HALO :], ids_row], axis=0), 1)
    token_rows = jnp.concatenate([tokens, before[:HALO], ids_row[:8], before[HALO : HALO + 8]], axis=0)
    token_rows = gather_over_x(after(token_rows, every, held))
    slots = gather_over_cores(token_rows, *first_blocks)

    every = every.astype(F32)
    cuts = [n_norm, n_norm + n_gate, n_norm + n_gate + n_conv]
    gain_in = every[:, : cuts[0]].reshape(1, -1)
    gain_out = every[:, cuts[0] : cuts[1]].reshape(-1)
    bias_all = every[:, cuts[1] : cuts[2]].reshape(-1)
    taps_all = every[:, cuts[2] : cuts[2] + CONV * n_conv].reshape(-1, CONV, n_conv)
    taps_all = taps_all.transpose(1, 0, 2).reshape(CONV, XBC)
    conv_all = jnp.concatenate([taps_all, bias_all[None], jnp.zeros((3, XBC), F32)], axis=0)
    taps_x = lax.dynamic_slice_in_dim(conv_all, me * cols, cols, 1)
    taps_b = conv_all[:, INNER:]
    gain_g = jnp.broadcast_to(lax.dynamic_slice_in_dim(gain_out, me * cols, cols, 0), (8, cols))
    a_g = lax.dynamic_slice_in_dim(a_log, me * heads, heads, 0)
    bias_g = lax.dynamic_slice_in_dim(dt_bias, me * heads, heads, 0)
    skip_g = lax.dynamic_slice_in_dim(skip_d, me * heads, heads, 0)
    head_rows = jnp.pad(jnp.stack([bias_g, jnp.exp(a_g)]), ((0, 6), (0, 128 - heads)))
    skip_l = jnp.broadcast_to(jnp.repeat(skip_g, HEADDIM), (8, cols))

    tall = long // 3
    normed = pl.pallas_call(
        norm_kernel,
        grid=(long // tall,),
        in_specs=[pl.BlockSpec((tall, width), lambda i: (i, 0))] * groups
        + [pl.BlockSpec((8, width), lambda i: (0, 0))],
        out_specs=pl.BlockSpec((groups, tall, width), lambda i: (0, i, 0)),
        out_shape=shape(groups, long, width, dtype=BF),
        compiler_params=params(1),
        cost_estimate=cost(10 * groups * rows * width, 4 * groups * rows * width),
        name="input_norm",
    )(*slots, jnp.broadcast_to(gain_in, (8, width)))
    ids = jnp.concatenate([s[long : long + 1, :rows] for s in slots], axis=0)
    halo_ids = jnp.concatenate([s[long + 8 : long + 9, rows - HALO : rows] for s in slots], axis=0)
    ids = jnp.concatenate([jnp.where(place == 0, jnp.asarray(-1, BF), halo_ids), ids], axis=1).astype(F32)
    seg = ids[:, HALO:]
    seg_rows = jnp.stack(
        [(ids[:, HALO - k : HALO - k + rows] == seg).astype(F32) for k in range(1, CONV)]
        + [seg, (seg == ids[:, HALO - 1 : HALO]).astype(F32)]
        + [jnp.zeros_like(seg)] * 3,
        axis=1,
    )

    b_behind = jnp.stack([lax.rem(lax.axis_index("b") - sb + nb, nb) for sb in range(nb)])
    behind = jnp.stack([position_of(-sa, -sb) for sa in range(na) for sb in range(nb)])

    def place_rows(blocks, moves, outs, at, *others):
        return pl.pallas_call(
            lambda *refs: place_kernel(*refs, moves=moves, n_in=len(blocks) + len(others)),
            grid_spec=pltpu.PrefetchScalarGridSpec(
                num_scalar_prefetch=1,
                grid=(1,),
                in_specs=[pl.BlockSpec(v.shape, lambda i, s: (0, 0)) for v in blocks]
                + [anywhere] * len(others),
                out_specs=[pl.BlockSpec(v.shape, lambda i, s: (0, 0)) for v in outs],
            ),
            out_shape=outs,
            compiler_params=params(1, 56),
            name="place_weights",
        )(at, *blocks, *others)

    def in_moves(source, target, own_lane, lane, wide, held_by, many):
        return [
            (
                source + sb, a * many + i * in_rows, own_lane,
                target, ((held_by + i) * positions + a * nb) * in_rows, sb, lane, in_rows, wide,
            )
            for sb in range(nb) for a in range(na) for i in range(min(groups, many // in_rows))
        ]

    def whole_rows(blocks, many, parts):
        out = jnp.zeros((parts, na, nb, many) + blocks[0].shape[-1:], BF)
        for sb in range(nb):
            v = blocks[sb].reshape(na, parts, many, -1).transpose(1, 0, 2, 3)[:, :, None]
            out = lax.dynamic_update_slice_in_dim(out, v, b_behind[sb], 2)
        return out.reshape(parts * positions * many, -1)

    def flat2(v):
        return v.reshape(-1, v.shape[-1])

    if aligned:
        moves = [
            (k, g * in_rows, 0, 0, g * positions * in_rows, k, 0, in_rows, first_cols)
            for k in range(positions) for g in range(groups)
        ]
        (w_first,) = place_rows(first_blocks, moves, [shape(width, first_cols, dtype=BF)], behind, normed)
    else:
        w_first = jnp.zeros((groups, positions, in_rows, first_cols), BF)
        for k in range(positions):
            v = first_blocks[k].reshape(groups, 1, in_rows, first_cols)
            w_first = lax.dynamic_update_slice_in_dim(w_first, v, behind[k], 1)
        w_first = w_first.reshape(width, first_cols)

    cot_rows = gather_over_x(after(cotangent, w_first))
    gate_block = held[:, :, first_cols:].reshape(-1, cols)
    if aligned:
        out_block = jnp.concatenate([out_proj[:, :cols], out_proj[:, cols:]], axis=0)
        gate_over_a = gather_over_a(after(gate_block, w_first))
    else:
        gate_over_a, out_over_a = gather_over_a(gate_block), gather_over_a(out_proj)

    normed_rows = normed.reshape(groups * long, width)
    proj = jnp.dot(normed_rows, w_first, preferred_element_type=F32).reshape(groups, long, first_cols)
    keys_at = WIDE // 128
    if aligned:
        gate_blocks = gather_over_b(after(gate_over_a, proj))

    def step_tile(t):
        return jnp.where(t == n_steps - 1, 0, LAST // WIDE + t)

    def tile(count):
        return pl.BlockSpec((1, count, WIDE), lambda q, t: (q, 0, t))

    def narrow(at):
        return pl.BlockSpec((1, long, 128), lambda q, t: (q, 0, at))

    def per_seq(count, wide):
        return pl.BlockSpec((1, count, wide), lambda q, t: (q, 0, 0))

    def lanes(count):
        return pl.BlockSpec((count, WIDE), lambda q, t: (0, t))

    by_step = pl.BlockSpec((1, 1, rows, 128), lambda q, t: (q, t, 0, 0))
    all_taps = pl.BlockSpec((8, state2), lambda q, t: (0, 0))

    col_table, row_table = pl.pallas_call(
        lambda *refs: table_kernel(*refs, heads=heads),
        grid=(groups,),
        in_specs=[
            pl.BlockSpec((1, rows, 128), lambda q: (q, 0, keys_at + 2)),
            pl.BlockSpec((1, 8, rows), lambda q: (q, 0, 0)),
            pl.BlockSpec((8, 128), lambda q: (0, 0)),
        ],
        out_specs=[
            pl.BlockSpec((1, n_steps, rows, 128), lambda q: (q, 0, 0, 0)),
            pl.BlockSpec((1, SEG_ROW + 8, rows), lambda q: (q, 0, 0)),
        ],
        out_shape=[shape(groups, n_steps, rows, 128), shape(groups, SEG_ROW + 8, rows)],
        compiler_params=params(1),
        cost_estimate=cost(100 * groups * rows * 128, 16 * groups * rows * 128),
        name="token_table",
    )(proj, seg_rows, head_rows)

    if aligned:
        out_block = after(out_block, w_first)
        out_over_a = jnp.stack([out_block] + [shift(out_block, "a", sa) for sa in range(1, na)])
    grid = (groups, n_steps)
    big = groups * rows * cols
    values_x, bc, own_state = pl.pallas_call(
        lambda *refs: conv_kernel(*refs[:6], *refs[-3:]),
        grid=grid,
        in_specs=[
            pl.BlockSpec((1, long, WIDE), lambda q, t: (q, 0, step_tile(t))),
            narrow(keys_at), narrow(keys_at + 1), lanes(8), all_taps, by_step,
        ],
        out_specs=[tile(rows), per_seq(rows, state2), tile(STATE)],
        out_shape=[
            shape(groups, rows, cols), shape(groups, rows, state2, dtype=BF), shape(groups, STATE, cols),
        ],
        compiler_params=params(),
        cost_estimate=cost(20 * big * STATE, 8 * big),
        name="conv_and_state",
    )(proj, proj, proj, taps_x, taps_b, col_table)

    if aligned:
        out_blocks = gather_over_b(after(out_over_a, values_x))
    else:
        gate_blocks, out_blocks = gather_over_b(gate_over_a), gather_over_b(out_over_a)

    hops = -(-(LONGEST - 1) // rows)
    kept = col_table[:, :, GROUP - 1, CARRY : CARRY + 2 * PAIRS]
    for c in range(1, rows // GROUP):
        kept = kept * col_table[:, :, (c + 1) * GROUP - 1, CARRY : CARRY + 2 * PAIRS]
    device_decay = jnp.repeat(kept.reshape(groups, heads), HEADDIM, axis=-1)[:, None]

    def entering(own, sign):
        sent = jnp.concatenate(
            [own, jnp.broadcast_to(device_decay, (groups, 16, cols))], axis=1
        ).astype(BF)
        total_in, weight = None, None
        for hop in range(1, hops + 1):
            got = along(sent, sign * hop).astype(F32)
            state, decay = got[:, :STATE], got[:, STATE : STATE + 1]
            total_in = state if hop == 1 else total_in + weight * state
            weight = decay if hop == 1 else weight * decay
        return total_in

    incoming = entering(own_state, 1)

    mixed_local = pl.pallas_call(
        mix_kernel,
        grid=grid,
        in_specs=[tile(rows), per_seq(rows, state2), by_step, per_seq(SEG_ROW + 8, rows), lanes(8)],
        out_specs=tile(rows),
        out_shape=shape(groups, rows, cols),
        scratch_shapes=[pltpu.VMEM((rows // GROUP, GROUP, GROUP), F32)] * 2,
        compiler_params=params(),
        cost_estimate=cost(80 * big * GROUP, 8 * big),
        name="mix_within_block",
    )(values_x, bc, col_table, row_table, skip_l)

    if aligned:
        many = groups * in_rows
        moves = in_moves(0, 0, 0, LAST, cols, 0, many)
        moves.append((nb, 0, 0, 0, 0, None, 0, width, LAST))
        moves.append((nb, 0, LAST, 0, 0, None, LAST + cols, width, early))
        blocks = [flat2(v) for v in gate_blocks] + [w_first]
        (w_all,) = place_rows(blocks, moves, [shape(width, all_cols, dtype=BF)], b_behind, mixed_local)
        moves = [
            (sb, sa * many + half * out_rows, 0, 0, 0, sa * nb + sb, half * cols, out_rows, cols)
            for sb in range(nb) for sa in range(na) for half in range(2)
        ]
        blocks = [flat2(v) for v in out_blocks]
        (w_out,) = place_rows(blocks, moves, [shape(cols, width, dtype=BF)], behind)
    else:
        w_out = whole_rows(out_blocks, out_rows, 1)
        w_gate = whole_rows(gate_blocks, in_rows, groups)
        w_all = jnp.concatenate([w_first[:, :LAST], w_gate, w_first[:, LAST:]], axis=1)

    cot = jnp.stack(gather_over_cores(cot_rows, mixed_local))
    gate_z = jnp.dot(normed_rows, w_all[:, LAST : LAST + cols], preferred_element_type=F32)
    gate_z = gate_z.reshape(groups, long, cols)
    d_normed = jnp.einsum("qtd,cd->qtc", cot, w_out, preferred_element_type=F32)

    mixed_y, sums = pl.pallas_call(
        gate_kernel,
        grid=grid,
        in_specs=[
            tile(rows), per_seq(rows, state2), tile(STATE), tile(rows), tile(rows), lanes(8), by_step,
        ],
        out_specs=[tile(rows), per_seq(8, rows)],
        out_shape=[shape(groups, rows, cols), shape(groups, 8, rows)],
        scratch_shapes=[pltpu.VMEM((rows, 128), F32)],
        compiler_params=params(),
        cost_estimate=cost(2 * big * STATE, 16 * big),
        name="gate",
    )(mixed_local, bc, incoming, gate_z, d_normed, gain_g, col_table)
    sums = sum_over_group(sums)

    gate_tile = LAST // WIDE
    normed_out, d_y, d_all, pull, gate_sums = pl.pallas_call(
        gate_back_kernel,
        grid=grid,
        in_specs=[
            tile(rows), tile(rows), tile(rows), lanes(8), per_seq(8, rows), per_seq(rows, state2), by_step,
        ],
        out_specs=[
            tile(rows), tile(rows),
            pl.BlockSpec((1, long, WIDE), lambda q, t: (q, 0, gate_tile + t)), tile(STATE), tile(8),
        ],
        out_shape=[
            shape(groups, rows, cols, dtype=BF), shape(groups, rows, cols),
            shape(groups, long, all_cols, dtype=BF), shape(groups, STATE, cols), shape(groups, 8, cols),
        ],
        compiler_params=params(),
        cost_estimate=cost(2 * big * STATE, 20 * big),
        name="gate_back",
    )(mixed_y, gate_z, d_normed, gain_g, sums, bc, col_table)

    later = entering(pull, -1)

    ahead = jnp.stack([a * nb + lax.rem(lax.axis_index("b") + rb, nb) for rb in range(nb) for a in range(na)])

    def split(grad, many):
        shaped = grad.reshape(-1, positions, many, grad.shape[1])
        g, _, r, c = shaped.shape
        out = pl.pallas_call(
            split_kernel,
            grid_spec=pltpu.PrefetchScalarGridSpec(
                num_scalar_prefetch=1,
                grid=(positions,),
                in_specs=[pl.BlockSpec((g, 1, r, c), lambda k, at: (0, at[k], 0, 0))],
                out_specs=pl.BlockSpec((1, g, r, c), lambda k, at: (k, 0, 0, 0)),
            ),
            out_shape=shape(positions, g, r, c, dtype=BF),
            compiler_params=params(1),
            cost_estimate=cost(grad.size, 6 * grad.size),
            name="split_gradient",
        )(ahead, shaped)
        return out.reshape(nb, na, g, r, c)

    def split_both(grad, other):
        many = groups * in_rows
        return pl.pallas_call(
            split_both_kernel,
            grid_spec=pltpu.PrefetchScalarGridSpec(
                num_scalar_prefetch=1,
                grid=(positions,),
                in_specs=[
                    pl.BlockSpec((groups, 1, in_rows, cols), lambda k, at: (0, at[k], 0, 0)),
                    pl.BlockSpec((1, 1, out_rows, width), lambda k, at: (0, at[k], 0, 0)),
                ],
                out_specs=pl.BlockSpec((1, many, width), lambda k, at: (k, 0, 0)),
            ),
            out_shape=shape(positions, many, width, dtype=BF),
            compiler_params=params(1),
            cost_estimate=cost(2 * grad.size, 12 * grad.size),
            name="split_gradients",
        )(
            ahead, grad.reshape(groups, positions, in_rows, cols), other.reshape(1, positions, out_rows, width)
        ).reshape(nb, na, many, width)

    def grad_of(d_values, low, high):
        d_rows = d_values[:, :, low:high].reshape(groups * long, high - low)
        return jnp.dot(normed_rows.T, d_rows, preferred_element_type=F32)

    grad_out = jnp.einsum("qtc,qtd->cd", normed_out, cot, preferred_element_type=F32)
    grad_gate_cols = grad_of(d_all, LAST, LAST + cols)
    if aligned:
        weights_split = [split_both(grad_gate_cols, grad_out)]
    else:
        weights_split = [split(grad_gate_cols, in_rows), split(grad_out, out_rows)]
    by_core = normed_out.reshape(n_x, 2, rows, cols)

    def outward(values):
        return jnp.einsum("qtc,cd->qtd", values, w_out, preferred_element_type=F32)

    out_sent = outward(by_core[:, 1])
    out_kept = outward(by_core[:, 0])

    d_parts, g_x, g_skip = None, [], []
    waits = list(weights_split)
    split_early = []
    for t in range(n_steps):
        first, last = t == 0, t == n_steps - 1

        def block(*dims, at=(0, 0)):
            return pl.BlockSpec((1,) + dims, lambda q, at=at: (q,) + at)

        def flat(*dims, at=(0, 0)):
            return pl.BlockSpec(dims, lambda q, at=at: at)

        tile_at = 0 if last else LAST // WIDE + t
        operands = [
            (values_x, block(rows, WIDE, at=(0, t))), (bc, block(rows, state2)),
            (d_y, block(rows, WIDE, at=(0, t))), (incoming, block(STATE, WIDE, at=(0, t))),
            (later, block(STATE, WIDE, at=(0, t))),
            (col_table, block(1, rows, 128, at=(t, 0, 0))), (row_table, block(SEG_ROW + 8, rows)),
            (skip_l, flat(8, WIDE, at=(0, t))), (proj, block(long, WIDE, at=(0, tile_at))),
            (taps_x, flat(8, WIDE, at=(0, t))),
        ]
        if not first:
            operands.append((d_parts, block(rows, 2 * state2)))
        if last:
            operands += [
                (proj, block(long, 128, at=(0, keys_at + i))) for i in range(3)
            ] + [(taps_b, flat(8, state2)), (head_rows, flat(8, 128))]
        used = len(operands)
        operands += [(d_all, anywhere)] + [(v, anywhere) for v in waits]
        d_tile = 0 if last else (LAST + cols) // WIDE + t
        made = [
            (block(long, LAST if last else WIDE, at=(0, d_tile)), d_all.shape, BF),
            (block(8, WIDE), (groups, 8, WIDE), F32), (block(8, WIDE), (groups, 8, WIDE), F32),
        ]
        if last:
            made += [
                (block(8, state2), (groups, 8, state2), F32), (block(8, 128), (groups, 8, 128), F32),
            ]
        else:
            made += [(block(rows, 2 * state2), (groups, rows, 2 * state2), F32)]

        def body(*refs, t=t, first=first, last=last, used=used, n_out=len(made)):
            mix_back_kernel(
                *refs[:used], *refs[-n_out - 1 :], base=2 * PAIRS * t, first=first, last=last
            )

        outs = pl.pallas_call(
            body,
            grid=(groups,),
            in_specs=[spec for _, spec in operands],
            out_specs=[spec for spec, _, _ in made],
            out_shape=[jax.ShapeDtypeStruct(s, d) for _, s, d in made],
            scratch_shapes=[pltpu.VMEM((rows, WIDE), F32)],
            input_output_aliases={used: 0},
            compiler_params=params(1),
            cost_estimate=cost(100 * big * GROUP, 16 * big),
            name="mix_back",
        )(*[v for v, _ in operands])
        d_all = outs[0]
        g_x.append(outs[1])
        g_skip.append(outs[2])
        if last:
            g_b, g_head = outs[3:]
        else:
            d_parts = outs[3]
            low = LAST + cols + t * WIDE
            split_early.append(split(grad_of(d_all, low, low + WIDE), in_rows))
            if first:
                weight_sums = [sum_over_b(v) for v in weights_split]
                out_own, out_others = sum_over_cores(out_kept, out_sent)
            waits = [split_early[-1]] + weight_sums * first + out_others * first
    if n_steps == 1:
        weight_sums = [sum_over_b(v) for v in weights_split]
        out_own, out_others = sum_over_cores(out_kept, out_sent)

    weight_totals = [sum_over_a(v) for v in weight_sums]
    stream = tokens.astype(F32)
    output = (stream + sum_to_owner(out_own, out_others)).astype(BF)
    early_sums = [sum_over_b(v, d_all) for v in split_early]

    if aligned:
        gate_part = weight_totals[0][:, :cols].reshape(groups, in_rows, cols)
        both = weight_totals[0][:, cols:]
        grad_out_proj = jnp.concatenate([both[:out_rows], both[out_rows:]], axis=1)
    else:
        gate_part, grad_out_proj = weight_totals[0], weight_totals[1][0]

    def to_owners(v):
        return exchange(v.astype(BF), ("x", "core"))

    d_all = after(d_all, output, *weight_totals)
    spill = along(d_all[:, rows:], -1)
    grad_last = grad_of(d_all, 0, LAST)
    split_last = split(grad_last, in_rows)
    last_sum = sum_over_b(split_last)
    early_part = [sum_over_a(after(v, *weight_totals)) for v in early_sums]
    d_sent = after(d_all, split_last, spill, *early_part)
    end = d_sent[:, rows - HALO : rows] + spill
    d_sent = lax.dynamic_update_slice_in_dim(d_sent, end, rows - HALO, 1)
    early_part = to_owners(jnp.concatenate([gate_part] + early_part, axis=2))

    def inward(d_values, core, kind):
        d_by = d_values.reshape(n_x, 2, long, all_cols)[:, core]
        return jnp.einsum("qtc,dc->qtd", d_by, w_all, preferred_element_type=F32).astype(kind)

    in_sent = inward(d_sent, 1, BF)
    in_kept = inward(d_sent, 0, F32)
    in_own, in_both = sum_over_cores(in_kept, after(in_sent, last_sum, early_part))
    in_others = [shift(v, "x", -sx - 1) for sx, v in enumerate(in_both)]

    def by_rows(wide=width):
        return pl.BlockSpec((128, wide), lambda i: (i, 0))

    grad_tokens = pl.pallas_call(
        norm_back_kernel,
        grid=(rows // 128,),
        in_specs=[by_rows()] * (3 + len(in_others)) + [pl.BlockSpec((8, width), lambda i: (0, 0))],
        out_specs=by_rows(),
        out_shape=shape(rows, width),
        compiler_params=params(1),
        name="input_norm_back",
    )(tokens, cotangent, in_own, *in_others, jnp.broadcast_to(gain_in, (8, width)))

    pieces = [to_owners(sum_over_a(after(last_sum, in_kept, *in_both))), early_part]
    grad_in_proj, gain_products = pl.pallas_call(
        lambda *refs: unpack_kernel(*refs, cols=cols, heads=heads),
        grid=(1,),
        in_specs=[pl.BlockSpec(p.shape, lambda i: (0, 0, 0)) for p in pieces]
        + [pl.BlockSpec(in_proj.shape, lambda i: (0, 0))],
        out_specs=[
            pl.BlockSpec(in_proj.shape, lambda i: (0, 0)), pl.BlockSpec((in_rows, 128), lambda i: (0, 0)),
        ],
        out_shape=[shape(*in_proj.shape), shape(in_rows, 128)],
        compiler_params=params(1),
        name="unpack_gradient",
    )(*pieces, in_proj)
    grad_norm = gain_products[:, 0] / norm_gain.astype(F32)

    def placed(v):
        out = jnp.zeros((groups,) + v.shape, F32)
        return lax.dynamic_update_slice_in_dim(out, v[None], me, 0)

    g_x = jnp.sum(jnp.concatenate(g_x, axis=2), axis=0)[: CONV + 1]
    g_b = jnp.sum(g_b, axis=0)[: CONV + 1]
    g_skip = jnp.sum(jnp.concatenate([g[:, 0] for g in g_skip], axis=1), axis=0)
    grad_skip_g = jnp.sum(g_skip.reshape(1, heads, HEADDIM), axis=2)
    g_head = jnp.sum(g_head, axis=0)[:2, :heads]
    pieces = [
        placed(g_x), g_b, placed(jnp.sum(gate_sums[:, 0], axis=0)),
        placed(jnp.concatenate([g_head, grad_skip_g], axis=0)),
    ]
    flat = jnp.concatenate([p.reshape(-1) for p in pieces])
    count = flat.shape[0]
    flat = jnp.pad(flat, (0, -count % 1024)).reshape(-1, 128)
    marks = [grad_last, split_last, in_sent, in_kept, in_own]
    flat = sum_over(flat, ("x", "a", "b", "core"), marks).reshape(-1)
    at, back = 0, []
    for p in pieces:
        back.append(flat[at : at + p.size].reshape(p.shape))
        at += p.size
    conv_x, conv_b, gate_all, head_all = back
    conv_sum = jnp.concatenate([conv_x.transpose(1, 0, 2).reshape(CONV + 1, INNER), conv_b], axis=1)
    conv_own = lax.dynamic_slice_in_dim(conv_sum, index * n_conv, n_conv, 1)
    grad_gate = lax.dynamic_slice_in_dim(gate_all.reshape(-1), index * n_gate, n_gate, 0)
    head_all = head_all.transpose(1, 0, 2).reshape(3, HEADS)
    return (
        output, grad_tokens, grad_in_proj, conv_own[:CONV], conv_own[CONV], grad_out_proj,
        grad_norm, grad_gate, head_all[0], head_all[1], head_all[2],
    )


def solution(mesh):
    n_dp, n_seq = mesh.shape["dp"], mesh.shape["seq"]
    slow = 4 if n_seq % 4 == 0 else 1
    finer = Mesh(
        mesh.devices.reshape(n_dp // 2, 2, slow, n_seq // slow), ("x", "core", "a", "b")
    )
    every = ("x", "core", "a", "b")
    rows, flat, second, copied = P(every, None), P(every), P(None, every), P()
    in_specs = (rows, flat, rows, second, flat, rows, flat, flat, copied, copied, copied, rows)
    out_specs = (rows, rows, rows, second, flat, rows, flat, flat, copied, copied, copied)
    return jax.shard_map(
        on_device, mesh=finer, in_specs=in_specs, out_specs=out_specs, check_vma=False
    )
```

time: 871 us -> 632 us (0.73)
  waiting for transfers between devices: 242 us -> 110 us
  local copies, waits for them, and re-layouts: 143 us -> 66.8 us
  Pallas kernels: 159 us -> 193 us
  other arithmetic: 76.6 us -> 47.1 us
  starting transfers between devices: 132 us -> 103 us
    ppermute x72 -> x27, waiting for transfers between devices: 180 us -> 82.6 us  [shift(): return lax.ppermute(v, axis, [(i, (i + step) % n) for i in range(n)])]
    ppermute x72 -> x27, starting transfers between devices: 101 us -> 37.9 us  [shift(): return lax.ppermute(v, axis, [(i, (i + step) % n) for i in range(n)])]
    pallas_call x3 -> x38, Pallas kernels: 112 us -> 165 us  [the longest x2 84.5 us: on_device(): pl.pallas_call(body, grid=(groups,), in_specs=[spec for _, spec in operan...]
    dynamic_update_slice x56 -> x1, local copies, waits for them, and re-layouts: 50.2 us -> 0.06 us  [on_device(): every = lax.dynamic_update_slice_in_dim(every, small[None], index, 0)]
    ppermute x17 -> x10, waiting for transfers between devices: 55.9 us -> 9.59 us  [sum_over(): moved = lax.ppermute(v, axis, [(i, i ^ step) for i in range(n)])]
    all_to_all x0 -> x7, starting transfers between devices: none -> 32.9 us  [exchange(): return lax.all_to_all(v, axes, 0, 0, tiled=True)]
    convert_element_type x20 -> x8, other arithmetic: 31 us -> 15.6 us  [the longest x3 8.62 us: sum_over_b(): return total.astype(BF)]
    all_to_all x0 -> x7, waiting for transfers between devices: none -> 14.6 us  [exchange(): return lax.all_to_all(v, axes, 0, 0, tiled=True)]
  transfers between devices with their start and end apart: 98 -> 50, of which waited for: 37 -> 16; matrix products, arithmetic and copies ran while one was open for 32% -> 29% of each run, Pallas kernels for 13% -> 25%
where the time goes in v2:
time: 632 us; the launch traced here: 620 us
  Pallas kernels  193 us (31%)
  waiting for transfers between devices  110 us (17%)
  starting transfers between devices  103 us (16%)
  matrix products  97.8 us (15%)
  local copies, waits for them, and re-layouts  66.8 us (11%)
  other arithmetic  47.1 us (7%)
    pallas_call x2, Pallas kernels, on_device(): pl.pallas_call(body, grid=(groups,), in_specs=[spec for _, spec in operan...  84.5 us
    ppermute x27, waiting for transfers between devices, shift(): return lax.ppermute(v, axis, [(i, (i + step) % n) for i in range(n)])  82.6 us
    ppermute x27, starting transfers between devices, shift(): return lax.ppermute(v, axis, [(i, (i + step) % n) for i in range(n)])  37.9 us
    all_to_all x7, starting transfers between devices, exchange(): return lax.all_to_all(v, axes, 0, 0, tiled=True)  32.9 us
    dot_general x3, matrix products, grad_of(): return jnp.dot(normed_rows.T, d_rows, preferred_element_type=F32)  23.4 us
    dot_general x2, matrix products, inward(): jnp.einsum('qtc,dc->qtd', d_by, w_all, preferred_element_type=F32)  21.7 us
    unnamed x138, local copies, waits for them, and re-layouts  20.2 us
    pallas_call x1, Pallas kernels, on_device(): pl.pallas_call(lambda *refs: conv_kernel(*refs[:6], *refs[-3:]), grid=gri...  18.2 us
  transfers between devices with their start and end apart: 50, of which 16 were waited for; matrix products, arithmetic and copies ran while one was open for 29% of the time, Pallas kernels for 25%

profile of v2, /device:TPU:0, one launch (start us, length us, event | category | flops | bytes accessed | tf_op | source)
XLA Modules:
  0.0 620.1 jit_solution(7822448831900781622)
XLA Ops:
  44.6 6.7 %collective-permute-done.9.refs_3_ = bf16[192,1152]{1,0:T(8,128)(2,1)S(1)} collective-permute-done((bf16[192,1152]{1,0:T(8,128)(2,1)S(1)}, bf16[192,1152]{1,0:T(8,128)(2,1)S(1)}, u32[]{:S(2)}, u32[]{:S(2)}) %collective-permute-start.9) | collective-permute-done | bytes 442400 | tf_op jit(solution)/shard_map/ppermute | solution.py:33
  53.6 16.2 %collective-permute-done.11.refs_5_ = bf16[192,1152]{1,0:T(8,128)(2,1)S(1)} collective-permute-done((bf16[192,1152]{1,0:T(8,128)(2,1)S(1)}, bf16[192,1152]{1,0:T(8,128)(2,1)S(1)}, u32[]{:S(2)}, u32[]{:S(2)}) %collective-permute-start.11) | collective-permute-done | bytes 442400 | tf_op jit(solution)/shard_map/ppermute | solution.py:33
  72.0 10.9 %collective-permute-done.12.refs_6_ = bf16[192,1152]{1,0:T(8,128)(2,1)S(1)} collective-permute-done((bf16[192,1152]{1,0:T(8,128)(2,1)S(1)}, bf16[192,1152]{1,0:T(8,128)(2,1)S(1)}, u32[]{:S(2)}, u32[]{:S(2)}) %collective-permute-start.12) | collective-permute-done | bytes 442400 | tf_op jit(solution)/shard_map/ppermute | solution.py:33
  82.9 8.7 %collective-permute-done.14.refs_8_ = bf16[192,1152]{1,0:T(8,128)(2,1)S(1)} collective-permute-done((bf16[192,1152]{1,0:T(8,128)(2,1)S(1)}, bf16[192,1152]{1,0:T(8,128)(2,1)S(1)}, u32[]{:S(2)}, u32[]{:S(2)}) %collective-permute-start.14) | collective-permute-done | bytes 442400 | tf_op jit(solution)/shard_map/ppermute | solution.py:33
  106.5 6.3 %input_norm.1.refs_9_ = bf16[4,528,1536]{2,1,0:T(8,128)(2,1)} custom-call(bf16[544,1536]{1,0:T(8,128)(2,1)S(1)} %copy-done.4, bf16[544,1536]{1,0:T(8,128)(2,1)} %collective-permute-done.6.refs_1_, bf16[544,1536]{1,0:T(8,128)(2,1)S(1)} %copy-done.9, bf16[544,1536]{1,0:T(8,128)(2,1)} %collective-permute-done.15.refs_3_, ...), custom_call_target="tpu_custom_call" | custom-call | flops 31457280 | bytes 12582912 | tf_op jit(solution)/shard_map/input_norm/pallas_call | solution.py:686
  118.1 10.9 %collective-permute-start.24 = (bf16[192,768]{1,0:T(8,128)(2,1)}, bf16[192,768]{1,0:T(8,128)(2,1)}, u32[]{:S(2)}, u32[]{:S(2)}) collective-permute-start(bf16[192,768]{1,0:T(8,128)(2,1)} %in_order.33), channel_id=1, source_target_pairs={{0,6},{2,0},{4,2},{6,4},{1,7},{3,1},{5,3},{7,5},{8,14},{10,8},{12,... | collective-permute-start | bytes 884744 | tf_op jit(solution)/shard_map/ppermute | solution.py:33
  138.2 14.1 %fusion.7.refs_0_.refs_1_.refs_2_.refs_8_.refs_11_.refs_12_.refs_13_ = f32[4,528,1152]{2,1,0:T(8,128)} fusion(bf16[4,528,1536]{2,1,0:T(8,128)(2,1)} %input_norm.1.refs_9_, bf16[1536,1152]{1,0:T(8,128)(2,1)} %place_weights.3.refs_1_.refs_3_), kind=kOutput, calls=%fused_computation.13 | convolution fusion | flops 7474249728 | bytes 19759104 | tf_op jit(solution)/shard_map/dot_general | solution.py:767
  156.7 18.2 %conv_and_state.1 = (f32[4,512,768]{2,1,0:T(8,128)}, bf16[4,512,256]{2,1,0:T(8,128)(2,1)S(1)}, f32[4,128,768]{2,1,0:T(8,128)S(1)}) custom-call(f32[4,528,1152]{2,1,0:T(8,128)} %fusion.7.refs_0_.refs_1_.refs_2_.refs_8_.refs_11_.refs_12_.refs_13_, f32[4,528,1152]{2,1,0:T(8,128)} %fusion.7.refs_0_.refs_1_.refs_2_.refs_8_.refs_11_.refs_12_.refs_13_, ...), custom_call_target="tpu_custom_call" | custom-call | flops 4026531840 | bytes 12582912 | tf_op jit(solution)/shard_map/conv_and_state/pallas_call | solution.py:813
  193.4 16.8 %mix_within_block.1.refs_4_.refs_1_.yl_ref = f32[4,512,768]{2,1,0:T(8,128)} custom-call(f32[4,512,768]{2,1,0:T(8,128)} %get-tuple-element.35.x_ref.refs_1_.refs_0_, bf16[4,512,256]{2,1,0:T(8,128)(2,1)S(1)} %get-tuple-element.36.bc_ref.refs_1_, f32[4,2,512,128]{3,2,1,0:T(8,128)S(1)} %get-tuple-element.34.refs_5_.ct_ref, ...), custom_call_target="tpu_custom_call" | custom-call | flops 32212254720 | bytes 12582912 | tf_op jit(solution)/shard_map/mix_within_block/pallas_call | solution.py:854
  210.3 13.6 %collective-permute-done.20.refs_0_ = bf16[512,1536]{1,0:T(8,128)(2,1)} collective-permute-done((bf16[512,1536]{1,0:T(8,128)(2,1)}, bf16[512,1536]{1,0:T(8,128)(2,1)}, u32[]{:S(2)}, u32[]{:S(2)}) %collective-permute-start.20) | collective-permute-done | bytes 1572896 | tf_op jit(solution)/shard_map/ppermute | solution.py:33
  232.6 19.3 %collective-permute-done.18 = bf16[4,192,768]{2,1,0:T(8,128)(2,1)} collective-permute-done((bf16[4,192,768]{2,1,0:T(8,128)(2,1)}, bf16[4,192,768]{2,1,0:T(8,128)(2,1)}, u32[]{:S(2)}, u32[]{:S(2)}) %collective-permute-start.18) | collective-permute-done | bytes 1179680 | tf_op jit(solution)/shard_map/ppermute | solution.py:33
  251.9 6.3 %place_weights.4 = bf16[1536,1920]{1,0:T(8,128)(2,1)} custom-call(s32[2]{0:T(128)} %pad_add_fusion.refs_0_, bf16[768,768]{1,0:T(8,128)(2,1)} %bitcast.20.refs_1_, bf16[768,768]{1,0:T(8,128)(2,1)} %bitcast.21.refs_2_, bf16[1536,1152]{1,0:T(8,128)(2,1)} %place_weights.3.refs_1_.refs_3_, f32[4,512,768]{2,1,0:T(8,128)} %mix_within_block.1.refs_4_.refs_1_.yl_ref), custom_call_target="tpu_custom_call" | custom-call | tf_op jit(solution)/shard_map/place_weights/pallas_call | solution.py:712
  258.2 9.9 %fusion.14.z_ref = f32[4,528,768]{2,1,0:T(8,128)} fusion(bf16[4,528,1536]{2,1,0:T(8,128)(2,1)} %input_norm.1.refs_9_, bf16[1536,1920]{1,0:T(8,128)(2,1)} %place_weights.4), kind=kOutput, calls=%fused_computation.25 | convolution fusion | flops 4982833152 | bytes 15335424 | tf_op jit(solution)/shard_map/dot_general | solution.py:885
  268.1 8.8 %fusion.17.dn_ref = f32[4,512,768]{2,1,0:T(8,128)} fusion(bf16[768,1536]{1,0:T(8,128)(2,1)S(1)} %copy-done.36, bf16[1,512,1536]{2,1,0:T(8,128)(2,1)} %bitcast.26, bf16[1,512,1536]{2,1,0:T(8,128)(2,1)} %bitcast.25, bf16[1,512,1536]{2,1,0:T(8,128)(2,1)} %bitcast.24, bf16[1,512,1536]{2,1,0:T(8,128)(2,1)} %bitcast.23), kind=kOutput, calls=%fused_computation.28 | convolution fusion | flops 4841275392 | bytes 14942208 | tf_op jit(solution)/shard_map/qtd,cd->qtc/dot_general | solution.py:887
  276.9 13.0 %gate.1 = (f32[4,512,768]{2,1,0:T(8,128)}, f32[4,8,512]{2,1,0:T(8,128)S(1)}) custom-call(f32[4,512,768]{2,1,0:T(8,128)} %mix_within_block.1.refs_4_.refs_1_.yl_ref, bf16[4,512,256]{2,1,0:T(8,128)(2,1)S(1)} %get-tuple-element.36.bc_ref.refs_1_, f32[4,128,768]{2,1,0:T(8,128)S(1)} %slice_add_fusion.1.inc_ref.refs_3_, f32[4,528,768]{2,1,0:T(8,128)} %fusion.14.z_ref, ...), custom_call_target="tpu_custom_call" | custom-call | flops 402653184 | bytes 25165824 | tf_op jit(solution)/shard_map/gate/pallas_call | solution.py:889
  291.9 9.3 %copy.80 = bf16[1536,2112]{1,0:T(8,128)(2,1)} copy(bf16[1536,2112]{0,1:T(8,128)(2,1)} %bitcast.181) | data formatting | bytes 12976128 | tf_op jit(solution)/shard_map/dot_general | solution.py:969
  302.0 15.1 %gate_back.1 = (bf16[4,512,768]{2,1,0:T(8,128)(2,1)}, f32[4,512,768]{2,1,0:T(8,128)}, bf16[4,528,1920]{2,1,0:T(8,128)(2,1)}, f32[4,128,768]{2,1,0:T(8,128)S(1)}, f32[4,8,768]{2,1,0:T(8,128)S(1)}) custom-call(f32[4,512,768]{2,1,0:T(8,128)} %get-tuple-element.39.y_ref, f32[4,528,768]{2,1,0:T(8,128)} %fusion.14.z_ref, f32[4,512,768]{2,1,0:T(8,128)} %fusion.17.dn_ref, ...), custom_call_target="tpu_custom_call" | custom-call | flops 402653184 | bytes 31457280 | tf_op jit(solution)/shard_map/gate_back/pallas_call | solution.py:905
  321.1 5.5 convolution_convert_fusion
  328.8 7.2 %fusion.40.v_ref = f32[4,8,48,768]{3,2,1,0:T(8,128)} fusion(bf16[4,8,48,2112]{3,2,1,0:T(8,128)(2,1)S(1)} %bitcast.188, bf16[2112,768,1,1]{1,0,3,2:T(8,128)(2,1)S(1)} %bitcast.196), kind=kOutput, calls=%fused_computation.115 | convolution fusion | flops 4982833152 | bytes 14450688 | tf_op jit(solution)/shard_map/dot_general | solution.py:969
  336.0 8.7 %fusion.21 = f32[768,1536,1]{1,0,2:T(8,128)} fusion(bf16[4,512,768]{2,1,0:T(8,128)(2,1)S(1)} %copy-done.61, bf16[1,512,1536]{2,1,0:T(8,128)(2,1)} %bitcast.26, bf16[1,512,1536]{2,1,0:T(8,128)(2,1)} %bitcast.25, bf16[1,512,1536]{2,1,0:T(8,128)(2,1)} %bitcast.24, bf16[1,512,1536]{2,1,0:T(8,128)(2,1)} %bitcast.23), kind=kOutput, calls=%fused_computation.43 | convolution fusion | flops 4841275392 | bytes 14155776 | tf_op jit(solution)/shard_map/qtc,qtd->cd/dot_general | solution.py:971
  344.8 6.4 %split_gradients.1 = bf16[8,192,1536]{2,1,0:T(8,128)(2,1)S(1)} custom-call(s32[8]{0:T(128)S(1)} %stack.176.at_ref, f32[4,8,48,768]{3,2,1,0:T(8,128)} %fusion.40.v_ref, f32[1,8,96,1536]{3,2,1,0:T(8,128)} %bitcast.189), custom_call_target="tpu_custom_call" | custom-call | flops 2359296 | bytes 14155776 | tf_op jit(solution)/shard_map/split_gradients/pallas_call | solution.py:948
  365.0 39.3 %mix_back.2 = (bf16[4,528,1920]{2,1,0:T(8,128)(2,1)}, f32[4,8,384]{2,1,0:T(8,128)S(1)}, f32[4,8,384]{2,1,0:T(8,128)S(1)}, f32[4,512,512]{2,1,0:T(8,128)}) custom-call(f32[4,512,768]{2,1,0:T(8,128)} %get-tuple-element.35.x_ref.refs_1_.refs_0_, bf16[4,512,256]{2,1,0:T(8,128)(2,1)S(1)} %get-tuple-element.36.bc_ref.refs_1_, ...), custom_call_target="tpu_custom_call", output_to_operand_aliasing={{0}: (10, {})} | custom-call | flops 40265318400 | bytes 25165824 | tf_op jit(solution)/shard_map/mix_back/pallas_call | solution.py:1031
  406.0 5.9 fusion.41.v_ref
  417.8 7.4 %all-to-all-start.2 = ((bf16[4,192,1536]{2,1,0:T(8,128)(2,1)}), bf16[4,192,1536]{2,1,0:T(8,128)(2,1)}, u32[]{:S(2)}, u32[]{:S(2)}) async-start(bf16[4,192,1536]{2,1,0:T(8,128)(2,1)} %add_convert_fusion.refs_18_), calls=%async_computation.2 | async-start | bytes 4718592 | tf_op jit(solution)/shard_map/all_to_all | solution.py:43
  425.3 5.7 convert_add_fusion.1
  434.8 45.2 %mix_back.3 = (bf16[4,528,1920]{2,1,0:T(8,128)(2,1)}, f32[4,8,384]{2,1,0:T(8,128)S(1)}, f32[4,8,384]{2,1,0:T(8,128)S(1)}, f32[4,8,256]{2,1,0:T(8,128)S(1)}, f32[4,8,128]{2,1,0:T(8,128)S(1)}) custom-call(f32[4,512,768]{2,1,0:T(8,128)} %get-tuple-element.35.x_ref.refs_1_.refs_0_, ...), custom_call_target="tpu_custom_call", output_to_operand_aliasing={{0}: (16, {})} | custom-call | flops 40265318400 | bytes 25165824 | tf_op jit(solution)/shard_map/mix_back/pallas_call | solution.py:1031
  491.6 5.1 all-to-all-start.3
  496.7 10.3 %fusion.9 = f32[1536,768,1]{1,0,2:T(8,128)} fusion(bf16[4,528,1536]{2,1,0:T(8,128)(2,1)} %input_norm.1.refs_9_, bf16[4,528,1920]{2,1,0:T(8,128)(2,1)} %in_order.35.refs_0_), kind=kOutput, calls=%fused_computation.17 | convolution fusion | flops 4982833152 | bytes 14450688 | tf_op jit(solution)/shard_map/dot_general | solution.py:969
  514.1 5.3 split_gradient.3
  532.9 11.4 %fusion.4.refs_0_.refs_1_ = bf16[2,528,1536]{2,1,0:T(8,128)(2,1)} fusion(bf16[1536,1920]{1,0:T(8,128)(2,1)} %place_weights.4, bf16[2,2,528,1920]{3,2,1,0:T(8,128)(2,1)} %bitcast.179), kind=kOutput, calls=%fused_computation.11 | convolution fusion | flops 6230163456 | bytes 13197312 | tf_op jit(solution)/shard_map/qtc,dc->qtd/dot_general | solution.py:1088
  551.1 10.2 %fusion.2.refs_1_ = f32[2,528,1536]{2,1,0:T(8,128)S(1)} fusion(bf16[1536,1920]{1,0:T(8,128)(2,1)} %place_weights.4, bf16[2,2,528,1920]{3,2,1,0:T(8,128)(2,1)} %bitcast.180), kind=kOutput, calls=%fused_computation.5 | convolution fusion | flops 6228541440 | bytes 16441344 | tf_op jit(solution)/shard_map/qtc,dc->qtd/dot_general | solution.py:1088
  587.5 14.6 %all-to-all-done.5 = bf16[4,4,48,768]{3,2,1,0:T(8,128)(2,1)} async-done(((bf16[4,4,48,768]{3,2,1,0:T(8,128)(2,1)}), bf16[4,4,48,768]{3,2,1,0:T(8,128)(2,1)}, u32[]{:S(2)}, u32[]{:S(2)}) %all-to-all-start.5) | async-done | bytes 1179680 | tf_op jit(solution)/shard_map/all_to_all | solution.py:43
  (420 shorter events, 225.2 us)
Async XLA Ops:
  2.7 27.0 %all-to-all-start = ((bf16[4,48,1920]{2,1,0:T(8,128)(2,1)}), bf16[4,48,1920]{2,1,0:T(8,128)(2,1)S(1)}, u32[]{:S(2)}, u32[]{:S(2)}) async-start(bf16[4,48,1920]{2,1,0:T(8,128)(2,1)} %pack_weights.1.refs_1_), calls=%async_computation | async-start | bytes 1474560 | tf_op jit(solution)/shard_map/all_to_all | solution.py:43
  33.4 59.0 %collective-permute-start.7 = (bf16[544,1536]{1,0:T(8,128)(2,1)}, bf16[544,1536]{1,0:T(8,128)(2,1)S(1)}, u32[]{:S(2)}, u32[]{:S(2)}) collective-permute-start(bf16[544,1536]{1,0:T(8,128)(2,1)} %in_order.27.refs_0_), channel_id=1, source_target_pairs={{0,16},{16,0},{1,17},{17,1},{2,18},{18,2},{3,19},{19,3},{4,20},{20... | collective-permute-start | bytes 5013512 | tf_op jit(solution)/shard_map/ppermute | solution.py:33
  37.8 32.0 %collective-permute-start.11 = (bf16[192,1152]{1,0:T(8,128)(2,1)S(1)}, bf16[192,1152]{1,0:T(8,128)(2,1)S(1)}, u32[]{:S(2)}, u32[]{:S(2)}) collective-permute-start(bf16[192,1152]{1,0:T(8,128)(2,1)S(1)} %bitcast.191), channel_id=1, source_target_pairs={{0,4},{2,6},{4,0},{6,2},{1,5},{3,7},{5,1},{7,3},{8,12},{10,14},{12... | collective-permute-start | bytes 1327112 | tf_op jit(solution)/shard_map/ppermute | solution.py:33
  40.8 31.0 %collective-permute-start.13 = (bf16[192,1152]{1,0:T(8,128)(2,1)S(1)}, bf16[192,1152]{1,0:T(8,128)(2,1)S(1)}, u32[]{:S(2)}, u32[]{:S(2)}) collective-permute-start(bf16[192,1152]{1,0:T(8,128)(2,1)S(1)} %bitcast.192), channel_id=1, source_target_pairs={{0,6},{2,0},{4,2},{6,4},{1,7},{3,1},{5,3},{7,5},{8,14},{10,8},{12,... | collective-permute-start | bytes 1327112 | tf_op jit(solution)/shard_map/ppermute | solution.py:33
  41.8 30.1 %collective-permute-start.8 = (bf16[192,1152]{1,0:T(8,128)(2,1)S(1)}, bf16[192,1152]{1,0:T(8,128)(2,1)S(1)}, u32[]{:S(2)}, u32[]{:S(2)}) collective-permute-start(bf16[192,1152]{1,0:T(8,128)(2,1)S(1)} %bitcast.193), channel_id=1, source_target_pairs={{0,1},{1,0},{2,3},{3,2},{4,5},{5,4},{6,7},{7,6},{8,9},{9,8},{10,11... | collective-permute-start | bytes 1327112 | tf_op jit(solution)/shard_map/ppermute | solution.py:33
  51.4 20.6 %collective-permute-start.10 = (bf16[192,1152]{1,0:T(8,128)(2,1)S(1)}, bf16[192,1152]{1,0:T(8,128)(2,1)S(1)}, u32[]{:S(2)}, u32[]{:S(2)}) collective-permute-start(bf16[192,1152]{1,0:T(8,128)(2,1)S(1)} %collective-permute-done.9.refs_3_), channel_id=1, source_target_pairs={{0,1},{1,0},{2,3},{3,2},{4,5},{5,4},{6,7},{7,6},{8,9},{9,8},{10,11... | collective-permute-start | bytes 1327112 | tf_op jit(solution)/shard_map/ppermute | solution.py:33
  72.0 33.1 %collective-permute-start.6 = (bf16[544,1536]{1,0:T(8,128)(2,1)}, bf16[544,1536]{1,0:T(8,128)(2,1)}, u32[]{:S(2)}, u32[]{:S(2)}) collective-permute-start(bf16[544,1536]{1,0:T(8,128)(2,1)} %in_order.27.refs_0_), channel_id=1, source_target_pairs={{0,8},{8,0},{1,9},{9,1},{2,10},{10,2},{3,11},{11,3},{4,12},{12,4},... | collective-permute-start | bytes 5013512 | tf_op jit(solution)/shard_map/ppermute | solution.py:33
  118.1 70.3 %collective-permute-start.24 = (bf16[192,768]{1,0:T(8,128)(2,1)}, bf16[192,768]{1,0:T(8,128)(2,1)}, u32[]{:S(2)}, u32[]{:S(2)}) collective-permute-start(bf16[192,768]{1,0:T(8,128)(2,1)} %in_order.33), channel_id=1, source_target_pairs={{0,6},{2,0},{4,2},{6,4},{1,7},{3,1},{5,3},{7,5},{8,14},{10,8},{12,... | collective-permute-start | bytes 884744 | tf_op jit(solution)/shard_map/ppermute | solution.py:33
  129.0 60.0 %collective-permute-start.23 = (bf16[192,768]{1,0:T(8,128)(2,1)}, bf16[192,768]{1,0:T(8,128)(2,1)}, u32[]{:S(2)}, u32[]{:S(2)}) collective-permute-start(bf16[192,768]{1,0:T(8,128)(2,1)} %in_order.33), channel_id=1, source_target_pairs={{0,4},{2,6},{4,0},{6,2},{1,5},{3,7},{5,1},{7,3},{8,12},{10,14},{12... | collective-permute-start | bytes 884744 | tf_op jit(solution)/shard_map/ppermute | solution.py:33
  129.0 60.0 %collective-permute-start.22 = (bf16[192,768]{1,0:T(8,128)(2,1)}, bf16[192,768]{1,0:T(8,128)(2,1)}, u32[]{:S(2)}, u32[]{:S(2)}) collective-permute-start(bf16[192,768]{1,0:T(8,128)(2,1)} %in_order.33), channel_id=1, source_target_pairs={{0,2},{2,4},{4,6},{6,0},{1,3},{3,5},{5,7},{7,1},{8,10},{10,12},{12... | collective-permute-start | bytes 884744 | tf_op jit(solution)/shard_map/ppermute | solution.py:33
  133.6 58.4 %all-to-all-start.1 = ((bf16[4,192,768]{2,1,0:T(8,128)(2,1)}), bf16[4,192,768]{2,1,0:T(8,128)(2,1)}, u32[]{:S(2)}, u32[]{:S(2)}) async-start(bf16[4,192,768]{2,1,0:T(8,128)(2,1)} %broadcast_in_dim.84), calls=%async_computation.1 | async-start | bytes 2359296 | tf_op jit(solution)/shard_map/all_to_all | solution.py:43
  178.9 45.0 %collective-permute-start.16 = (bf16[4,144,768]{2,1,0:T(8,128)(2,1)}, bf16[4,144,768]{2,1,0:T(8,128)(2,1)}, u32[]{:S(2)}, u32[]{:S(2)}) collective-permute-start(bf16[4,144,768]{2,1,0:T(8,128)(2,1)} %pad_maximum_fusion.3), channel_id=1, source_target_pairs={{0,1},{1,2},{2,3},{3,4},{4,5},{5,6},{6,7},{8,9},{9,10},{10,11},{11... | collective-permute-start | bytes 2654216 | tf_op jit(solution)/shard_map/ppermute | solution.py:39
  183.5 43.9 %collective-permute-start.17 = (bf16[4,144,768]{2,1,0:T(8,128)(2,1)}, bf16[4,144,768]{2,1,0:T(8,128)(2,1)}, u32[]{:S(2)}, u32[]{:S(2)}) collective-permute-start(bf16[4,144,768]{2,1,0:T(8,128)(2,1)} %pad_maximum_fusion.3), channel_id=1, source_target_pairs={{0,2},{1,3},{2,4},{3,5},{4,6},{5,7},{8,10},{9,11},{10,12},{11,13},... | collective-permute-start | bytes 2654216 | tf_op jit(solution)/shard_map/ppermute | solution.py:39
  188.4 35.5 %collective-permute-start.20 = (bf16[512,1536]{1,0:T(8,128)(2,1)}, bf16[512,1536]{1,0:T(8,128)(2,1)}, u32[]{:S(2)}, u32[]{:S(2)}) collective-permute-start(bf16[512,1536]{1,0:T(8,128)(2,1)} %in_order.31), channel_id=1, source_target_pairs={{0,16},{16,0},{1,17},{17,1},{2,18},{18,2},{3,19},{19,3},{4,20},{20... | collective-permute-start | bytes 4718600 | tf_op jit(solution)/shard_map/ppermute | solution.py:33
  191.4 37.3 %collective-permute-start.25 = (bf16[4,192,768]{2,1,0:T(8,128)(2,1)}, bf16[4,192,768]{2,1,0:T(8,128)(2,1)}, u32[]{:S(2)}, u32[]{:S(2)}) collective-permute-start(bf16[4,192,768]{2,1,0:T(8,128)(2,1)} %in_order.34), channel_id=1, source_target_pairs={{0,1},{1,0},{2,3},{3,2},{4,5},{5,4},{6,7},{7,6},{8,9},{9,8},{10,11... | collective-permute-start | bytes 3538952 | tf_op jit(solution)/shard_map/ppermute | solution.py:33
  191.9 59.9 %collective-permute-start.18 = (bf16[4,192,768]{2,1,0:T(8,128)(2,1)}, bf16[4,192,768]{2,1,0:T(8,128)(2,1)}, u32[]{:S(2)}, u32[]{:S(2)}) collective-permute-start(bf16[4,192,768]{2,1,0:T(8,128)(2,1)} %in_order.30), channel_id=1, source_target_pairs={{0,1},{1,0},{2,3},{3,2},{4,5},{5,4},{6,7},{7,6},{8,9},{9,8},{10,11... | collective-permute-start | bytes 3538952 | tf_op jit(solution)/shard_map/ppermute | solution.py:33
  223.9 44.2 %collective-permute-start.19 = (bf16[512,1536]{1,0:T(8,128)(2,1)}, bf16[512,1536]{1,0:T(8,128)(2,1)}, u32[]{:S(2)}, u32[]{:S(2)}) collective-permute-start(bf16[512,1536]{1,0:T(8,128)(2,1)} %in_order.31), channel_id=1, source_target_pairs={{0,8},{8,0},{1,9},{9,1},{2,10},{10,2},{3,11},{11,3},{4,12},{12,4},... | collective-permute-start | bytes 4718600 | tf_op jit(solution)/shard_map/ppermute | solution.py:33
  223.9 44.2 %collective-permute-start.21 = (bf16[512,1536]{1,0:T(8,128)(2,1)}, bf16[512,1536]{1,0:T(8,128)(2,1)}, u32[]{:S(2)}, u32[]{:S(2)}) collective-permute-start(bf16[512,1536]{1,0:T(8,128)(2,1)} %in_order.32), channel_id=1, source_target_pairs={{0,8},{8,0},{1,9},{9,1},{2,10},{10,2},{3,11},{11,3},{4,12},{12,4},... | collective-permute-start | bytes 4718600 | tf_op jit(solution)/shard_map/ppermute | solution.py:33
  318.2 40.2 %collective-permute-start.30 = (bf16[4,144,768]{2,1,0:T(8,128)(2,1)}, bf16[4,144,768]{2,1,0:T(8,128)(2,1)S(1)}, u32[]{:S(2)}, u32[]{:S(2)}) collective-permute-start(bf16[4,144,768]{2,1,0:T(8,128)(2,1)} %pad_maximum_fusion.2), channel_id=1, source_target_pairs={{1,0},{2,1},{3,2},{4,3},{5,4},{6,5},{7,6},{9,8},{10,9},{11,10},{12... | collective-permute-start | bytes 2654216 | tf_op jit(solution)/shard_map/ppermute | solution.py:39
  319.8 43.8 %collective-permute-start.31 = (bf16[4,144,768]{2,1,0:T(8,128)(2,1)}, bf16[4,144,768]{2,1,0:T(8,128)(2,1)}, u32[]{:S(2)}, u32[]{:S(2)}) collective-permute-start(bf16[4,144,768]{2,1,0:T(8,128)(2,1)} %pad_maximum_fusion.2), channel_id=1, source_target_pairs={{2,0},{3,1},{4,2},{5,3},{6,4},{7,5},{10,8},{11,9},{12,10},{13,11},... | collective-permute-start | bytes 2654216 | tf_op jit(solution)/shard_map/ppermute | solution.py:39
  326.6 98.6 %collective-permute-start.28 = (bf16[2,512,1536]{2,1,0:T(8,128)(2,1)}, bf16[2,512,1536]{2,1,0:T(8,128)(2,1)}, u32[]{:S(2)}, u32[]{:S(2)}) collective-permute-start(bf16[2,512,1536]{2,1,0:T(8,128)(2,1)} %convolution_convert_fusion), channel_id=1, source_target_pairs={{0,8},{8,0},{1,9},{9,1},{2,10},{10,2},{3,11},{11,3},{4,12},{12,4},... | collective-permute-start | bytes 9437192 | tf_op jit(solution)/shard_map/ppermute | solution.py:33
  355.0 59.2 %collective-permute-start.32 = (bf16[4,192,1536]{2,1,0:T(8,128)(2,1)}, bf16[4,192,1536]{2,1,0:T(8,128)(2,1)}, u32[]{:S(2)}, u32[]{:S(2)}) collective-permute-start(bf16[4,192,1536]{2,1,0:T(8,128)(2,1)} %slice.367), channel_id=1, source_target_pairs={{0,1},{1,0},{2,3},{3,2},{4,5},{5,4},{6,7},{7,6},{8,9},{9,8},{10,11... | collective-permute-start | bytes 7077896 | tf_op jit(solution)/shard_map/ppermute | solution.py:33
  414.1 67.9 %collective-permute-start.34 = (bf16[4,4,48,384]{3,2,1,0:T(8,128)(2,1)}, bf16[4,4,48,384]{3,2,1,0:T(8,128)(2,1)}, u32[]{:S(2)}, u32[]{:S(2)}) collective-permute-start(bf16[4,4,48,384]{3,2,1,0:T(8,128)(2,1)} %get-tuple-element.63), channel_id=1, source_target_pairs={{0,1},{1,0},{2,3},{3,2},{4,5},{5,4},{6,7},{7,6},{8,9},{9,8},{10,11... | collective-permute-start | bytes 1769480 | tf_op jit(solution)/shard_map/ppermute | solution.py:33
  417.8 70.6 %all-to-all-start.2 = ((bf16[4,192,1536]{2,1,0:T(8,128)(2,1)}), bf16[4,192,1536]{2,1,0:T(8,128)(2,1)}, u32[]{:S(2)}, u32[]{:S(2)}) async-start(bf16[4,192,1536]{2,1,0:T(8,128)(2,1)} %add_convert_fusion.refs_18_), calls=%async_computation.2 | async-start | bytes 4718592 | tf_op jit(solution)/shard_map/all_to_all | solution.py:43
  432.3 52.0 %collective-permute-start.29 = (bf16[512,1536]{1,0:T(8,128)(2,1)}, bf16[512,1536]{1,0:T(8,128)(2,1)}, u32[]{:S(2)}, u32[]{:S(2)}) collective-permute-start(bf16[512,1536]{1,0:T(8,128)(2,1)} %fusion.20.refs_19_), channel_id=1, source_target_pairs={{0,16},{16,0},{1,17},{17,1},{2,18},{18,2},{3,19},{19,3},{4,20},{20... | collective-permute-start | bytes 4718600 | tf_op jit(solution)/shard_map/ppermute | solution.py:33
  480.5 26.5 %collective-permute-start.38 = (f32[160,128]{1,0:T(8,128)S(1)}, f32[160,128]{1,0:T(8,128)S(1)}, u32[]{:S(2)}, u32[]{:S(2)}) collective-permute-start(f32[160,128]{1,0:T(8,128)S(1)} %fusion.23.refs_0_), channel_id=1, source_target_pairs={{0,16},{16,0},{1,17},{17,1},{2,18},{18,2},{3,19},{19,3},{4,20},{20... | collective-permute-start | bytes 245768 | tf_op jit(solution)/shard_map/ppermute | solution.py:130
  491.6 35.0 %all-to-all-start.3 = ((bf16[4,4,48,384]{3,2,1,0:T(8,128)(2,1)}), bf16[4,4,48,384]{3,2,1,0:T(8,128)(2,1)S(1)}, u32[]{:S(2)}, u32[]{:S(2)}) async-start(bf16[4,4,48,384]{3,2,1,0:T(8,128)(2,1)} %in_order.37), calls=%async_computation.3 | async-start | bytes 1179648 | tf_op jit(solution)/shard_map/all_to_all | solution.py:43
  520.6 27.1 %collective-permute-start.35 = (bf16[4,4,48,768]{3,2,1,0:T(8,128)(2,1)}, bf16[4,4,48,768]{3,2,1,0:T(8,128)(2,1)}, u32[]{:S(2)}, u32[]{:S(2)}) collective-permute-start(bf16[4,4,48,768]{3,2,1,0:T(8,128)(2,1)} %slice.376), channel_id=1, source_target_pairs={{0,1},{1,0},{2,3},{3,2},{4,5},{5,4},{6,7},{7,6},{8,9},{9,8},{10,11... | collective-permute-start | bytes 3538952 | tf_op jit(solution)/shard_map/ppermute | solution.py:33
  524.1 20.2 %collective-permute-start.40 = (f32[160,128]{1,0:T(8,128)S(1)}, f32[160,128]{1,0:T(8,128)S(1)}, u32[]{:S(2)}, u32[]{:S(2)}) collective-permute-start(f32[160,128]{1,0:T(8,128)S(1)} %add.259.refs_0_), channel_id=1, source_target_pairs={{0,4},{2,6},{4,0},{6,2},{1,5},{3,7},{5,1},{7,3},{8,12},{10,14},{12... | collective-permute-start | bytes 245768 | tf_op jit(solution)/shard_map/ppermute | solution.py:130
  527.5 22.8 %all-to-all-start.4 = ((bf16[4,48,1152]{2,1,0:T(8,128)(2,1)}), bf16[4,48,1152]{2,1,0:T(8,128)(2,1)S(1)}, u32[]{:S(2)}, u32[]{:S(2)}) async-start(bf16[4,48,1152]{2,1,0:T(8,128)(2,1)} %pad_maximum_fusion.8), calls=%async_computation.4 | async-start | bytes 884736 | tf_op jit(solution)/shard_map/all_to_all | solution.py:43
  568.1 34.0 %all-to-all-start.5 = ((bf16[4,4,48,768]{3,2,1,0:T(8,128)(2,1)}), bf16[4,4,48,768]{3,2,1,0:T(8,128)(2,1)}, u32[]{:S(2)}, u32[]{:S(2)}) async-start(bf16[4,4,48,768]{3,2,1,0:T(8,128)(2,1)} %in_order.40), calls=%async_computation.5 | async-start | bytes 2359296 | tf_op jit(solution)/shard_map/all_to_all | solution.py:43
  572.8 38.0 %collective-permute-start.37 = (bf16[528,1536]{1,0:T(8,128)(2,1)}, bf16[528,1536]{1,0:T(8,128)(2,1)}, u32[]{:S(2)}, u32[]{:S(2)}) collective-permute-start(bf16[528,1536]{1,0:T(8,128)(2,1)} %fusion.19.refs_2_), channel_id=1, source_target_pairs={{0,16},{16,0},{1,17},{17,1},{2,18},{18,2},{3,19},{19,3},{4,20},{20... | collective-permute-start | bytes 4866056 | tf_op jit(solution)/shard_map/ppermute | solution.py:33
  (86 other events, 1326.6 us)

commit v3 on v2

--- a/solution.py
+++ b/solution.py
@@ -15,6 +15,7 @@
 XBC = 3328
 LONGEST = 1024
 HALO = 16
+TILE = 128
 PAIRS = 3
 WIDE = PAIRS * 128
 LAST = WIDE + 3 * 128
@@ -154,6 +155,14 @@
     return jnp.where(low_half(table.shape[0]), table[:, at : at + 1], table[:, at + 1 : at + 2])
 
 
+def lane_wise(table, kind):
+    high = table.astype(BF)
+    low = (table - high.astype(F32)).astype(BF)
+    head_of = lax.broadcasted_iota(jnp.int32, (128, WIDE), 1) // HEADDIM + kind
+    pick = (head_of == lax.broadcasted_iota(jnp.int32, (128, WIDE), 0)).astype(BF)
+    return nn(jnp.concatenate([high, low], axis=1), jnp.concatenate([pick, pick], axis=0))
+
+
 def lanes_of(pair):
     return slice(pair * 128, (pair + 1) * 128)
 
@@ -174,30 +183,36 @@
     return jnp.concatenate(out, axis=0)
 
 
-def to_block_end(endn, carry, chunks):
-    out, run = [endn[rows_of(chunks - 1)]], carry[end_of(chunks - 1)]
+def to_block_end(endn, table, chunks):
+    out, run = [endn[rows_of(chunks - 1)]], None
     for c in range(chunks - 2, -1, -1):
+        keep = lane_wise(table[(c + 2) * GROUP - 8 : (c + 2) * GROUP], CARRY)[7:]
+        run = keep if run is None else run * keep
         out.insert(0, endn[rows_of(c)] * run)
-        run = run * carry[end_of(c)]
     return jnp.concatenate(out, axis=0)
 
 
-def convolved(ext, taps, same):
-    rows = ext.shape[0] - HALO
-    pre = taps[CONV : CONV + 1] + taps[CONV - 1 : CONV] * ext[HALO:]
+def earlier_rows(v, k):
+    return pltpu.roll(v, k, 0)[: v.shape[0] - HALO]
+
+
+def convolved(v, taps, same):
+    rows = v.shape[0] - HALO
+    pre = taps[CONV : CONV + 1] + taps[CONV - 1 : CONV] * v[:rows]
     for k in range(1, CONV):
-        pre = pre + same[k - 1] * (taps[CONV - 1 - k : CONV - k] * ext[HALO - k : HALO - k + rows])
+        pre = pre + same[k - 1] * (taps[CONV - 1 - k : CONV - k] * earlier_rows(v, k))
     return pre
 
 
-def extended(v):
-    rows = v.shape[0] - HALO
-    v = v.astype(BF).astype(F32)
-    return jnp.concatenate([v[rows:], v[:rows]], axis=0)
+def rounded(v):
+    return v.astype(BF).astype(F32)
 
 
 def same_columns(table):
-    return [table[:, SAME + k : SAME + k + 1] for k in range(CONV - 1)]
+    rows = table.shape[0]
+    return [
+        jnp.broadcast_to(table[:, SAME + k : SAME + k + 1], (rows, 128)) for k in range(CONV - 1)
+    ]
 
 
 def pack_kernel(weight_ref, first_ref, cols, heads):
@@ -312,17 +327,17 @@
     @pl.when(pl.program_id(1) == 0)
     def _():
         for i, main in enumerate((bm_ref, cm_ref)):
-            pre = convolved(extended(main[0]), tb_ref[:, lanes_of(i)], same)
+            pre = convolved(rounded(main[0]), tb_ref[:, lanes_of(i)], same)
             bc_ref[0, :, lanes_of(i)] = (pre * jax.nn.sigmoid(pre)).astype(BF)
 
     weighted = []
+    left = to_block_end(lane_wise(table, ENDN), table, chunks) * lane_wise(table, DT)
     for j in range(PAIRS):
         at = lanes_of(j)
-        pre = convolved(extended(xm_ref[0, :, at]), tx_ref[:, at], same)
+        pre = convolved(rounded(xm_ref[0, :, at]), tx_ref[:, at], same)
         x = pre * jax.nn.sigmoid(pre)
         x_ref[0, :, at] = x
-        left = to_block_end(spread(table, ENDN, j), spread(table, CARRY, j), chunks)
-        weighted.append((left * spread(table, DT, j) * x).astype(BF))
+        weighted.append((left[:, at] * x).astype(BF))
     own_ref[0] = tn(bc_ref[0, :, :STATE], jnp.concatenate(weighted, axis=1))
 
 
@@ -350,29 +365,35 @@
             score[c] = nt(bc_ref[0, rows_of(c), STATE:], bc_ref[0, rows_of(c), :STATE])
             mask[c] = causal(table, rt_ref[0, SEG_ROW : SEG_ROW + 1, :], c, False)
 
-    for j in range(PAIRS):
-        at = lanes_of(j)
-        x = x_ref[0, :, at]
-        xd = x * spread(table, DT, j)
-        parts = halves_of(xd, low_half(xd.shape[0]))
-        carry = spread(table, CARRY, j)
-        ending = (spread(table, ENDN, j) * xd).astype(BF)
-        cum_rows = [rt_ref[0, pl.ds(base + 2 * j + e, 1), :] for e in range(2)]
-        state = None
-        for c in range(chunks):
-            rows = rows_of(c)
-            y = skip_ref[0:1, at] * x[rows]
-            for e in range(2):
-                h = 2 * j + e
-                row = cum_rows[e][:, rows]
-                mixing = score[c] * jnp.exp(table[rows, CUM + h : CUM + h + 1] - row + mask[c])
-                y = y + nn(mixing.astype(BF), parts[e][rows])
-            if c:
-                y = y + carry[rows] * nn(bc_ref[0, rows, STATE:], state.astype(BF))
-            y_ref[0, rows, at] = y
-            if c + 1 < chunks:
-                added = tn(bc_ref[0, rows, :STATE], ending[rows])
-                state = added if c == 0 else carry[end_of(c)] * state + added
+    dts, endns = lane_wise(table, DT), lane_wise(table, ENDN)
+    carries = [lane_wise(table[rows_of(c)], CARRY) for c in range(1, chunks)]
+    states = None
+    for c in range(chunks):
+        rows = rows_of(c)
+        x = x_ref[0, rows, :]
+        xd = x * dts[rows]
+        xdb = xd.astype(BF)
+        y_in = skip_ref[0:1, :] * x
+        if c:
+            y_in = y_in + carries[c - 1] * nn(bc_ref[0, rows, STATE:], states.astype(BF))
+        if c + 1 < chunks:
+            added = tn(bc_ref[0, rows, :STATE], (endns[rows] * xd).astype(BF))
+            states = added if c == 0 else carries[c - 1][GROUP - 1 :] * states + added
+        for j in range(PAIRS):
+            at = lanes_of(j)
+            cum_rows = [rt_ref[0, pl.ds(base + 2 * j + e, 1), :] for e in range(2)]
+            for top in range(0, GROUP, TILE):
+                here, live = slice(top, top + TILE), slice(0, top + TILE)
+                tile_rows = slice(c * GROUP + top, c * GROUP + top + TILE)
+                scores, masks = score[c, here, live], mask[c, here, live]
+                mixing = []
+                for e in range(2):
+                    h = 2 * j + e
+                    row = cum_rows[e][:, c * GROUP : c * GROUP + top + TILE]
+                    decay = jnp.exp(table[tile_rows, CUM + h : CUM + h + 1] - row + masks)
+                    mixing.append((scores * decay).astype(BF))
+                y = nn(jnp.concatenate(mixing, axis=0), xdb[live, at])
+                y_ref[0, tile_rows, at] = y_in[here, at] + jnp.where(low_half(TILE), y[:TILE], y[TILE:])
 
 
 def gate_kernel(yl_ref, bc_ref, inc_ref, z_ref, dn_ref, gain_ref, ct_ref, y_ref, sums_ref, held):
@@ -380,9 +401,10 @@
     chunks = table.shape[0] // GROUP
     from_state = nn(bc_ref[0, :, STATE:], inc_ref[0].astype(BF))
     squares, pulled = None, None
+    reach = from_start(lane_wise(table, CARRY), chunks)
     for j in range(PAIRS):
         at = lanes_of(j)
-        y = yl_ref[0, :, at] + from_start(spread(table, CARRY, j), chunks) * from_state[:, at]
+        y = yl_ref[0, :, at] + reach[:, at] * from_state[:, at]
         y_ref[0, :, at] = y
         z = z_ref[0, :, at]
         gated = y * (z * jax.nn.sigmoid(z))
@@ -417,6 +439,7 @@
     r = lax.rsqrt(sums[:, 0:1] * (1.0 / INNER) + EPSILON)
     along_unit = r * (1.0 / INNER) * sums[:, 1:2]
     pulled = []
+    reach = from_start(lane_wise(table, CARRY), chunks)
     for j in range(PAIRS):
         at = lanes_of(j)
         gain = gain_ref[0:1, at]
@@ -430,32 +453,28 @@
         dy_ref[0, :, at] = dy
         dz_ref[0, : y.shape[0], at] = (dg * y * (sig * (1.0 + z * (1.0 - sig)))).astype(BF)
         dz_ref[0, y.shape[0] :, at] = jnp.zeros((HALO, 128), BF)
-        pulled.append((from_start(spread(table, CARRY, j), chunks) * dy).astype(BF))
+        pulled.append((reach[:, at] * dy).astype(BF))
         grad = jnp.sum(dn * unit, axis=0, keepdims=True)
         gg_ref[0, :, at] = jnp.broadcast_to(grad, (8, 128))
     pull_ref[0] = tn(bc_ref[0, :, STATE:], jnp.concatenate(pulled, axis=1))
 
 
-def conv_back(d_conv, ext, taps, same):
+def conv_back(d_conv, v, taps, same):
     rows, width = d_conv.shape
-    pre = convolved(ext, taps, same)
+    pre = convolved(v, taps, same)
     sig = jax.nn.sigmoid(pre)
     d_pre = d_conv * (sig * (1.0 + pre * (1.0 - sig)))
-    d_ext = jnp.concatenate(
-        [jnp.zeros((HALO, width), F32), taps[CONV - 1 : CONV] * d_pre], axis=0
-    )
-    grads = [None] * 8
-    grads[CONV - 1] = jnp.sum(d_pre * ext[HALO:], axis=0, keepdims=True)
+    none = jnp.zeros((HALO, width), F32)
+    d_v = jnp.concatenate([taps[CONV - 1 : CONV] * d_pre, none], axis=0)
+    grads = [jnp.zeros((1, width), F32)] * 8
+    grads[CONV - 1] = jnp.sum(d_pre * v[:rows], axis=0, keepdims=True)
     grads[CONV] = jnp.sum(d_pre, axis=0, keepdims=True)
     for k in range(1, CONV):
         kept = same[k - 1] * d_pre
-        grads[CONV - 1 - k] = jnp.sum(kept * ext[HALO - k : HALO - k + rows], axis=0, keepdims=True)
-        d_ext = d_ext + taps[CONV - 1 - k : CONV - k] * jnp.concatenate(
-            [jnp.zeros((HALO - k, width), F32), kept, jnp.zeros((k, width), F32)], axis=0
-        )
-    grads = [g if g is not None else jnp.zeros((1, width), F32) for g in grads]
-    d_rows = jnp.concatenate([d_ext[HALO:], d_ext[:HALO]], axis=0).astype(BF)
-    return d_rows, jnp.concatenate(grads, axis=0)
+        grads[CONV - 1 - k] = jnp.sum(kept * earlier_rows(v, k), axis=0, keepdims=True)
+        moved = pltpu.roll(jnp.concatenate([kept, none], axis=0), rows + HALO - k, 0)
+        d_v = d_v + taps[CONV - 1 - k : CONV - k] * moved
+    return d_v.astype(BF), jnp.concatenate(grads, axis=0)
 
 
 def mix_back_kernel(*refs, base, first, last):
@@ -467,28 +486,29 @@
     if last:
         bm_ref, cm_ref, dt_ref, tb_ref, par_ref = refs[at_ref : at_ref + 5]
     if last:
-        d_ref, gx_ref, gs_ref, gb_ref, gh_ref = refs[-6:-1]
+        d_ref, gx_ref, gs_ref, gb_ref, gh_ref = refs[-11:-6]
     else:
-        d_ref, gx_ref, gs_ref, part_ref = refs[-5:-1]
-    d_x = refs[-1]
+        d_ref, gx_ref, gs_ref, part_ref = refs[-10:-6]
+    d_x, score_ref, mask_ref, d_score_ref, d_step_ref, cross_ref = refs[-6:]
 
     table = ct_ref[0, 0]
     chunks = x_ref.shape[1] // GROUP
+    cross_ref[2 * PAIRS :] = jnp.zeros((8 - 2 * PAIRS, cross_ref.shape[1]), F32)
     down = lax.broadcasted_iota(jnp.int32, (GROUP, GROUP), 0)
     right = lax.broadcasted_iota(jnp.int32, (GROUP, GROUP), 1)
     before = (right < down).astype(BF)
     upto = (right >= down).astype(BF)
+    upto_t, crossed = (down >= right).astype(BF), down < right
     same = same_columns(table)
-    lane = lax.broadcasted_iota(jnp.int32, (GROUP, 128), 1)
     half = low_half(GROUP)
-
-    def lane_wise(kind, c):
-        return jnp.concatenate([spread(table[rows_of(c)], kind, j) for j in range(PAIRS)], axis=1)
-
-    carries = [lane_wise(CARRY, c) for c in range(chunks)]
+    head_of = lax.broadcasted_iota(jnp.int32, (WIDE, 128), 0) // HEADDIM + base
+    pick = (head_of == lax.broadcasted_iota(jnp.int32, (WIDE, 128), 1)).astype(BF)
+
+    carries = [lane_wise(table[rows_of(c)], CARRY) for c in range(chunks)]
     pulled = [carries[c] * dy_ref[0, rows_of(c), :] for c in range(chunks)]
-    xds = [x_ref[0, rows_of(c), :] * lane_wise(DT, c) for c in range(chunks)]
-    endns = [lane_wise(ENDN, c) for c in range(chunks)]
+    dts = [lane_wise(table[rows_of(c)], DT) for c in range(chunks)]
+    xds = [x_ref[0, rows_of(c), :] * dts[c] for c in range(chunks)]
+    endns = [lane_wise(table[rows_of(c)], ENDN) for c in range(chunks)]
     endings = [endns[c] * xds[c] for c in range(chunks)]
     states, adjoints = [inc_ref[0]], [adj_ref[0]]
     for c in range(chunks - 1):
@@ -505,57 +525,66 @@
         state_b, adj_b = states[c].astype(BF), adjoints[c].astype(BF)
         from_state = pulled[c] * nn(reads, state_b)
         to_end = nn(keys, adj_b)
-        across = nn(upto, from_state.astype(BF)) + nn(before, (endings[c] * to_end).astype(BF))
-        across = across + carries[c][GROUP - 1 :] * jnp.sum(
-            states[c] * adjoints[c], axis=0, keepdims=True
-        )
+        whole = carries[c][GROUP - 1 :] * jnp.sum(states[c] * adjoints[c], axis=0, keepdims=True)
+        logs = nn(upto, nn(from_state.astype(BF), pick).astype(BF))
+        logs = logs + nn(before, nn((endings[c] * to_end).astype(BF), pick).astype(BF))
+        logs = logs + nn(jnp.broadcast_to(whole, (8, WIDE)).astype(BF), pick)[:1]
         d_k, d_r = nt(endings[c].astype(BF), adj_b), nt(pulled[c].astype(BF), state_b)
         score = nt(keys, reads)
         mask = causal(table, rt_ref[0, SEG_ROW : SEG_ROW + 1, :], c, True)
-        d_scores = None
-        logs, steps = jnp.zeros((GROUP, 128), F32), jnp.zeros((GROUP, 128), F32)
+        score_ref[...], mask_ref[...] = score, mask
         for j in range(PAIRS):
             at = lanes_of(j)
             dy = dy_ref[0, rows, at]
             dyb = dy.astype(BF)
             parts = halves_of(xds[c][:, at], half)
-            d_xd = []
-            crossings = []
+            crossings = [None, None]
+            for top in range(0, GROUP, TILE):
+                here, live = slice(top, top + TILE), slice(top // 128 * 128, GROUP)
+                tile_rows = slice(c * GROUP + top, c * GROUP + top + TILE)
+                scores = score_ref[here, live]
+                weighted = nt(jnp.concatenate([parts[0][here], parts[1][here]], axis=0), dyb[live])
+                decays = []
+                for e in range(2):
+                    h = 2 * j + e
+                    row = rt_ref[0, base + h : base + h + 1, rows][:, live]
+                    decays.append(jnp.exp(row - table[tile_rows, CUM + h : CUM + h + 1] + mask_ref[here, live]))
+                weighted = [decays[0] * weighted[:TILE], decays[1] * weighted[TILE:]]
+                d_scores = weighted[0] + weighted[1]
+                mixing = jnp.concatenate([(scores * v).astype(BF) for v in decays], axis=0)
+                d_xd = nn(mixing, dyb[live])
+                d_xd = [d_xd[:TILE], d_xd[TILE:]]
+                after_t = nn(jnp.concatenate([(scores * v).astype(BF) for v in weighted], axis=0), upto_t[live])
+                for e in range(2):
+                    mine = jnp.where(crossed[here], after_t[e * TILE : (e + 1) * TILE], 0.0)
+                    crossing = jnp.sum(mine, axis=0, keepdims=True)
+                    crossings[e] = crossing if top == 0 else crossings[e] + crossing
+                if j == 0:
+                    d_score_ref[here, live] = d_scores
+                else:
+                    d_score_ref[here, live] += d_scores
+                u = jnp.where(half[:TILE], d_xd[0], d_xd[1]) + endns[c][here, at] * to_end[here, at]
+                x = x_ref[0, tile_rows, at]
+                d_x[tile_rows, at] = dts[c][here, at] * u + skip_ref[0:1, at] * dy[here]
+                d_step_ref[here, at] = (x * u).astype(BF)
             for e in range(2):
-                h = 2 * j + e
-                row = rt_ref[0, base + h : base + h + 1, rows]
-                decay = jnp.exp(row - table[rows, CUM + h : CUM + h + 1] + mask)
-                weighted = decay * nt(parts[e], dyb)
-                d_scores = weighted if d_scores is None else d_scores + weighted
-                d_xd.append(nn((score * decay).astype(BF), dyb))
-                crossing = nn(before, (score * weighted).astype(BF))
-                crossings.append(
-                    jnp.sum(jnp.where(right >= down, crossing, 0.0), axis=1, keepdims=True)
-                )
-            u = jnp.where(half, d_xd[0], d_xd[1]) + endns[c][:, at] * to_end[:, at]
-            x = x_ref[0, rows, at]
-            d_x[rows, at] = spread(table[rows], DT, j) * u + skip_ref[0:1, at] * dy
-            d_step = x * u
-            for e in range(2):
-                keep = half if e == 0 else jnp.logical_not(half)
-                log_e = crossings[e] + jnp.sum(
-                    jnp.where(keep, across[:, at], 0.0), axis=1, keepdims=True
-                )
-                step_e = jnp.sum(jnp.where(keep, d_step, 0.0), axis=1, keepdims=True)
-                place = lane == base + 2 * j + e
-                logs = jnp.where(place, log_e, logs)
-                steps = jnp.where(place, step_e, steps)
+                cross_ref[2 * j + e : 2 * j + e + 1, rows] = crossings[e]
         all_logs.append(logs)
-        all_steps.append(steps)
-        ds = d_scores.astype(BF)
+        all_steps.append(nn(d_step_ref[...], pick))
+        if GROUP > 128:
+            d_score_ref[128:, :128] = jnp.zeros((GROUP - 128, 128), F32)
+        ds = d_score_ref[...].astype(BF)
         d_keys.append(d_k + nn(ds, reads))
         d_reads.append(d_r + tn(ds, keys))
+    turned = jnp.concatenate([cross_ref[...], jnp.zeros((120, cross_ref.shape[1]), F32)], axis=0).T
+    turned = pltpu.roll(turned, base, 1) if base else turned
+    all_logs = [v + turned[rows_of(c)] for c, v in enumerate(all_logs)]
 
     for j in range(PAIRS):
         at = lanes_of(j)
         grad = jnp.sum(dy_ref[0, :, at] * x_ref[0, :, at], axis=0, keepdims=True)
         gs_ref[0, :, at] = jnp.broadcast_to(grad, (8, 128))
-        d_rows, grads = conv_back(d_x[:, at], extended(xm_ref[0, :, at]), tx_ref[:, at], same)
+        d_rows, grads = conv_back(d_x[:, at], rounded(xm_ref[0, :, at]), tx_ref[:, at], same)
         d_ref[0, :, at], gx_ref[0, :, at] = d_rows, grads
 
     state2 = 2 * STATE
@@ -566,7 +595,7 @@
             whole = whole + before_ref[0, :, at]
         if last:
             main_ref = (bm_ref, cm_ref)[i]
-            d_rows, grads = conv_back(whole, extended(main_ref[0]), tb_ref[:, at], same)
+            d_rows, grads = conv_back(whole, rounded(main_ref[0]), tb_ref[:, at], same)
             d_ref[0, :, lanes_of(PAIRS + i)], gb_ref[0, :, at] = d_rows, grads
         else:
             part_ref[0, :, at] = whole
@@ -613,8 +642,8 @@
     )
 
 
-def cost(flops, size):
-    return pl.CostEstimate(flops=int(flops), bytes_accessed=int(size), transcendentals=0)
+def cost(flops, size, part=1):
+    return pl.CostEstimate(flops=int(flops) // part, bytes_accessed=int(size) // part, transcendentals=0)
 
 
 def on_device(
@@ -691,7 +720,7 @@
         out_specs=pl.BlockSpec((groups, tall, width), lambda i: (0, i, 0)),
         out_shape=shape(groups, long, width, dtype=BF),
         compiler_params=params(1),
-        cost_estimate=cost(10 * groups * rows * width, 4 * groups * rows * width),
+        cost_estimate=cost(10 * groups * rows * width, 4 * groups * rows * width, 16),
         name="input_norm",
     )(*slots, jnp.broadcast_to(gain_in, (8, width)))
     ids = jnp.concatenate([s[long : long + 1, :rows] for s in slots], axis=0)
@@ -767,7 +796,7 @@
     proj = jnp.dot(normed_rows, w_first, preferred_element_type=F32).reshape(groups, long, first_cols)
     keys_at = WIDE // 128
     if aligned:
-        gate_blocks = gather_over_b(after(gate_over_a, proj))
+        gate_blocks = gather_over_b(gate_over_a)
 
     def step_tile(t):
         return jnp.where(t == n_steps - 1, 0, LAST // WIDE + t)
@@ -801,7 +830,7 @@
         ],
         out_shape=[shape(groups, n_steps, rows, 128), shape(groups, SEG_ROW + 8, rows)],
         compiler_params=params(1),
-        cost_estimate=cost(100 * groups * rows * 128, 16 * groups * rows * 128),
+        cost_estimate=cost(100 * groups * rows * 128, 16 * groups * rows * 128, 16),
         name="token_table",
     )(proj, seg_rows, head_rows)
 
@@ -822,12 +851,12 @@
             shape(groups, rows, cols), shape(groups, rows, state2, dtype=BF), shape(groups, STATE, cols),
         ],
         compiler_params=params(),
-        cost_estimate=cost(20 * big * STATE, 8 * big),
+        cost_estimate=cost(20 * big * STATE, 8 * big, 16),
         name="conv_and_state",
     )(proj, proj, proj, taps_x, taps_b, col_table)
 
     if aligned:
-        out_blocks = gather_over_b(after(out_over_a, values_x))
+        out_blocks = gather_over_b(out_over_a)
     else:
         gate_blocks, out_blocks = gather_over_b(gate_over_a), gather_over_b(out_over_a)
 
@@ -859,7 +888,7 @@
         out_shape=shape(groups, rows, cols),
         scratch_shapes=[pltpu.VMEM((rows // GROUP, GROUP, GROUP), F32)] * 2,
         compiler_params=params(),
-        cost_estimate=cost(80 * big * GROUP, 8 * big),
+        cost_estimate=cost(80 * big * GROUP, 8 * big, 16),
         name="mix_within_block",
     )(values_x, bc, col_table, row_table, skip_l)
 
@@ -896,7 +925,7 @@
         out_shape=[shape(groups, rows, cols), shape(groups, 8, rows)],
         scratch_shapes=[pltpu.VMEM((rows, 128), F32)],
         compiler_params=params(),
-        cost_estimate=cost(2 * big * STATE, 16 * big),
+        cost_estimate=cost(2 * big * STATE, 16 * big, 16),
         name="gate",
     )(mixed_local, bc, incoming, gate_z, d_normed, gain_g, col_table)
     sums = sum_over_group(sums)
@@ -975,6 +1004,7 @@
     else:
         weights_split = [split(grad_gate_cols, in_rows), split(grad_out, out_rows)]
     by_core = normed_out.reshape(n_x, 2, rows, cols)
+    w_out = after(w_out, weights_split[0])
 
     def outward(values):
         return jnp.einsum("qtc,cd->qtd", values, w_out, preferred_element_type=F32)
@@ -1025,7 +1055,7 @@
 
         def body(*refs, t=t, first=first, last=last, used=used, n_out=len(made)):
             mix_back_kernel(
-                *refs[:used], *refs[-n_out - 1 :], base=2 * PAIRS * t, first=first, last=last
+                *refs[:used], *refs[-n_out - 6 :], base=2 * PAIRS * t, first=first, last=last
             )
 
         outs = pl.pallas_call(
@@ -1034,7 +1064,9 @@
             in_specs=[spec for _, spec in operands],
             out_specs=[spec for spec, _, _ in made],
             out_shape=[jax.ShapeDtypeStruct(s, d) for _, s, d in made],
-            scratch_shapes=[pltpu.VMEM((rows, WIDE), F32)],
+            scratch_shapes=[pltpu.VMEM((rows, WIDE), F32)]
+            + [pltpu.VMEM((GROUP, GROUP), F32)] * 3
+            + [pltpu.VMEM((GROUP, WIDE), BF), pltpu.VMEM((8, rows), F32)],
             input_output_aliases={used: 0},
             compiler_params=params(1),
             cost_estimate=cost(100 * big * GROUP, 16 * big),

time: 632 us -> 610 us (0.965)
  Pallas kernels: 193 us -> 158 us
  waiting for transfers between devices: 110 us -> 123 us
    pallas_call x2, Pallas kernels: 84.5 us -> 54.5 us  [on_device(): pl.pallas_call(body, grid=(groups,), in_specs=[spec for _, spec in operan...]
    ppermute x27, waiting for transfers between devices: 82.6 us -> 92.3 us  [shift(): return lax.ppermute(v, axis, [(i, (i + step) % n) for i in range(n)])]
    unnamed x138 -> x136, local copies, waits for them, and re-layouts: 20.2 us -> 21.4 us
  transfers between devices with their start and end apart: 50 -> 50, of which waited for: 16 -> 18; matrix products, arithmetic and copies ran while one was open for 29% -> 30% of each run, Pallas kernels for 25% -> 19%
where the time goes in v3:
time: 610 us; the launch traced here: 598 us
  Pallas kernels  158 us (26%)
  waiting for transfers between devices  123 us (20%)
  starting transfers between devices  102 us (17%)
  matrix products  98.7 us (16%)
  local copies, waits for them, and re-layouts  67.2 us (11%)
  other arithmetic  47.8 us (8%)
    ppermute x27, waiting for transfers between devices, shift(): return lax.ppermute(v, axis, [(i, (i + step) % n) for i in range(n)])  92.3 us
    pallas_call x2, Pallas kernels, on_device(): pl.pallas_call(body, grid=(groups,), in_specs=[spec for _, spec in operan...  54.5 us
    ppermute x27, starting transfers between devices, shift(): return lax.ppermute(v, axis, [(i, (i + step) % n) for i in range(n)])  37.7 us
    all_to_all x7, starting transfers between devices, exchange(): return lax.all_to_all(v, axes, 0, 0, tiled=True)  34.1 us
    dot_general x3, matrix products, grad_of(): return jnp.dot(normed_rows.T, d_rows, preferred_element_type=F32)  23.4 us
    dot_general x2, matrix products, inward(): jnp.einsum('qtc,dc->qtd', d_by, w_all, preferred_element_type=F32)  21.6 us
    unnamed x136, local copies, waits for them, and re-layouts  21.4 us
    all_to_all x7, waiting for transfers between devices, exchange(): return lax.all_to_all(v, axes, 0, 0, tiled=True)  19 us
  transfers between devices with their start and end apart: 50, of which 18 were waited for; matrix products, arithmetic and copies ran while one was open for 30% of the time, Pallas kernels for 19%

profile of v3, /device:TPU:0, one launch (start us, length us, event | category | flops | bytes accessed | tf_op | source)
XLA Modules:
  0.0 598.5 jit_solution(17703423037546758356)
XLA Ops:
  44.6 6.7 %collective-permute-done.9.refs_3_ = bf16[192,1152]{1,0:T(8,128)(2,1)S(1)} collective-permute-done((bf16[192,1152]{1,0:T(8,128)(2,1)S(1)}, bf16[192,1152]{1,0:T(8,128)(2,1)S(1)}, u32[]{:S(2)}, u32[]{:S(2)}) %collective-permute-start.9) | collective-permute-done | bytes 442400 | tf_op jit(solution)/shard_map/ppermute | solution.py:34
  53.6 16.2 %collective-permute-done.11.refs_5_ = bf16[192,1152]{1,0:T(8,128)(2,1)S(1)} collective-permute-done((bf16[192,1152]{1,0:T(8,128)(2,1)S(1)}, bf16[192,1152]{1,0:T(8,128)(2,1)S(1)}, u32[]{:S(2)}, u32[]{:S(2)}) %collective-permute-start.11) | collective-permute-done | bytes 442400 | tf_op jit(solution)/shard_map/ppermute | solution.py:34
  72.0 10.9 %collective-permute-done.12.refs_6_ = bf16[192,1152]{1,0:T(8,128)(2,1)S(1)} collective-permute-done((bf16[192,1152]{1,0:T(8,128)(2,1)S(1)}, bf16[192,1152]{1,0:T(8,128)(2,1)S(1)}, u32[]{:S(2)}, u32[]{:S(2)}) %collective-permute-start.12) | collective-permute-done | bytes 442400 | tf_op jit(solution)/shard_map/ppermute | solution.py:34
  82.9 8.7 %collective-permute-done.14.refs_8_ = bf16[192,1152]{1,0:T(8,128)(2,1)S(1)} collective-permute-done((bf16[192,1152]{1,0:T(8,128)(2,1)S(1)}, bf16[192,1152]{1,0:T(8,128)(2,1)S(1)}, u32[]{:S(2)}, u32[]{:S(2)}) %collective-permute-start.14) | collective-permute-done | bytes 442400 | tf_op jit(solution)/shard_map/ppermute | solution.py:34
  106.0 6.3 %input_norm.1.refs_9_ = bf16[4,528,1536]{2,1,0:T(8,128)(2,1)} custom-call(bf16[544,1536]{1,0:T(8,128)(2,1)S(1)} %copy-done.4, bf16[544,1536]{1,0:T(8,128)(2,1)} %collective-permute-done.6.refs_1_, bf16[544,1536]{1,0:T(8,128)(2,1)S(1)} %copy-done.9, bf16[544,1536]{1,0:T(8,128)(2,1)} %collective-permute-done.15.refs_3_, ...), custom_call_target="tpu_custom_call" | custom-call | flops 1966080 | bytes 786432 | tf_op jit(solution)/shard_map/input_norm/pallas_call | solution.py:715
  117.5 8.1 %collective-permute-start.22 = (bf16[192,768]{1,0:T(8,128)(2,1)}, bf16[192,768]{1,0:T(8,128)(2,1)}, u32[]{:S(2)}, u32[]{:S(2)}) collective-permute-start(bf16[192,768]{1,0:T(8,128)(2,1)} %in_order.31), channel_id=1, source_target_pairs={{0,2},{2,4},{4,6},{6,0},{1,3},{3,5},{5,7},{7,1},{8,10},{10,12},{12... | collective-permute-start | bytes 884744 | tf_op jit(solution)/shard_map/ppermute | solution.py:34
  137.7 14.0 %fusion.7.refs_0_.refs_1_.refs_2_.refs_8_.refs_11_.refs_12_.refs_13_ = f32[4,528,1152]{2,1,0:T(8,128)} fusion(bf16[4,528,1536]{2,1,0:T(8,128)(2,1)} %input_norm.1.refs_9_, bf16[1536,1152]{1,0:T(8,128)(2,1)} %place_weights.3.refs_1_.refs_3_), kind=kOutput, calls=%fused_computation.13 | convolution fusion | flops 7474249728 | bytes 19759104 | tf_op jit(solution)/shard_map/dot_general | solution.py:796
  156.6 16.1 %conv_and_state.1 = (f32[4,512,768]{2,1,0:T(8,128)}, bf16[4,512,256]{2,1,0:T(8,128)(2,1)S(1)}, f32[4,128,768]{2,1,0:T(8,128)S(1)}) custom-call(f32[4,528,1152]{2,1,0:T(8,128)} %fusion.7.refs_0_.refs_1_.refs_2_.refs_8_.refs_11_.refs_12_.refs_13_, f32[4,528,1152]{2,1,0:T(8,128)} %fusion.7.refs_0_.refs_1_.refs_2_.refs_8_.refs_11_.refs_12_.refs_13_, ...), custom_call_target="tpu_custom_call" | custom-call | flops 251658240 | bytes 786432 | tf_op jit(solution)/shard_map/conv_and_state/pallas_call | solution.py:842
  190.5 13.2 %mix_within_block.1.refs_4_.refs_1_.yl_ref = f32[4,512,768]{2,1,0:T(8,128)} custom-call(f32[4,512,768]{2,1,0:T(8,128)} %get-tuple-element.35.x_ref.refs_0_, bf16[4,512,256]{2,1,0:T(8,128)(2,1)S(1)} %get-tuple-element.36.bc_ref.refs_1_, f32[4,2,512,128]{3,2,1,0:T(8,128)S(1)} %get-tuple-element.34.refs_5_.ct_ref, ...), custom_call_target="tpu_custom_call" | custom-call | flops 2013265920 | bytes 786432 | tf_op jit(solution)/shard_map/mix_within_block/pallas_call | solution.py:883
  208.4 17.7 %collective-permute-done.25 = bf16[4,192,768]{2,1,0:T(8,128)(2,1)} collective-permute-done((bf16[4,192,768]{2,1,0:T(8,128)(2,1)}, bf16[4,192,768]{2,1,0:T(8,128)(2,1)}, u32[]{:S(2)}, u32[]{:S(2)}) %collective-permute-start.25) | collective-permute-done | bytes 1179680 | tf_op jit(solution)/shard_map/ppermute | solution.py:34
  230.0 19.8 %collective-permute-done.18 = bf16[4,192,768]{2,1,0:T(8,128)(2,1)} collective-permute-done((bf16[4,192,768]{2,1,0:T(8,128)(2,1)}, bf16[4,192,768]{2,1,0:T(8,128)(2,1)}, u32[]{:S(2)}, u32[]{:S(2)}) %collective-permute-start.18) | collective-permute-done | bytes 1179680 | tf_op jit(solution)/shard_map/ppermute | solution.py:34
  249.8 6.3 %place_weights.4 = bf16[1536,1920]{1,0:T(8,128)(2,1)} custom-call(s32[2]{0:T(128)} %pad_add_fusion.refs_0_, bf16[768,768]{1,0:T(8,128)(2,1)} %bitcast.20.refs_1_, bf16[768,768]{1,0:T(8,128)(2,1)} %bitcast.21.refs_2_, bf16[1536,1152]{1,0:T(8,128)(2,1)} %place_weights.3.refs_1_.refs_3_, f32[4,512,768]{2,1,0:T(8,128)} %mix_within_block.1.refs_4_.refs_1_.yl_ref), custom_call_target="tpu_custom_call" | custom-call | tf_op jit(solution)/shard_map/place_weights/pallas_call | solution.py:741
  256.1 9.9 %fusion.14.z_ref = f32[4,528,768]{2,1,0:T(8,128)} fusion(bf16[4,528,1536]{2,1,0:T(8,128)(2,1)} %input_norm.1.refs_9_, bf16[1536,1920]{1,0:T(8,128)(2,1)} %place_weights.4), kind=kOutput, calls=%fused_computation.25 | convolution fusion | flops 4982833152 | bytes 15335424 | tf_op jit(solution)/shard_map/dot_general | solution.py:914
  266.1 8.8 %fusion.17.dn_ref = f32[4,512,768]{2,1,0:T(8,128)} fusion(bf16[768,1536]{1,0:T(8,128)(2,1)S(1)} %copy-done.31, bf16[1,512,1536]{2,1,0:T(8,128)(2,1)} %bitcast.26, bf16[1,512,1536]{2,1,0:T(8,128)(2,1)} %bitcast.25, bf16[1,512,1536]{2,1,0:T(8,128)(2,1)} %bitcast.24, bf16[1,512,1536]{2,1,0:T(8,128)(2,1)} %bitcast.23), kind=kOutput, calls=%fused_computation.28 | convolution fusion | flops 4841275392 | bytes 14942208 | tf_op jit(solution)/shard_map/qtd,cd->qtc/dot_general | solution.py:916
  274.9 12.6 %gate.1 = (f32[4,512,768]{2,1,0:T(8,128)}, f32[4,8,512]{2,1,0:T(8,128)S(1)}) custom-call(f32[4,512,768]{2,1,0:T(8,128)} %mix_within_block.1.refs_4_.refs_1_.yl_ref, bf16[4,512,256]{2,1,0:T(8,128)(2,1)S(1)} %get-tuple-element.36.bc_ref.refs_1_, f32[4,128,768]{2,1,0:T(8,128)S(1)} %slice_add_fusion.1.inc_ref.refs_3_, f32[4,528,768]{2,1,0:T(8,128)} %fusion.14.z_ref, ...), custom_call_target="tpu_custom_call" | custom-call | flops 25165824 | bytes 1572864 | tf_op jit(solution)/shard_map/gate/pallas_call | solution.py:918
  290.3 9.3 %copy.78 = bf16[1536,2112]{1,0:T(8,128)(2,1)} copy(bf16[1536,2112]{0,1:T(8,128)(2,1)} %bitcast.183) | data formatting | bytes 12976128 | tf_op jit(solution)/shard_map/dot_general | solution.py:998
  299.7 16.2 %gate_back.1 = (bf16[4,512,768]{2,1,0:T(8,128)(2,1)}, f32[4,512,768]{2,1,0:T(8,128)}, bf16[4,528,1920]{2,1,0:T(8,128)(2,1)}, f32[4,128,768]{2,1,0:T(8,128)S(1)}, f32[4,8,768]{2,1,0:T(8,128)S(1)}) custom-call(f32[4,512,768]{2,1,0:T(8,128)} %get-tuple-element.39.y_ref, f32[4,528,768]{2,1,0:T(8,128)} %fusion.14.z_ref, f32[4,512,768]{2,1,0:T(8,128)} %fusion.17.dn_ref, ...), custom_call_target="tpu_custom_call" | custom-call | flops 402653184 | bytes 31457280 | tf_op jit(solution)/shard_map/gate_back/pallas_call | solution.py:934
  321.8 7.2 %fusion.40.v_ref = f32[4,8,48,768]{3,2,1,0:T(8,128)} fusion(bf16[4,8,48,2112]{3,2,1,0:T(8,128)(2,1)S(1)} %bitcast.189, bf16[2112,768,1,1]{1,0,3,2:T(8,128)(2,1)S(1)} %bitcast.197), kind=kOutput, calls=%fused_computation.115 | convolution fusion | flops 4982833152 | bytes 14450688 | tf_op jit(solution)/shard_map/dot_general | solution.py:998
  329.1 8.7 %fusion.21 = f32[768,1536,1]{1,0,2:T(8,128)} fusion(bf16[4,512,768]{2,1,0:T(8,128)(2,1)S(1)} %copy-done.60, bf16[1,512,1536]{2,1,0:T(8,128)(2,1)} %bitcast.26, bf16[1,512,1536]{2,1,0:T(8,128)(2,1)} %bitcast.25, bf16[1,512,1536]{2,1,0:T(8,128)(2,1)} %bitcast.24, bf16[1,512,1536]{2,1,0:T(8,128)(2,1)} %bitcast.23), kind=kOutput, calls=%fused_computation.43 | convolution fusion | flops 4841275392 | bytes 14155776 | tf_op jit(solution)/shard_map/qtc,qtd->cd/dot_general | solution.py:1000
  337.8 6.4 %split_gradients.1 = bf16[8,192,1536]{2,1,0:T(8,128)(2,1)S(1)} custom-call(s32[8]{0:T(128)S(1)} %stack.176.at_ref, f32[4,8,48,768]{3,2,1,0:T(8,128)} %fusion.40.v_ref, f32[1,8,96,1536]{3,2,1,0:T(8,128)} %bitcast.190), custom_call_target="tpu_custom_call" | custom-call | flops 2359296 | bytes 14155776 | tf_op jit(solution)/shard_map/split_gradients/pallas_call | solution.py:977
  351.1 6.4 %convolution_convert_fusion = bf16[2,512,1536]{2,1,0:T(8,128)(2,1)} fusion(bf16[768,1536]{1,0:T(8,128)(2,1)} %in_order.32, bf16[2,2,512,768]{3,2,1,0:T(8,128)(2,1)} %bitcast.211), kind=kOutput, calls=%fused_computation.12 | convolution fusion | flops 2417491968 | bytes 7077888 | tf_op jit(solution)/shard_map/qtc,cd->qtd/dot_general | solution.py:1010
  362.8 24.9 %mix_back.2 = (bf16[4,528,1920]{2,1,0:T(8,128)(2,1)}, f32[4,8,384]{2,1,0:T(8,128)S(1)}, f32[4,8,384]{2,1,0:T(8,128)S(1)}, f32[4,512,512]{2,1,0:T(8,128)}) custom-call(f32[4,512,768]{2,1,0:T(8,128)} %get-tuple-element.35.x_ref.refs_0_, bf16[4,512,256]{2,1,0:T(8,128)(2,1)S(1)} %get-tuple-element.36.bc_ref.refs_1_, ...), custom_call_target="tpu_custom_call", output_to_operand_aliasing={{0}: (10, {})} | custom-call | flops 40265318400 | bytes 25165824 | tf_op jit(solution)/shard_map/mix_back/pallas_call | solution.py:1061
  389.5 5.9 fusion.41.v_ref
  407.2 9.4 %all-to-all-start.2 = ((bf16[4,192,1536]{2,1,0:T(8,128)(2,1)}), bf16[4,192,1536]{2,1,0:T(8,128)(2,1)}, u32[]{:S(2)}, u32[]{:S(2)}) async-start(bf16[4,192,1536]{2,1,0:T(8,128)(2,1)} %add_convert_fusion.refs_18_), calls=%async_computation.2 | async-start | bytes 4718592 | tf_op jit(solution)/shard_map/all_to_all | solution.py:44
  416.6 5.7 convert_add_fusion.1
  426.1 29.5 %mix_back.3 = (bf16[4,528,1920]{2,1,0:T(8,128)(2,1)}, f32[4,8,384]{2,1,0:T(8,128)S(1)}, f32[4,8,384]{2,1,0:T(8,128)S(1)}, f32[4,8,256]{2,1,0:T(8,128)S(1)}, f32[4,8,128]{2,1,0:T(8,128)S(1)}) custom-call(f32[4,512,768]{2,1,0:T(8,128)} %get-tuple-element.35.x_ref.refs_0_, ...), custom_call_target="tpu_custom_call", output_to_operand_aliasing={{0}: (16, {})} | custom-call | flops 40265318400 | bytes 25165824 | tf_op jit(solution)/shard_map/mix_back/pallas_call | solution.py:1061
  474.2 10.3 %fusion.9 = f32[1536,768,1]{1,0,2:T(8,128)} fusion(bf16[4,528,1536]{2,1,0:T(8,128)(2,1)} %input_norm.1.refs_9_, bf16[4,528,1920]{2,1,0:T(8,128)(2,1)} %in_order.33.refs_0_), kind=kOutput, calls=%fused_computation.17 | convolution fusion | flops 4982833152 | bytes 14450688 | tf_op jit(solution)/shard_map/dot_general | solution.py:998
  491.6 5.3 split_gradient.3
  510.4 11.4 %fusion.4.refs_0_.refs_1_ = bf16[2,528,1536]{2,1,0:T(8,128)(2,1)} fusion(bf16[1536,1920]{1,0:T(8,128)(2,1)} %place_weights.4, bf16[2,2,528,1920]{3,2,1,0:T(8,128)(2,1)} %bitcast.181), kind=kOutput, calls=%fused_computation.11 | convolution fusion | flops 6230163456 | bytes 13197312 | tf_op jit(solution)/shard_map/qtc,dc->qtd/dot_general | solution.py:1120
  528.8 10.2 %fusion.2.refs_1_ = f32[2,528,1536]{2,1,0:T(8,128)S(1)} fusion(bf16[1536,1920]{1,0:T(8,128)(2,1)} %place_weights.4, bf16[2,2,528,1920]{3,2,1,0:T(8,128)(2,1)} %bitcast.182), kind=kOutput, calls=%fused_computation.5 | convolution fusion | flops 6228541440 | bytes 16441344 | tf_op jit(solution)/shard_map/qtc,dc->qtd/dot_general | solution.py:1120
  545.9 5.5 all-to-all-start.5
  565.8 14.9 %all-to-all-done.5 = bf16[4,4,48,768]{3,2,1,0:T(8,128)(2,1)} async-done(((bf16[4,4,48,768]{3,2,1,0:T(8,128)(2,1)}), bf16[4,4,48,768]{3,2,1,0:T(8,128)(2,1)}, u32[]{:S(2)}, u32[]{:S(2)}) %all-to-all-start.5) | async-done | bytes 1179680 | tf_op jit(solution)/shard_map/all_to_all | solution.py:44
  (417 shorter events, 233.6 us)
Async XLA Ops:
  2.7 27.0 %all-to-all-start = ((bf16[4,48,1920]{2,1,0:T(8,128)(2,1)}), bf16[4,48,1920]{2,1,0:T(8,128)(2,1)S(1)}, u32[]{:S(2)}, u32[]{:S(2)}) async-start(bf16[4,48,1920]{2,1,0:T(8,128)(2,1)} %pack_weights.1.refs_1_), calls=%async_computation | async-start | bytes 1474560 | tf_op jit(solution)/shard_map/all_to_all | solution.py:44
  33.4 59.0 %collective-permute-start.7 = (bf16[544,1536]{1,0:T(8,128)(2,1)}, bf16[544,1536]{1,0:T(8,128)(2,1)S(1)}, u32[]{:S(2)}, u32[]{:S(2)}) collective-permute-start(bf16[544,1536]{1,0:T(8,128)(2,1)} %in_order.26.refs_0_), channel_id=1, source_target_pairs={{0,16},{16,0},{1,17},{17,1},{2,18},{18,2},{3,19},{19,3},{4,20},{20... | collective-permute-start | bytes 5013512 | tf_op jit(solution)/shard_map/ppermute | solution.py:34
  37.8 32.0 %collective-permute-start.11 = (bf16[192,1152]{1,0:T(8,128)(2,1)S(1)}, bf16[192,1152]{1,0:T(8,128)(2,1)S(1)}, u32[]{:S(2)}, u32[]{:S(2)}) collective-permute-start(bf16[192,1152]{1,0:T(8,128)(2,1)S(1)} %bitcast.192), channel_id=1, source_target_pairs={{0,4},{2,6},{4,0},{6,2},{1,5},{3,7},{5,1},{7,3},{8,12},{10,14},{12... | collective-permute-start | bytes 1327112 | tf_op jit(solution)/shard_map/ppermute | solution.py:34
  40.8 31.0 %collective-permute-start.13 = (bf16[192,1152]{1,0:T(8,128)(2,1)S(1)}, bf16[192,1152]{1,0:T(8,128)(2,1)S(1)}, u32[]{:S(2)}, u32[]{:S(2)}) collective-permute-start(bf16[192,1152]{1,0:T(8,128)(2,1)S(1)} %bitcast.193), channel_id=1, source_target_pairs={{0,6},{2,0},{4,2},{6,4},{1,7},{3,1},{5,3},{7,5},{8,14},{10,8},{12,... | collective-permute-start | bytes 1327112 | tf_op jit(solution)/shard_map/ppermute | solution.py:34
  41.8 30.1 %collective-permute-start.8 = (bf16[192,1152]{1,0:T(8,128)(2,1)S(1)}, bf16[192,1152]{1,0:T(8,128)(2,1)S(1)}, u32[]{:S(2)}, u32[]{:S(2)}) collective-permute-start(bf16[192,1152]{1,0:T(8,128)(2,1)S(1)} %bitcast.194), channel_id=1, source_target_pairs={{0,1},{1,0},{2,3},{3,2},{4,5},{5,4},{6,7},{7,6},{8,9},{9,8},{10,11... | collective-permute-start | bytes 1327112 | tf_op jit(solution)/shard_map/ppermute | solution.py:34
  51.3 20.6 %collective-permute-start.10 = (bf16[192,1152]{1,0:T(8,128)(2,1)S(1)}, bf16[192,1152]{1,0:T(8,128)(2,1)S(1)}, u32[]{:S(2)}, u32[]{:S(2)}) collective-permute-start(bf16[192,1152]{1,0:T(8,128)(2,1)S(1)} %collective-permute-done.9.refs_3_), channel_id=1, source_target_pairs={{0,1},{1,0},{2,3},{3,2},{4,5},{5,4},{6,7},{7,6},{8,9},{9,8},{10,11... | collective-permute-start | bytes 1327112 | tf_op jit(solution)/shard_map/ppermute | solution.py:34
  71.9 32.6 %collective-permute-start.6 = (bf16[544,1536]{1,0:T(8,128)(2,1)}, bf16[544,1536]{1,0:T(8,128)(2,1)}, u32[]{:S(2)}, u32[]{:S(2)}) collective-permute-start(bf16[544,1536]{1,0:T(8,128)(2,1)} %in_order.26.refs_0_), channel_id=1, source_target_pairs={{0,8},{8,0},{1,9},{9,1},{2,10},{10,2},{3,11},{11,3},{4,12},{12,4},... | collective-permute-start | bytes 5013512 | tf_op jit(solution)/shard_map/ppermute | solution.py:34
  117.5 63.8 %collective-permute-start.22 = (bf16[192,768]{1,0:T(8,128)(2,1)}, bf16[192,768]{1,0:T(8,128)(2,1)}, u32[]{:S(2)}, u32[]{:S(2)}) collective-permute-start(bf16[192,768]{1,0:T(8,128)(2,1)} %in_order.31), channel_id=1, source_target_pairs={{0,2},{2,4},{4,6},{6,0},{1,3},{3,5},{5,7},{7,1},{8,10},{10,12},{12... | collective-permute-start | bytes 884744 | tf_op jit(solution)/shard_map/ppermute | solution.py:34
  125.6 60.2 %collective-permute-start.23 = (bf16[192,768]{1,0:T(8,128)(2,1)}, bf16[192,768]{1,0:T(8,128)(2,1)}, u32[]{:S(2)}, u32[]{:S(2)}) collective-permute-start(bf16[192,768]{1,0:T(8,128)(2,1)} %in_order.31), channel_id=1, source_target_pairs={{0,4},{2,6},{4,0},{6,2},{1,5},{3,7},{5,1},{7,3},{8,12},{10,14},{12... | collective-permute-start | bytes 884744 | tf_op jit(solution)/shard_map/ppermute | solution.py:34
  129.0 56.8 %collective-permute-start.24 = (bf16[192,768]{1,0:T(8,128)(2,1)}, bf16[192,768]{1,0:T(8,128)(2,1)}, u32[]{:S(2)}, u32[]{:S(2)}) collective-permute-start(bf16[192,768]{1,0:T(8,128)(2,1)} %in_order.31), channel_id=1, source_target_pairs={{0,6},{2,0},{4,2},{6,4},{1,7},{3,1},{5,3},{7,5},{8,14},{10,8},{12,... | collective-permute-start | bytes 884744 | tf_op jit(solution)/shard_map/ppermute | solution.py:34
  130.8 72.9 %collective-permute-start.20 = (bf16[512,1536]{1,0:T(8,128)(2,1)}, bf16[512,1536]{1,0:T(8,128)(2,1)}, u32[]{:S(2)}, u32[]{:S(2)}) collective-permute-start(bf16[512,1536]{1,0:T(8,128)(2,1)} %in_order.29), channel_id=1, source_target_pairs={{0,16},{16,0},{1,17},{17,1},{2,18},{18,2},{3,19},{19,3},{4,20},{20... | collective-permute-start | bytes 4718600 | tf_op jit(solution)/shard_map/ppermute | solution.py:34
  133.4 55.9 %all-to-all-start.1 = ((bf16[4,192,768]{2,1,0:T(8,128)(2,1)}), bf16[4,192,768]{2,1,0:T(8,128)(2,1)}, u32[]{:S(2)}, u32[]{:S(2)}) async-start(bf16[4,192,768]{2,1,0:T(8,128)(2,1)} %broadcast_in_dim.84), calls=%async_computation.1 | async-start | bytes 2359296 | tf_op jit(solution)/shard_map/all_to_all | solution.py:44
  176.8 26.8 %collective-permute-start.16 = (bf16[4,144,768]{2,1,0:T(8,128)(2,1)}, bf16[4,144,768]{2,1,0:T(8,128)(2,1)}, u32[]{:S(2)}, u32[]{:S(2)}) collective-permute-start(bf16[4,144,768]{2,1,0:T(8,128)(2,1)} %pad_maximum_fusion.3), channel_id=1, source_target_pairs={{0,1},{1,2},{2,3},{3,4},{4,5},{5,6},{6,7},{8,9},{9,10},{10,11},{11... | collective-permute-start | bytes 2654216 | tf_op jit(solution)/shard_map/ppermute | solution.py:40
  181.4 25.7 %collective-permute-start.17 = (bf16[4,144,768]{2,1,0:T(8,128)(2,1)}, bf16[4,144,768]{2,1,0:T(8,128)(2,1)}, u32[]{:S(2)}, u32[]{:S(2)}) collective-permute-start(bf16[4,144,768]{2,1,0:T(8,128)(2,1)} %pad_maximum_fusion.3), channel_id=1, source_target_pairs={{0,2},{1,3},{2,4},{3,5},{4,6},{5,7},{8,10},{9,11},{10,12},{11,13},... | collective-permute-start | bytes 2654216 | tf_op jit(solution)/shard_map/ppermute | solution.py:40
  188.2 37.9 %collective-permute-start.25 = (bf16[4,192,768]{2,1,0:T(8,128)(2,1)}, bf16[4,192,768]{2,1,0:T(8,128)(2,1)}, u32[]{:S(2)}, u32[]{:S(2)}) collective-permute-start(bf16[4,192,768]{2,1,0:T(8,128)(2,1)} %pad_maximum_fusion.4), channel_id=1, source_target_pairs={{0,1},{1,0},{2,3},{3,2},{4,5},{5,4},{6,7},{7,6},{8,9},{9,8},{10,11... | collective-permute-start | bytes 3538952 | tf_op jit(solution)/shard_map/ppermute | solution.py:34
  189.3 60.5 %collective-permute-start.18 = (bf16[4,192,768]{2,1,0:T(8,128)(2,1)}, bf16[4,192,768]{2,1,0:T(8,128)(2,1)}, u32[]{:S(2)}, u32[]{:S(2)}) collective-permute-start(bf16[4,192,768]{2,1,0:T(8,128)(2,1)} %all-to-all-done.1), channel_id=1, source_target_pairs={{0,1},{1,0},{2,3},{3,2},{4,5},{5,4},{6,7},{7,6},{8,9},{9,8},{10,11... | collective-permute-start | bytes 3538952 | tf_op jit(solution)/shard_map/ppermute | solution.py:34
  203.6 62.4 %collective-permute-start.19 = (bf16[512,1536]{1,0:T(8,128)(2,1)}, bf16[512,1536]{1,0:T(8,128)(2,1)}, u32[]{:S(2)}, u32[]{:S(2)}) collective-permute-start(bf16[512,1536]{1,0:T(8,128)(2,1)} %in_order.29), channel_id=1, source_target_pairs={{0,8},{8,0},{1,9},{9,1},{2,10},{10,2},{3,11},{11,3},{4,12},{12,4},... | collective-permute-start | bytes 4718600 | tf_op jit(solution)/shard_map/ppermute | solution.py:34
  203.6 62.4 %collective-permute-start.21 = (bf16[512,1536]{1,0:T(8,128)(2,1)}, bf16[512,1536]{1,0:T(8,128)(2,1)}, u32[]{:S(2)}, u32[]{:S(2)}) collective-permute-start(bf16[512,1536]{1,0:T(8,128)(2,1)} %in_order.30), channel_id=1, source_target_pairs={{0,8},{8,0},{1,9},{9,1},{2,10},{10,2},{3,11},{11,3},{4,12},{12,4},... | collective-permute-start | bytes 4718600 | tf_op jit(solution)/shard_map/ppermute | solution.py:34
  316.9 40.9 %collective-permute-start.30 = (bf16[4,144,768]{2,1,0:T(8,128)(2,1)}, bf16[4,144,768]{2,1,0:T(8,128)(2,1)S(1)}, u32[]{:S(2)}, u32[]{:S(2)}) collective-permute-start(bf16[4,144,768]{2,1,0:T(8,128)(2,1)} %pad_maximum_fusion.2), channel_id=1, source_target_pairs={{1,0},{2,1},{3,2},{4,3},{5,4},{6,5},{7,6},{9,8},{10,9},{11,10},{12... | collective-permute-start | bytes 2654216 | tf_op jit(solution)/shard_map/ppermute | solution.py:40
  318.2 43.2 %collective-permute-start.31 = (bf16[4,144,768]{2,1,0:T(8,128)(2,1)}, bf16[4,144,768]{2,1,0:T(8,128)(2,1)}, u32[]{:S(2)}, u32[]{:S(2)}) collective-permute-start(bf16[4,144,768]{2,1,0:T(8,128)(2,1)} %pad_maximum_fusion.2), channel_id=1, source_target_pairs={{2,0},{3,1},{4,2},{5,3},{6,4},{7,5},{10,8},{11,9},{12,10},{13,11},... | collective-permute-start | bytes 2654216 | tf_op jit(solution)/shard_map/ppermute | solution.py:40
  348.0 55.5 %collective-permute-start.32 = (bf16[4,192,1536]{2,1,0:T(8,128)(2,1)}, bf16[4,192,1536]{2,1,0:T(8,128)(2,1)}, u32[]{:S(2)}, u32[]{:S(2)}) collective-permute-start(bf16[4,192,1536]{2,1,0:T(8,128)(2,1)} %slice.367), channel_id=1, source_target_pairs={{0,1},{1,0},{2,3},{3,2},{4,5},{5,4},{6,7},{7,6},{8,9},{9,8},{10,11... | collective-permute-start | bytes 7077896 | tf_op jit(solution)/shard_map/ppermute | solution.py:34
  357.5 59.1 %collective-permute-start.28 = (bf16[2,512,1536]{2,1,0:T(8,128)(2,1)}, bf16[2,512,1536]{2,1,0:T(8,128)(2,1)}, u32[]{:S(2)}, u32[]{:S(2)}) collective-permute-start(bf16[2,512,1536]{2,1,0:T(8,128)(2,1)} %convolution_convert_fusion), channel_id=1, source_target_pairs={{0,8},{8,0},{1,9},{9,1},{2,10},{10,2},{3,11},{11,3},{4,12},{12,4},... | collective-permute-start | bytes 9437192 | tf_op jit(solution)/shard_map/ppermute | solution.py:34
  398.6 58.3 %collective-permute-start.34 = (bf16[4,4,48,384]{3,2,1,0:T(8,128)(2,1)}, bf16[4,4,48,384]{3,2,1,0:T(8,128)(2,1)}, u32[]{:S(2)}, u32[]{:S(2)}) collective-permute-start(bf16[4,4,48,384]{3,2,1,0:T(8,128)(2,1)} %get-tuple-element.63), channel_id=1, source_target_pairs={{0,1},{1,0},{2,3},{3,2},{4,5},{5,4},{6,7},{7,6},{8,9},{9,8},{10,11... | collective-permute-start | bytes 1769480 | tf_op jit(solution)/shard_map/ppermute | solution.py:34
  407.2 60.2 %all-to-all-start.2 = ((bf16[4,192,1536]{2,1,0:T(8,128)(2,1)}), bf16[4,192,1536]{2,1,0:T(8,128)(2,1)}, u32[]{:S(2)}, u32[]{:S(2)}) async-start(bf16[4,192,1536]{2,1,0:T(8,128)(2,1)} %add_convert_fusion.refs_18_), calls=%async_computation.2 | async-start | bytes 4718592 | tf_op jit(solution)/shard_map/all_to_all | solution.py:44
  423.7 35.5 %collective-permute-start.29 = (bf16[512,1536]{1,0:T(8,128)(2,1)}, bf16[512,1536]{1,0:T(8,128)(2,1)}, u32[]{:S(2)}, u32[]{:S(2)}) collective-permute-start(bf16[512,1536]{1,0:T(8,128)(2,1)} %fusion.20.refs_19_), channel_id=1, source_target_pairs={{0,16},{16,0},{1,17},{17,1},{2,18},{18,2},{3,19},{19,3},{4,20},{20... | collective-permute-start | bytes 4718600 | tf_op jit(solution)/shard_map/ppermute | solution.py:34
  456.2 28.3 %collective-permute-start.38 = (f32[160,128]{1,0:T(8,128)S(1)}, f32[160,128]{1,0:T(8,128)S(1)}, u32[]{:S(2)}, u32[]{:S(2)}) collective-permute-start(f32[160,128]{1,0:T(8,128)S(1)} %fusion.23.refs_0_), channel_id=1, source_target_pairs={{0,16},{16,0},{1,17},{17,1},{2,18},{18,2},{3,19},{19,3},{4,20},{20... | collective-permute-start | bytes 245768 | tf_op jit(solution)/shard_map/ppermute | solution.py:131
  470.5 33.5 %all-to-all-start.3 = ((bf16[4,4,48,384]{3,2,1,0:T(8,128)(2,1)}), bf16[4,4,48,384]{3,2,1,0:T(8,128)(2,1)S(1)}, u32[]{:S(2)}, u32[]{:S(2)}) async-start(bf16[4,4,48,384]{3,2,1,0:T(8,128)(2,1)} %in_order.35), calls=%async_computation.3 | async-start | bytes 1179648 | tf_op jit(solution)/shard_map/all_to_all | solution.py:44
  498.1 27.3 %collective-permute-start.35 = (bf16[4,4,48,768]{3,2,1,0:T(8,128)(2,1)}, bf16[4,4,48,768]{3,2,1,0:T(8,128)(2,1)}, u32[]{:S(2)}, u32[]{:S(2)}) collective-permute-start(bf16[4,4,48,768]{3,2,1,0:T(8,128)(2,1)} %slice.376), channel_id=1, source_target_pairs={{0,1},{1,0},{2,3},{3,2},{4,5},{5,4},{6,7},{7,6},{8,9},{9,8},{10,11... | collective-permute-start | bytes 3538952 | tf_op jit(solution)/shard_map/ppermute | solution.py:34
  501.6 20.2 %collective-permute-start.40 = (f32[160,128]{1,0:T(8,128)S(1)}, f32[160,128]{1,0:T(8,128)S(1)}, u32[]{:S(2)}, u32[]{:S(2)}) collective-permute-start(f32[160,128]{1,0:T(8,128)S(1)} %add.259.refs_0_), channel_id=1, source_target_pairs={{0,4},{2,6},{4,0},{6,2},{1,5},{3,7},{5,1},{7,3},{8,12},{10,14},{12... | collective-permute-start | bytes 245768 | tf_op jit(solution)/shard_map/ppermute | solution.py:131
  505.0 23.0 %all-to-all-start.4 = ((bf16[4,48,1152]{2,1,0:T(8,128)(2,1)}), bf16[4,48,1152]{2,1,0:T(8,128)(2,1)S(1)}, u32[]{:S(2)}, u32[]{:S(2)}) async-start(bf16[4,48,1152]{2,1,0:T(8,128)(2,1)} %pad_maximum_fusion.8), calls=%async_computation.4 | async-start | bytes 884736 | tf_op jit(solution)/shard_map/all_to_all | solution.py:44
  545.9 34.8 %all-to-all-start.5 = ((bf16[4,4,48,768]{3,2,1,0:T(8,128)(2,1)}), bf16[4,4,48,768]{3,2,1,0:T(8,128)(2,1)}, u32[]{:S(2)}, u32[]{:S(2)}) async-start(bf16[4,4,48,768]{3,2,1,0:T(8,128)(2,1)} %in_order.38), calls=%async_computation.5 | async-start | bytes 2359296 | tf_op jit(solution)/shard_map/all_to_all | solution.py:44
  551.3 37.9 %collective-permute-start.37 = (bf16[528,1536]{1,0:T(8,128)(2,1)}, bf16[528,1536]{1,0:T(8,128)(2,1)}, u32[]{:S(2)}, u32[]{:S(2)}) collective-permute-start(bf16[528,1536]{1,0:T(8,128)(2,1)} %fusion.19.refs_2_), channel_id=1, source_target_pairs={{0,16},{16,0},{1,17},{17,1},{2,18},{18,2},{3,19},{19,3},{4,20},{20... | collective-permute-start | bytes 4866056 | tf_op jit(solution)/shard_map/ppermute | solution.py:34
  (85 other events, 1140.0 us)

commit v4 on v3

--- a/solution.py
+++ b/solution.py
@@ -788,15 +788,13 @@
     gate_block = held[:, :, first_cols:].reshape(-1, cols)
     if aligned:
         out_block = jnp.concatenate([out_proj[:, :cols], out_proj[:, cols:]], axis=0)
-        gate_over_a = gather_over_a(after(gate_block, w_first))
+        gate_over_a = gather_over_a(after(gate_block, *first_blocks))
     else:
         gate_over_a, out_over_a = gather_over_a(gate_block), gather_over_a(out_proj)
 
     normed_rows = normed.reshape(groups * long, width)
     proj = jnp.dot(normed_rows, w_first, preferred_element_type=F32).reshape(groups, long, first_cols)
     keys_at = WIDE // 128
-    if aligned:
-        gate_blocks = gather_over_b(gate_over_a)
 
     def step_tile(t):
         return jnp.where(t == n_steps - 1, 0, LAST // WIDE + t)
@@ -835,8 +833,9 @@
     )(proj, seg_rows, head_rows)
 
     if aligned:
-        out_block = after(out_block, w_first)
-        out_over_a = jnp.stack([out_block] + [shift(out_block, "a", sa) for sa in range(1, na)])
+        out_block = after(out_block, *first_blocks)
+        out_over_a = [shift(out_block, "a", sa) for sa in range(1, na)]
+        out_over_a = jnp.stack([out_block] + [after(v, col_table) for v in out_over_a])
     grid = (groups, n_steps)
     big = groups * rows * cols
     values_x, bc, own_state = pl.pallas_call(
@@ -857,6 +856,7 @@
 
     if aligned:
         out_blocks = gather_over_b(out_over_a)
+        gate_blocks = gather_over_b(after(gate_over_a, col_table))
     else:
         gate_blocks, out_blocks = gather_over_b(gate_over_a), gather_over_b(out_over_a)
 
@@ -881,16 +881,18 @@
     incoming = entering(own_state, 1)
 
     mixed_local = pl.pallas_call(
-        mix_kernel,
+        lambda *refs: mix_kernel(*refs[:5], *refs[6:]),
         grid=grid,
-        in_specs=[tile(rows), per_seq(rows, state2), by_step, per_seq(SEG_ROW + 8, rows), lanes(8)],
+        in_specs=[
+            tile(rows), per_seq(rows, state2), by_step, per_seq(SEG_ROW + 8, rows), lanes(8), anywhere,
+        ],
         out_specs=tile(rows),
         out_shape=shape(groups, rows, cols),
         scratch_shapes=[pltpu.VMEM((rows // GROUP, GROUP, GROUP), F32)] * 2,
         compiler_params=params(),
         cost_estimate=cost(80 * big * GROUP, 8 * big, 16),
         name="mix_within_block",
-    )(values_x, bc, col_table, row_table, skip_l)
+    )(values_x, bc, col_table, row_table, skip_l, out_blocks[-1])
 
     if aligned:
         many = groups * in_rows

time: 610 us -> 586 us (0.961)
  waiting for transfers between devices: 123 us -> 100 us
    ppermute x27, waiting for transfers between devices: 92.3 us -> 71.2 us  [shift(): return lax.ppermute(v, axis, [(i, (i + step) % n) for i in range(n)])]
    unnamed x136 -> x150, local copies, waits for them, and re-layouts: 21.4 us -> 22.7 us
  transfers between devices with their start and end apart: 50 -> 50, of which waited for: 18 -> 18; matrix products, arithmetic and copies ran while one was open for 30% -> 31% of each run, Pallas kernels for 19% -> 22%
where the time goes in v4:
time: 586 us; the launch traced here: 574 us
  Pallas kernels  158 us (27%)
  starting transfers between devices  104 us (18%)
  waiting for transfers between devices  100 us (17%)
  matrix products  97.3 us (17%)
  local copies, waits for them, and re-layouts  65.8 us (11%)
  other arithmetic  46.9 us (8%)
    ppermute x27, waiting for transfers between devices, shift(): return lax.ppermute(v, axis, [(i, (i + step) % n) for i in range(n)])  71.2 us
    pallas_call x2, Pallas kernels, on_device(): pl.pallas_call(body, grid=(groups,), in_specs=[spec for _, spec in operan...  54.4 us
    ppermute x27, starting transfers between devices, shift(): return lax.ppermute(v, axis, [(i, (i + step) % n) for i in range(n)])  40.3 us
    all_to_all x7, starting transfers between devices, exchange(): return lax.all_to_all(v, axes, 0, 0, tiled=True)  33.3 us
    dot_general x3, matrix products, grad_of(): return jnp.dot(normed_rows.T, d_rows, preferred_element_type=F32)  23.5 us
    unnamed x150, local copies, waits for them, and re-layouts  22.7 us
    dot_general x2, matrix products, inward(): jnp.einsum('qtc,dc->qtd', d_by, w_all, preferred_element_type=F32)  21.7 us
    all_to_all x7, waiting for transfers between devices, exchange(): return lax.all_to_all(v, axes, 0, 0, tiled=True)  17.2 us
  transfers between devices with their start and end apart: 50, of which 18 were waited for; matrix products, arithmetic and copies ran while one was open for 31% of the time, Pallas kernels for 22%

profile of v4, /device:TPU:0, one launch (start us, length us, event | category | flops | bytes accessed | tf_op | source)
XLA Modules:
  0.0 574.3 jit_solution(16223177570082373325)
XLA Ops:
  44.6 6.7 %collective-permute-done.9.refs_3_ = bf16[192,1152]{1,0:T(8,128)(2,1)S(1)} collective-permute-done((bf16[192,1152]{1,0:T(8,128)(2,1)S(1)}, bf16[192,1152]{1,0:T(8,128)(2,1)S(1)}, u32[]{:S(2)}, u32[]{:S(2)}) %collective-permute-start.9) | collective-permute-done | bytes 442400 | tf_op jit(solution)/shard_map/ppermute | solution.py:34
  53.6 16.2 %collective-permute-done.11.refs_5_ = bf16[192,1152]{1,0:T(8,128)(2,1)S(1)} collective-permute-done((bf16[192,1152]{1,0:T(8,128)(2,1)S(1)}, bf16[192,1152]{1,0:T(8,128)(2,1)S(1)}, u32[]{:S(2)}, u32[]{:S(2)}) %collective-permute-start.11) | collective-permute-done | bytes 442400 | tf_op jit(solution)/shard_map/ppermute | solution.py:34
  72.0 10.9 %collective-permute-done.12.refs_6_ = bf16[192,1152]{1,0:T(8,128)(2,1)S(1)} collective-permute-done((bf16[192,1152]{1,0:T(8,128)(2,1)S(1)}, bf16[192,1152]{1,0:T(8,128)(2,1)S(1)}, u32[]{:S(2)}, u32[]{:S(2)}) %collective-permute-start.12) | collective-permute-done | bytes 442400 | tf_op jit(solution)/shard_map/ppermute | solution.py:34
  82.9 8.7 %collective-permute-done.14.refs_8_ = bf16[192,1152]{1,0:T(8,128)(2,1)S(1)} collective-permute-done((bf16[192,1152]{1,0:T(8,128)(2,1)S(1)}, bf16[192,1152]{1,0:T(8,128)(2,1)S(1)}, u32[]{:S(2)}, u32[]{:S(2)}) %collective-permute-start.14) | collective-permute-done | bytes 442400 | tf_op jit(solution)/shard_map/ppermute | solution.py:34
  100.5 8.1 %collective-permute-start.16 = (bf16[192,768]{1,0:T(8,128)(2,1)}, bf16[192,768]{1,0:T(8,128)(2,1)}, u32[]{:S(2)}, u32[]{:S(2)}) collective-permute-start(bf16[192,768]{1,0:T(8,128)(2,1)} %in_order.32), channel_id=1, source_target_pairs={{0,2},{2,4},{4,6},{6,0},{1,3},{3,5},{5,7},{7,1},{8,10},{10,12},{12... | collective-permute-start | bytes 884744 | tf_op jit(solution)/shard_map/ppermute | solution.py:34
  121.8 6.3 %input_norm.1.refs_9_ = bf16[4,528,1536]{2,1,0:T(8,128)(2,1)} custom-call(bf16[544,1536]{1,0:T(8,128)(2,1)S(1)} %copy-done.6, bf16[544,1536]{1,0:T(8,128)(2,1)} %collective-permute-done.6.refs_1_, bf16[544,1536]{1,0:T(8,128)(2,1)S(1)} %copy-done.11, bf16[544,1536]{1,0:T(8,128)(2,1)} %collective-permute-done.15.refs_3_, ...), custom_call_target="tpu_custom_call" | custom-call | flops 1966080 | bytes 786432 | tf_op jit(solution)/shard_map/input_norm/pallas_call | solution.py:715
  128.7 5.1 place_weights.3.refs_3_.refs_1_
  133.8 13.1 %fusion.7.refs_0_.refs_1_.refs_2_.refs_8_.refs_11_.refs_12_.refs_13_ = f32[4,528,1152]{2,1,0:T(8,128)} fusion(bf16[4,528,1536]{2,1,0:T(8,128)(2,1)S(1)} %copy-done.30, bf16[1536,1152]{1,0:T(8,128)(2,1)} %place_weights.3.refs_3_.refs_1_), kind=kOutput, calls=%fused_computation.13 | convolution fusion | flops 7474249728 | bytes 19759104 | tf_op jit(solution)/shard_map/dot_general | solution.py:796
  158.6 15.4 %conv_and_state.1 = (f32[4,512,768]{2,1,0:T(8,128)}, bf16[4,512,256]{2,1,0:T(8,128)(2,1)S(1)}, f32[4,128,768]{2,1,0:T(8,128)S(1)}) custom-call(f32[4,528,1152]{2,1,0:T(8,128)} %fusion.7.refs_0_.refs_1_.refs_2_.refs_8_.refs_11_.refs_12_.refs_13_, f32[4,528,1152]{2,1,0:T(8,128)} %fusion.7.refs_0_.refs_1_.refs_2_.refs_8_.refs_11_.refs_12_.refs_13_, ...), custom_call_target="tpu_custom_call" | custom-call | flops 251658240 | bytes 786432 | tf_op jit(solution)/shard_map/conv_and_state/pallas_call | solution.py:841
  188.6 13.1 %mix_within_block.1.refs_4_.refs_1_.yl_ref = f32[4,512,768]{2,1,0:T(8,128)} custom-call(f32[4,512,768]{2,1,0:T(8,128)} %get-tuple-element.35.refs_0_, bf16[4,512,256]{2,1,0:T(8,128)(2,1)S(1)} %get-tuple-element.36.refs_1_.bc_ref, f32[4,2,512,128]{3,2,1,0:T(8,128)S(1)} %copy-done.2, f32[4,24,512]{2,1,0:T(8,128)S(1)} %get-tuple-element.37.refs_3_.refs_6_, ...), custom_call_target="tpu_custom_call" | custom-call | flops 2013265920 | bytes 786432 | tf_op jit(solution)/shard_map/mix_within_block/pallas_call | solution.py:883
  211.0 16.7 %collective-permute-done.22 = bf16[4,192,768]{2,1,0:T(8,128)(2,1)} collective-permute-done((bf16[4,192,768]{2,1,0:T(8,128)(2,1)}, bf16[4,192,768]{2,1,0:T(8,128)(2,1)}, u32[]{:S(2)}, u32[]{:S(2)}) %collective-permute-start.22) | collective-permute-done | bytes 1179680 | tf_op jit(solution)/shard_map/ppermute | solution.py:34
  227.7 6.3 %place_weights.4 = bf16[1536,1920]{1,0:T(8,128)(2,1)} custom-call(s32[2]{0:T(128)} %pad_add_fusion.refs_0_, bf16[768,768]{1,0:T(8,128)(2,1)} %bitcast.24.refs_1_, bf16[768,768]{1,0:T(8,128)(2,1)} %bitcast.25.refs_2_, bf16[1536,1152]{1,0:T(8,128)(2,1)} %place_weights.3.refs_3_.refs_1_, f32[4,512,768]{2,1,0:T(8,128)} %mix_within_block.1.refs_4_.refs_1_.yl_ref), custom_call_target="tpu_custom_call" | custom-call | tf_op jit(solution)/shard_map/place_weights/pallas_call | solution.py:741
  234.0 9.9 %fusion.14.z_ref = f32[4,528,768]{2,1,0:T(8,128)} fusion(bf16[4,528,1536]{2,1,0:T(8,128)(2,1)} %input_norm.1.refs_9_, bf16[1536,1920]{1,0:T(8,128)(2,1)} %place_weights.4), kind=kOutput, calls=%fused_computation.25 | convolution fusion | flops 4982833152 | bytes 15335424 | tf_op jit(solution)/shard_map/dot_general | solution.py:916
  243.9 8.6 %fusion.17.dn_ref = f32[4,512,768]{2,1,0:T(8,128)} fusion(bf16[768,1536]{1,0:T(8,128)(2,1)S(1)} %copy-done.35, bf16[1,512,1536]{2,1,0:T(8,128)(2,1)} %bitcast.30, bf16[1,512,1536]{2,1,0:T(8,128)(2,1)} %bitcast.29, bf16[1,512,1536]{2,1,0:T(8,128)(2,1)} %bitcast.28, bf16[1,512,1536]{2,1,0:T(8,128)(2,1)S(1)} %bitcast.198), kind=kOutput, calls=%fused_computation.28 | convolution fusion | flops 4841275392 | bytes 14942208 | tf_op jit(solution)/shard_map/qtd,cd->qtc/dot_general | solution.py:918
  252.5 12.6 %gate.1 = (f32[4,512,768]{2,1,0:T(8,128)}, f32[4,8,512]{2,1,0:T(8,128)S(1)}) custom-call(f32[4,512,768]{2,1,0:T(8,128)} %mix_within_block.1.refs_4_.refs_1_.yl_ref, bf16[4,512,256]{2,1,0:T(8,128)(2,1)S(1)} %get-tuple-element.36.refs_1_.bc_ref, f32[4,128,768]{2,1,0:T(8,128)S(1)} %slice_add_fusion.1.inc_ref.refs_3_, f32[4,528,768]{2,1,0:T(8,128)} %fusion.14.z_ref, ...), custom_call_target="tpu_custom_call" | custom-call | flops 25165824 | bytes 1572864 | tf_op jit(solution)/shard_map/gate/pallas_call | solution.py:920
  267.1 9.3 %copy.82 = bf16[1536,2112]{1,0:T(8,128)(2,1)} copy(bf16[1536,2112]{0,1:T(8,128)(2,1)} %bitcast.183) | data formatting | bytes 12976128 | tf_op jit(solution)/shard_map/dot_general | solution.py:1000
  276.4 16.2 %gate_back.1 = (bf16[4,512,768]{2,1,0:T(8,128)(2,1)}, f32[4,512,768]{2,1,0:T(8,128)}, bf16[4,528,1920]{2,1,0:T(8,128)(2,1)}, f32[4,128,768]{2,1,0:T(8,128)S(1)}, f32[4,8,768]{2,1,0:T(8,128)S(1)}) custom-call(f32[4,512,768]{2,1,0:T(8,128)} %get-tuple-element.39.y_ref, f32[4,528,768]{2,1,0:T(8,128)} %fusion.14.z_ref, f32[4,512,768]{2,1,0:T(8,128)} %fusion.17.dn_ref, ...), custom_call_target="tpu_custom_call" | custom-call | flops 402653184 | bytes 31457280 | tf_op jit(solution)/shard_map/gate_back/pallas_call | solution.py:936
  298.6 7.2 %fusion.40.v_ref = f32[4,8,48,768]{3,2,1,0:T(8,128)} fusion(bf16[4,8,48,2112]{3,2,1,0:T(8,128)(2,1)S(1)} %bitcast.197, bf16[2112,768,1,1]{1,0,3,2:T(8,128)(2,1)S(1)} %bitcast.201), kind=kOutput, calls=%fused_computation.115 | convolution fusion | flops 4982833152 | bytes 14450688 | tf_op jit(solution)/shard_map/dot_general | solution.py:1000
  305.8 8.5 %fusion.21 = f32[768,1536,1]{1,0,2:T(8,128)} fusion(bf16[4,512,768]{2,1,0:T(8,128)(2,1)S(1)} %copy-done.67, bf16[1,512,1536]{2,1,0:T(8,128)(2,1)} %bitcast.30, bf16[1,512,1536]{2,1,0:T(8,128)(2,1)} %bitcast.29, bf16[1,512,1536]{2,1,0:T(8,128)(2,1)} %bitcast.28, bf16[1,512,1536]{2,1,0:T(8,128)(2,1)S(1)} %bitcast.199), kind=kOutput, calls=%fused_computation.43 | convolution fusion | flops 4841275392 | bytes 14155776 | tf_op jit(solution)/shard_map/qtc,qtd->cd/dot_general | solution.py:1002
  314.3 6.4 %split_gradients.1 = bf16[8,192,1536]{2,1,0:T(8,128)(2,1)S(1)} custom-call(s32[8]{0:T(128)S(1)} %stack.176.at_ref, f32[4,8,48,768]{3,2,1,0:T(8,128)} %fusion.40.v_ref, f32[1,8,96,1536]{3,2,1,0:T(8,128)} %bitcast.200), custom_call_target="tpu_custom_call" | custom-call | flops 2359296 | bytes 14155776 | tf_op jit(solution)/shard_map/split_gradients/pallas_call | solution.py:979
  327.7 6.4 %convolution_convert_fusion = bf16[2,512,1536]{2,1,0:T(8,128)(2,1)} fusion(bf16[768,1536]{1,0:T(8,128)(2,1)} %in_order.40, bf16[2,2,512,768]{3,2,1,0:T(8,128)(2,1)} %bitcast.215), kind=kOutput, calls=%fused_computation.12 | convolution fusion | flops 2417491968 | bytes 7077888 | tf_op jit(solution)/shard_map/qtc,cd->qtd/dot_general | solution.py:1012
  339.5 24.9 %mix_back.2 = (bf16[4,528,1920]{2,1,0:T(8,128)(2,1)}, f32[4,8,384]{2,1,0:T(8,128)S(1)}, f32[4,8,384]{2,1,0:T(8,128)S(1)}, f32[4,512,512]{2,1,0:T(8,128)}) custom-call(f32[4,512,768]{2,1,0:T(8,128)} %get-tuple-element.35.refs_0_, bf16[4,512,256]{2,1,0:T(8,128)(2,1)S(1)} %get-tuple-element.36.refs_1_.bc_ref, ...), custom_call_target="tpu_custom_call", output_to_operand_aliasing={{0}: (10, {})} | custom-call | flops 40265318400 | bytes 25165824 | tf_op jit(solution)/shard_map/mix_back/pallas_call | solution.py:1063
  366.2 5.9 %fusion.41.v_ref = f32[4,8,48,384]{3,2,1,0:T(8,128)S(1)} fusion(bf16[4,8,48,2112]{3,2,1,0:T(8,128)(2,1)} %bitcast.194, bf16[2112,384,1,1]{1,0,3,2:T(8,128)(2,1)S(1)} %bitcast.204), kind=kOutput, calls=%fused_computation.116 | convolution fusion | flops 2491416576 | bytes 10469376 | tf_op jit(solution)/shard_map/dot_general | solution.py:1000
  383.8 9.4 %all-to-all-start.2 = ((bf16[4,192,1536]{2,1,0:T(8,128)(2,1)}), bf16[4,192,1536]{2,1,0:T(8,128)(2,1)}, u32[]{:S(2)}, u32[]{:S(2)}) async-start(bf16[4,192,1536]{2,1,0:T(8,128)(2,1)} %add_convert_fusion.refs_18_), calls=%async_computation.2 | async-start | bytes 4718592 | tf_op jit(solution)/shard_map/all_to_all | solution.py:44
  393.2 5.7 convert_add_fusion.1
  402.7 29.5 %mix_back.3 = (bf16[4,528,1920]{2,1,0:T(8,128)(2,1)}, f32[4,8,384]{2,1,0:T(8,128)S(1)}, f32[4,8,384]{2,1,0:T(8,128)S(1)}, f32[4,8,256]{2,1,0:T(8,128)S(1)}, f32[4,8,128]{2,1,0:T(8,128)S(1)}) custom-call(f32[4,512,768]{2,1,0:T(8,128)} %get-tuple-element.35.refs_0_, ...), custom_call_target="tpu_custom_call", output_to_operand_aliasing={{0}: (16, {})} | custom-call | flops 40265318400 | bytes 25165824 | tf_op jit(solution)/shard_map/mix_back/pallas_call | solution.py:1063
  450.7 10.3 %fusion.9 = f32[1536,768,1]{1,0,2:T(8,128)} fusion(bf16[4,528,1536]{2,1,0:T(8,128)(2,1)} %input_norm.1.refs_9_, bf16[4,528,1920]{2,1,0:T(8,128)(2,1)} %in_order.41.refs_0_), kind=kOutput, calls=%fused_computation.17 | convolution fusion | flops 4982833152 | bytes 14450688 | tf_op jit(solution)/shard_map/dot_general | solution.py:1000
  468.1 5.3 split_gradient.3
  486.9 11.4 %fusion.4.refs_0_.refs_1_ = bf16[2,528,1536]{2,1,0:T(8,128)(2,1)} fusion(bf16[1536,1920]{1,0:T(8,128)(2,1)} %place_weights.4, bf16[2,2,528,1920]{3,2,1,0:T(8,128)(2,1)} %bitcast.181), kind=kOutput, calls=%fused_computation.11 | convolution fusion | flops 6230163456 | bytes 13197312 | tf_op jit(solution)/shard_map/qtc,dc->qtd/dot_general | solution.py:1122
  505.3 10.2 %fusion.2.refs_1_ = f32[2,528,1536]{2,1,0:T(8,128)S(1)} fusion(bf16[1536,1920]{1,0:T(8,128)(2,1)} %place_weights.4, bf16[2,2,528,1920]{3,2,1,0:T(8,128)(2,1)} %bitcast.182), kind=kOutput, calls=%fused_computation.5 | convolution fusion | flops 6228541440 | bytes 16441344 | tf_op jit(solution)/shard_map/qtc,dc->qtd/dot_general | solution.py:1122
  542.4 14.0 %all-to-all-done.5 = bf16[4,4,48,768]{3,2,1,0:T(8,128)(2,1)} async-done(((bf16[4,4,48,768]{3,2,1,0:T(8,128)(2,1)}), bf16[4,4,48,768]{3,2,1,0:T(8,128)(2,1)}, u32[]{:S(2)}, u32[]{:S(2)}) %all-to-all-start.5) | async-done | bytes 1179680 | tf_op jit(solution)/shard_map/all_to_all | solution.py:44
  565.0 5.1 input_norm_back.1
  (435 shorter events, 228.5 us)
Async XLA Ops:
  2.7 27.0 %all-to-all-start = ((bf16[4,48,1920]{2,1,0:T(8,128)(2,1)}), bf16[4,48,1920]{2,1,0:T(8,128)(2,1)S(1)}, u32[]{:S(2)}, u32[]{:S(2)}) async-start(bf16[4,48,1920]{2,1,0:T(8,128)(2,1)} %pack_weights.1.refs_1_), calls=%async_computation | async-start | bytes 1474560 | tf_op jit(solution)/shard_map/all_to_all | solution.py:44
  33.4 59.0 %collective-permute-start.7 = (bf16[544,1536]{1,0:T(8,128)(2,1)}, bf16[544,1536]{1,0:T(8,128)(2,1)S(1)}, u32[]{:S(2)}, u32[]{:S(2)}) collective-permute-start(bf16[544,1536]{1,0:T(8,128)(2,1)} %in_order.30.refs_0_), channel_id=1, source_target_pairs={{0,16},{16,0},{1,17},{17,1},{2,18},{18,2},{3,19},{19,3},{4,20},{20... | collective-permute-start | bytes 5013512 | tf_op jit(solution)/shard_map/ppermute | solution.py:34
  37.8 32.0 %collective-permute-start.11 = (bf16[192,1152]{1,0:T(8,128)(2,1)S(1)}, bf16[192,1152]{1,0:T(8,128)(2,1)S(1)}, u32[]{:S(2)}, u32[]{:S(2)}) collective-permute-start(bf16[192,1152]{1,0:T(8,128)(2,1)S(1)} %bitcast.187), channel_id=1, source_target_pairs={{0,4},{2,6},{4,0},{6,2},{1,5},{3,7},{5,1},{7,3},{8,12},{10,14},{12... | collective-permute-start | bytes 1327112 | tf_op jit(solution)/shard_map/ppermute | solution.py:34
  40.8 31.0 %collective-permute-start.13 = (bf16[192,1152]{1,0:T(8,128)(2,1)S(1)}, bf16[192,1152]{1,0:T(8,128)(2,1)S(1)}, u32[]{:S(2)}, u32[]{:S(2)}) collective-permute-start(bf16[192,1152]{1,0:T(8,128)(2,1)S(1)} %bitcast.188), channel_id=1, source_target_pairs={{0,6},{2,0},{4,2},{6,4},{1,7},{3,1},{5,3},{7,5},{8,14},{10,8},{12,... | collective-permute-start | bytes 1327112 | tf_op jit(solution)/shard_map/ppermute | solution.py:34
  41.8 30.1 %collective-permute-start.8 = (bf16[192,1152]{1,0:T(8,128)(2,1)S(1)}, bf16[192,1152]{1,0:T(8,128)(2,1)S(1)}, u32[]{:S(2)}, u32[]{:S(2)}) collective-permute-start(bf16[192,1152]{1,0:T(8,128)(2,1)S(1)} %bitcast.189), channel_id=1, source_target_pairs={{0,1},{1,0},{2,3},{3,2},{4,5},{5,4},{6,7},{7,6},{8,9},{9,8},{10,11... | collective-permute-start | bytes 1327112 | tf_op jit(solution)/shard_map/ppermute | solution.py:34
  51.3 20.6 %collective-permute-start.10 = (bf16[192,1152]{1,0:T(8,128)(2,1)S(1)}, bf16[192,1152]{1,0:T(8,128)(2,1)S(1)}, u32[]{:S(2)}, u32[]{:S(2)}) collective-permute-start(bf16[192,1152]{1,0:T(8,128)(2,1)S(1)} %collective-permute-done.9.refs_3_), channel_id=1, source_target_pairs={{0,1},{1,0},{2,3},{3,2},{4,5},{5,4},{6,7},{7,6},{8,9},{9,8},{10,11... | collective-permute-start | bytes 1327112 | tf_op jit(solution)/shard_map/ppermute | solution.py:34
  71.9 46.7 %collective-permute-start.6 = (bf16[544,1536]{1,0:T(8,128)(2,1)}, bf16[544,1536]{1,0:T(8,128)(2,1)}, u32[]{:S(2)}, u32[]{:S(2)}) collective-permute-start(bf16[544,1536]{1,0:T(8,128)(2,1)} %in_order.30.refs_0_), channel_id=1, source_target_pairs={{0,8},{8,0},{1,9},{9,1},{2,10},{10,2},{3,11},{11,3},{4,12},{12,4},... | collective-permute-start | bytes 5013512 | tf_op jit(solution)/shard_map/ppermute | solution.py:34
  93.6 26.4 %collective-permute-start.15 = (bf16[544,1536]{1,0:T(8,128)(2,1)}, bf16[544,1536]{1,0:T(8,128)(2,1)}, u32[]{:S(2)}, u32[]{:S(2)}) collective-permute-start(bf16[544,1536]{1,0:T(8,128)(2,1)} %in_order.31.refs_2_), channel_id=1, source_target_pairs={{0,8},{8,0},{1,9},{9,1},{2,10},{10,2},{3,11},{11,3},{4,12},{12,4},... | collective-permute-start | bytes 5013512 | tf_op jit(solution)/shard_map/ppermute | solution.py:34
  100.5 52.4 %collective-permute-start.16 = (bf16[192,768]{1,0:T(8,128)(2,1)}, bf16[192,768]{1,0:T(8,128)(2,1)}, u32[]{:S(2)}, u32[]{:S(2)}) collective-permute-start(bf16[192,768]{1,0:T(8,128)(2,1)} %in_order.32), channel_id=1, source_target_pairs={{0,2},{2,4},{4,6},{6,0},{1,3},{3,5},{5,7},{7,1},{8,10},{10,12},{12... | collective-permute-start | bytes 884744 | tf_op jit(solution)/shard_map/ppermute | solution.py:34
  108.7 44.3 %collective-permute-start.17 = (bf16[192,768]{1,0:T(8,128)(2,1)}, bf16[192,768]{1,0:T(8,128)(2,1)}, u32[]{:S(2)}, u32[]{:S(2)}) collective-permute-start(bf16[192,768]{1,0:T(8,128)(2,1)} %in_order.32), channel_id=1, source_target_pairs={{0,4},{2,6},{4,0},{6,2},{1,5},{3,7},{5,1},{7,3},{8,12},{10,14},{12... | collective-permute-start | bytes 884744 | tf_op jit(solution)/shard_map/ppermute | solution.py:34
  112.1 40.9 %collective-permute-start.18 = (bf16[192,768]{1,0:T(8,128)(2,1)}, bf16[192,768]{1,0:T(8,128)(2,1)}, u32[]{:S(2)}, u32[]{:S(2)}) collective-permute-start(bf16[192,768]{1,0:T(8,128)(2,1)} %in_order.32), channel_id=1, source_target_pairs={{0,6},{2,0},{4,2},{6,4},{1,7},{3,1},{5,3},{7,5},{8,14},{10,8},{12,... | collective-permute-start | bytes 884744 | tf_op jit(solution)/shard_map/ppermute | solution.py:34
  114.2 72.1 %all-to-all-start.1 = ((bf16[4,192,768]{2,1,0:T(8,128)(2,1)}), bf16[4,192,768]{2,1,0:T(8,128)(2,1)}, u32[]{:S(2)}, u32[]{:S(2)}) async-start(bf16[4,192,768]{2,1,0:T(8,128)(2,1)} %broadcast_in_dim.84), calls=%async_computation.1 | async-start | bytes 2359296 | tf_op jit(solution)/shard_map/all_to_all | solution.py:44
  156.2 32.4 %collective-permute-start.19 = (bf16[4,192,768]{2,1,0:T(8,128)(2,1)}, bf16[4,192,768]{2,1,0:T(8,128)(2,1)}, u32[]{:S(2)}, u32[]{:S(2)}) collective-permute-start(bf16[4,192,768]{2,1,0:T(8,128)(2,1)} %pad_maximum_fusion.4), channel_id=1, source_target_pairs={{0,1},{1,0},{2,3},{3,2},{4,5},{5,4},{6,7},{7,6},{8,9},{9,8},{10,11... | collective-permute-start | bytes 3538952 | tf_op jit(solution)/shard_map/ppermute | solution.py:34
  158.0 43.8 %collective-permute-start.24 = (bf16[512,1536]{1,0:T(8,128)(2,1)}, bf16[512,1536]{1,0:T(8,128)(2,1)}, u32[]{:S(2)}, u32[]{:S(2)}) collective-permute-start(bf16[512,1536]{1,0:T(8,128)(2,1)} %in_order.38), channel_id=1, source_target_pairs={{0,16},{16,0},{1,17},{17,1},{2,18},{18,2},{3,19},{19,3},{4,20},{20... | collective-permute-start | bytes 4718600 | tf_op jit(solution)/shard_map/ppermute | solution.py:34
  178.2 25.4 %collective-permute-start.20 = (bf16[4,144,768]{2,1,0:T(8,128)(2,1)}, bf16[4,144,768]{2,1,0:T(8,128)(2,1)}, u32[]{:S(2)}, u32[]{:S(2)}) collective-permute-start(bf16[4,144,768]{2,1,0:T(8,128)(2,1)} %pad_maximum_fusion.3), channel_id=1, source_target_pairs={{0,1},{1,2},{2,3},{3,4},{4,5},{5,6},{6,7},{8,9},{9,10},{10,11},{11... | collective-permute-start | bytes 2654216 | tf_op jit(solution)/shard_map/ppermute | solution.py:40
  181.9 23.8 %collective-permute-start.21 = (bf16[4,144,768]{2,1,0:T(8,128)(2,1)}, bf16[4,144,768]{2,1,0:T(8,128)(2,1)}, u32[]{:S(2)}, u32[]{:S(2)}) collective-permute-start(bf16[4,144,768]{2,1,0:T(8,128)(2,1)} %pad_maximum_fusion.3), channel_id=1, source_target_pairs={{0,2},{1,3},{2,4},{3,5},{4,6},{5,7},{8,10},{9,11},{10,12},{11,13},... | collective-permute-start | bytes 2654216 | tf_op jit(solution)/shard_map/ppermute | solution.py:40
  186.3 41.3 %collective-permute-start.22 = (bf16[4,192,768]{2,1,0:T(8,128)(2,1)}, bf16[4,192,768]{2,1,0:T(8,128)(2,1)}, u32[]{:S(2)}, u32[]{:S(2)}) collective-permute-start(bf16[4,192,768]{2,1,0:T(8,128)(2,1)} %in_order.37), channel_id=1, source_target_pairs={{0,1},{1,0},{2,3},{3,2},{4,5},{5,4},{6,7},{7,6},{8,9},{9,8},{10,11... | collective-permute-start | bytes 3538952 | tf_op jit(solution)/shard_map/ppermute | solution.py:34
  188.6 55.3 %collective-permute-start.23 = (bf16[512,1536]{1,0:T(8,128)(2,1)}, bf16[512,1536]{1,0:T(8,128)(2,1)}, u32[]{:S(2)}, u32[]{:S(2)}) collective-permute-start(bf16[512,1536]{1,0:T(8,128)(2,1)} %in_order.38), channel_id=1, source_target_pairs={{0,8},{8,0},{1,9},{9,1},{2,10},{10,2},{3,11},{11,3},{4,12},{12,4},... | collective-permute-start | bytes 4718600 | tf_op jit(solution)/shard_map/ppermute | solution.py:34
  201.8 42.1 %collective-permute-start.25 = (bf16[512,1536]{1,0:T(8,128)(2,1)}, bf16[512,1536]{1,0:T(8,128)(2,1)}, u32[]{:S(2)}, u32[]{:S(2)}) collective-permute-start(bf16[512,1536]{1,0:T(8,128)(2,1)} %in_order.39), channel_id=1, source_target_pairs={{0,8},{8,0},{1,9},{9,1},{2,10},{10,2},{3,11},{11,3},{4,12},{12,4},... | collective-permute-start | bytes 4718600 | tf_op jit(solution)/shard_map/ppermute | solution.py:34
  293.7 40.7 %collective-permute-start.30 = (bf16[4,144,768]{2,1,0:T(8,128)(2,1)}, bf16[4,144,768]{2,1,0:T(8,128)(2,1)S(1)}, u32[]{:S(2)}, u32[]{:S(2)}) collective-permute-start(bf16[4,144,768]{2,1,0:T(8,128)(2,1)} %pad_maximum_fusion.2), channel_id=1, source_target_pairs={{1,0},{2,1},{3,2},{4,3},{5,4},{6,5},{7,6},{9,8},{10,9},{11,10},{12... | collective-permute-start | bytes 2654216 | tf_op jit(solution)/shard_map/ppermute | solution.py:40
  294.9 43.2 %collective-permute-start.31 = (bf16[4,144,768]{2,1,0:T(8,128)(2,1)}, bf16[4,144,768]{2,1,0:T(8,128)(2,1)}, u32[]{:S(2)}, u32[]{:S(2)}) collective-permute-start(bf16[4,144,768]{2,1,0:T(8,128)(2,1)} %pad_maximum_fusion.2), channel_id=1, source_target_pairs={{2,0},{3,1},{4,2},{5,3},{6,4},{7,5},{10,8},{11,9},{12,10},{13,11},... | collective-permute-start | bytes 2654216 | tf_op jit(solution)/shard_map/ppermute | solution.py:40
  324.6 55.5 %collective-permute-start.32 = (bf16[4,192,1536]{2,1,0:T(8,128)(2,1)}, bf16[4,192,1536]{2,1,0:T(8,128)(2,1)}, u32[]{:S(2)}, u32[]{:S(2)}) collective-permute-start(bf16[4,192,1536]{2,1,0:T(8,128)(2,1)} %slice.367), channel_id=1, source_target_pairs={{0,1},{1,0},{2,3},{3,2},{4,5},{5,4},{6,7},{7,6},{8,9},{9,8},{10,11... | collective-permute-start | bytes 7077896 | tf_op jit(solution)/shard_map/ppermute | solution.py:34
  334.1 59.1 %collective-permute-start.28 = (bf16[2,512,1536]{2,1,0:T(8,128)(2,1)}, bf16[2,512,1536]{2,1,0:T(8,128)(2,1)}, u32[]{:S(2)}, u32[]{:S(2)}) collective-permute-start(bf16[2,512,1536]{2,1,0:T(8,128)(2,1)} %convolution_convert_fusion), channel_id=1, source_target_pairs={{0,8},{8,0},{1,9},{9,1},{2,10},{10,2},{3,11},{11,3},{4,12},{12,4},... | collective-permute-start | bytes 9437192 | tf_op jit(solution)/shard_map/ppermute | solution.py:34
  375.3 59.0 %collective-permute-start.34 = (bf16[4,4,48,384]{3,2,1,0:T(8,128)(2,1)}, bf16[4,4,48,384]{3,2,1,0:T(8,128)(2,1)}, u32[]{:S(2)}, u32[]{:S(2)}) collective-permute-start(bf16[4,4,48,384]{3,2,1,0:T(8,128)(2,1)} %get-tuple-element.63), channel_id=1, source_target_pairs={{0,1},{1,0},{2,3},{3,2},{4,5},{5,4},{6,7},{7,6},{8,9},{9,8},{10,11... | collective-permute-start | bytes 1769480 | tf_op jit(solution)/shard_map/ppermute | solution.py:34
  383.8 60.2 %all-to-all-start.2 = ((bf16[4,192,1536]{2,1,0:T(8,128)(2,1)}), bf16[4,192,1536]{2,1,0:T(8,128)(2,1)}, u32[]{:S(2)}, u32[]{:S(2)}) async-start(bf16[4,192,1536]{2,1,0:T(8,128)(2,1)} %add_convert_fusion.refs_18_), calls=%async_computation.2 | async-start | bytes 4718592 | tf_op jit(solution)/shard_map/all_to_all | solution.py:44
  400.3 36.3 %collective-permute-start.29 = (bf16[512,1536]{1,0:T(8,128)(2,1)}, bf16[512,1536]{1,0:T(8,128)(2,1)}, u32[]{:S(2)}, u32[]{:S(2)}) collective-permute-start(bf16[512,1536]{1,0:T(8,128)(2,1)} %fusion.20.refs_19_), channel_id=1, source_target_pairs={{0,16},{16,0},{1,17},{17,1},{2,18},{18,2},{3,19},{19,3},{4,20},{20... | collective-permute-start | bytes 4718600 | tf_op jit(solution)/shard_map/ppermute | solution.py:34
  432.7 28.4 %collective-permute-start.38 = (f32[160,128]{1,0:T(8,128)S(1)}, f32[160,128]{1,0:T(8,128)S(1)}, u32[]{:S(2)}, u32[]{:S(2)}) collective-permute-start(f32[160,128]{1,0:T(8,128)S(1)} %fusion.23.refs_0_), channel_id=1, source_target_pairs={{0,16},{16,0},{1,17},{17,1},{2,18},{18,2},{3,19},{19,3},{4,20},{20... | collective-permute-start | bytes 245768 | tf_op jit(solution)/shard_map/ppermute | solution.py:131
  447.1 33.6 %all-to-all-start.3 = ((bf16[4,4,48,384]{3,2,1,0:T(8,128)(2,1)}), bf16[4,4,48,384]{3,2,1,0:T(8,128)(2,1)S(1)}, u32[]{:S(2)}, u32[]{:S(2)}) async-start(bf16[4,4,48,384]{3,2,1,0:T(8,128)(2,1)} %in_order.43), calls=%async_computation.3 | async-start | bytes 1179648 | tf_op jit(solution)/shard_map/all_to_all | solution.py:44
  474.6 27.3 %collective-permute-start.35 = (bf16[4,4,48,768]{3,2,1,0:T(8,128)(2,1)}, bf16[4,4,48,768]{3,2,1,0:T(8,128)(2,1)}, u32[]{:S(2)}, u32[]{:S(2)}) collective-permute-start(bf16[4,4,48,768]{3,2,1,0:T(8,128)(2,1)} %slice.376), channel_id=1, source_target_pairs={{0,1},{1,0},{2,3},{3,2},{4,5},{5,4},{6,7},{7,6},{8,9},{9,8},{10,11... | collective-permute-start | bytes 3538952 | tf_op jit(solution)/shard_map/ppermute | solution.py:34
  481.6 22.9 %all-to-all-start.4 = ((bf16[4,48,1152]{2,1,0:T(8,128)(2,1)}), bf16[4,48,1152]{2,1,0:T(8,128)(2,1)S(1)}, u32[]{:S(2)}, u32[]{:S(2)}) async-start(bf16[4,48,1152]{2,1,0:T(8,128)(2,1)} %pad_maximum_fusion.8), calls=%async_computation.4 | async-start | bytes 884736 | tf_op jit(solution)/shard_map/all_to_all | solution.py:44
  522.4 34.1 %all-to-all-start.5 = ((bf16[4,4,48,768]{3,2,1,0:T(8,128)(2,1)}), bf16[4,4,48,768]{3,2,1,0:T(8,128)(2,1)}, u32[]{:S(2)}, u32[]{:S(2)}) async-start(bf16[4,4,48,768]{3,2,1,0:T(8,128)(2,1)} %in_order.46), calls=%async_computation.5 | async-start | bytes 2359296 | tf_op jit(solution)/shard_map/all_to_all | solution.py:44
  527.1 37.9 %collective-permute-start.37 = (bf16[528,1536]{1,0:T(8,128)(2,1)}, bf16[528,1536]{1,0:T(8,128)(2,1)}, u32[]{:S(2)}, u32[]{:S(2)}) collective-permute-start(bf16[528,1536]{1,0:T(8,128)(2,1)} %fusion.19.refs_2_), channel_id=1, source_target_pairs={{0,16},{16,0},{1,17},{17,1},{2,18},{18,2},{3,19},{19,3},{4,20},{20... | collective-permute-start | bytes 4866056 | tf_op jit(solution)/shard_map/ppermute | solution.py:34
  (92 other events, 973.1 us)

commit v5 on v4

--- a/solution.py
+++ b/solution.py
@@ -683,9 +683,11 @@
         name="pack_weights",
     )(in_proj)
     held = exchange(packed, ("x", "core"))
-    every = sum_over(every, ("a", "b", "x", "core"), [packed, packed, packed, held])
+    every = sum_over(every, ("x", "core", "a"), [packed])
     block = held[:, :, :first_cols].reshape(-1, first_cols)
+    block = after(block, every)
     first_over_a = [block] + [shift(block, "a", sa) for sa in range(1, na)]
+    every = sum_over(every, ("b",))
     first_blocks = [v for here in first_over_a for v in gather_over_b(here)]
 
     ids_row = jnp.pad(segment_ids.astype(BF)[None], ((0, 15), (0, width - rows)))

time: 586 us -> 577 us (0.985)
    unnamed x150 -> x146, local copies, waits for them, and re-layouts: 22.7 us -> 24.5 us
  transfers between devices with their start and end apart: 50 -> 50, of which waited for: 18 -> 15; matrix products, arithmetic and copies ran while one was open for 31% -> 31% of each run, Pallas kernels for 22% -> 22%
where the time goes in v5:
time: 577 us; the launch traced here: 566 us
  Pallas kernels  157 us (27%)
  waiting for transfers between devices  98.7 us (17%)
  starting transfers between devices  98.2 us (17%)
  matrix products  97.3 us (17%)
  local copies, waits for them, and re-layouts  68.2 us (12%)
  other arithmetic  44.5 us (8%)
    ppermute x27, waiting for transfers between devices, shift(): return lax.ppermute(v, axis, [(i, (i + step) % n) for i in range(n)])  71 us
    pallas_call x2, Pallas kernels, on_device(): pl.pallas_call(body, grid=(groups,), in_specs=[spec for _, spec in operan...  54.5 us
    ppermute x27, starting transfers between devices, shift(): return lax.ppermute(v, axis, [(i, (i + step) % n) for i in range(n)])  34.6 us
    all_to_all x7, starting transfers between devices, exchange(): return lax.all_to_all(v, axes, 0, 0, tiled=True)  33.4 us
    unnamed x146, local copies, waits for them, and re-layouts  24.5 us
    dot_general x3, matrix products, grad_of(): return jnp.dot(normed_rows.T, d_rows, preferred_element_type=F32)  23.5 us
    dot_general x2, matrix products, inward(): jnp.einsum('qtc,dc->qtd', d_by, w_all, preferred_element_type=F32)  21.7 us
    all_to_all x7, waiting for transfers between devices, exchange(): return lax.all_to_all(v, axes, 0, 0, tiled=True)  17.1 us
  transfers between devices with their start and end apart: 50, of which 15 were waited for; matrix products, arithmetic and copies ran while one was open for 31% of the time, Pallas kernels for 22%

profile of v5, /device:TPU:0, one launch (start us, length us, event | category | flops | bytes accessed | tf_op | source)
XLA Modules:
  0.0 566.1 jit_solution(16384894396695216998)
XLA Ops:
  38.4 9.5 %collective-permute-done.9.refs_3_ = bf16[192,1152]{1,0:T(8,128)(2,1)S(1)} collective-permute-done((bf16[192,1152]{1,0:T(8,128)(2,1)}, bf16[192,1152]{1,0:T(8,128)(2,1)S(1)}, u32[]{:S(2)}, u32[]{:S(2)}) %collective-permute-start.9) | collective-permute-done | bytes 442400 | tf_op jit(solution)/shard_map/ppermute | solution.py:34
  48.6 14.2 %collective-permute-done.11.refs_5_ = bf16[192,1152]{1,0:T(8,128)(2,1)S(1)} collective-permute-done((bf16[192,1152]{1,0:T(8,128)(2,1)}, bf16[192,1152]{1,0:T(8,128)(2,1)S(1)}, u32[]{:S(2)}, u32[]{:S(2)}) %collective-permute-start.11) | collective-permute-done | bytes 442400 | tf_op jit(solution)/shard_map/ppermute | solution.py:34
  64.9 11.0 %collective-permute-done.12.refs_6_ = bf16[192,1152]{1,0:T(8,128)(2,1)S(1)} collective-permute-done((bf16[192,1152]{1,0:T(8,128)(2,1)S(1)}, bf16[192,1152]{1,0:T(8,128)(2,1)S(1)}, u32[]{:S(2)}, u32[]{:S(2)}) %collective-permute-start.12) | collective-permute-done | bytes 442400 | tf_op jit(solution)/shard_map/ppermute | solution.py:34
  75.9 7.9 %collective-permute-done.14.refs_8_ = bf16[192,1152]{1,0:T(8,128)(2,1)S(1)} collective-permute-done((bf16[192,1152]{1,0:T(8,128)(2,1)S(1)}, bf16[192,1152]{1,0:T(8,128)(2,1)S(1)}, u32[]{:S(2)}, u32[]{:S(2)}) %collective-permute-start.14) | collective-permute-done | bytes 442400 | tf_op jit(solution)/shard_map/ppermute | solution.py:34
  92.7 9.2 %collective-permute-start.16 = (bf16[192,768]{1,0:T(8,128)(2,1)}, bf16[192,768]{1,0:T(8,128)(2,1)}, u32[]{:S(2)}, u32[]{:S(2)}) collective-permute-start(bf16[192,768]{1,0:T(8,128)(2,1)} %in_order.28), channel_id=1, source_target_pairs={{0,2},{2,4},{4,6},{6,0},{1,3},{3,5},{5,7},{7,1},{8,10},{10,12},{12... | collective-permute-start | bytes 884744 | tf_op jit(solution)/shard_map/ppermute | solution.py:34
  114.0 6.3 %input_norm.1.refs_9_ = bf16[4,528,1536]{2,1,0:T(8,128)(2,1)} custom-call(bf16[544,1536]{1,0:T(8,128)(2,1)S(1)} %copy-done.6, bf16[544,1536]{1,0:T(8,128)(2,1)} %collective-permute-done.6.refs_1_, bf16[544,1536]{1,0:T(8,128)(2,1)S(1)} %copy-done.11, bf16[544,1536]{1,0:T(8,128)(2,1)} %collective-permute-done.15.refs_3_, ...), custom_call_target="tpu_custom_call" | custom-call | flops 1966080 | bytes 786432 | tf_op jit(solution)/shard_map/input_norm/pallas_call | solution.py:717
  120.9 5.1 place_weights.3.refs_3_.refs_1_
  125.9 13.0 %fusion.7.refs_0_.refs_1_.refs_2_.refs_8_.refs_11_.refs_12_.refs_13_ = f32[4,528,1152]{2,1,0:T(8,128)} fusion(bf16[4,528,1536]{2,1,0:T(8,128)(2,1)S(1)} %copy-done.31, bf16[1536,1152]{1,0:T(8,128)(2,1)} %place_weights.3.refs_3_.refs_1_), kind=kOutput, calls=%fused_computation.13 | convolution fusion | flops 7474249728 | bytes 19759104 | tf_op jit(solution)/shard_map/dot_general | solution.py:798
  150.0 15.3 %conv_and_state.1 = (f32[4,512,768]{2,1,0:T(8,128)}, bf16[4,512,256]{2,1,0:T(8,128)(2,1)S(1)}, f32[4,128,768]{2,1,0:T(8,128)S(1)}) custom-call(f32[4,528,1152]{2,1,0:T(8,128)} %fusion.7.refs_0_.refs_1_.refs_2_.refs_8_.refs_11_.refs_12_.refs_13_, f32[4,528,1152]{2,1,0:T(8,128)} %fusion.7.refs_0_.refs_1_.refs_2_.refs_8_.refs_11_.refs_12_.refs_13_, ...), custom_call_target="tpu_custom_call" | custom-call | flops 251658240 | bytes 786432 | tf_op jit(solution)/shard_map/conv_and_state/pallas_call | solution.py:843
  179.9 13.1 %mix_within_block.1.refs_4_.refs_1_.yl_ref = f32[4,512,768]{2,1,0:T(8,128)} custom-call(f32[4,512,768]{2,1,0:T(8,128)} %get-tuple-element.35.refs_0_, bf16[4,512,256]{2,1,0:T(8,128)(2,1)S(1)} %get-tuple-element.36.refs_1_.bc_ref, f32[4,2,512,128]{3,2,1,0:T(8,128)S(1)} %copy-done.2, f32[4,24,512]{2,1,0:T(8,128)S(1)} %get-tuple-element.37.refs_3_.refs_6_, ...), custom_call_target="tpu_custom_call" | custom-call | flops 2013265920 | bytes 786432 | tf_op jit(solution)/shard_map/mix_within_block/pallas_call | solution.py:885
  201.7 16.7 %collective-permute-done.22 = bf16[4,192,768]{2,1,0:T(8,128)(2,1)} collective-permute-done((bf16[4,192,768]{2,1,0:T(8,128)(2,1)}, bf16[4,192,768]{2,1,0:T(8,128)(2,1)}, u32[]{:S(2)}, u32[]{:S(2)}) %collective-permute-start.22) | collective-permute-done | bytes 1179680 | tf_op jit(solution)/shard_map/ppermute | solution.py:34
  218.4 6.3 %place_weights.4 = bf16[1536,1920]{1,0:T(8,128)(2,1)} custom-call(s32[2]{0:T(128)} %pad_add_fusion.refs_0_, bf16[768,768]{1,0:T(8,128)(2,1)} %bitcast.24.refs_1_, bf16[768,768]{1,0:T(8,128)(2,1)} %bitcast.25.refs_2_, bf16[1536,1152]{1,0:T(8,128)(2,1)} %place_weights.3.refs_3_.refs_1_, f32[4,512,768]{2,1,0:T(8,128)} %mix_within_block.1.refs_4_.refs_1_.yl_ref), custom_call_target="tpu_custom_call" | custom-call | tf_op jit(solution)/shard_map/place_weights/pallas_call | solution.py:743
  224.7 9.9 %fusion.14.z_ref = f32[4,528,768]{2,1,0:T(8,128)} fusion(bf16[4,528,1536]{2,1,0:T(8,128)(2,1)} %input_norm.1.refs_9_, bf16[1536,1920]{1,0:T(8,128)(2,1)} %place_weights.4), kind=kOutput, calls=%fused_computation.25 | convolution fusion | flops 4982833152 | bytes 15335424 | tf_op jit(solution)/shard_map/dot_general | solution.py:918
  234.6 8.6 %fusion.17.dn_ref = f32[4,512,768]{2,1,0:T(8,128)} fusion(bf16[768,1536]{1,0:T(8,128)(2,1)S(1)} %copy-done.34, bf16[1,512,1536]{2,1,0:T(8,128)(2,1)} %bitcast.30, bf16[1,512,1536]{2,1,0:T(8,128)(2,1)} %bitcast.29, bf16[1,512,1536]{2,1,0:T(8,128)(2,1)} %bitcast.28, bf16[1,512,1536]{2,1,0:T(8,128)(2,1)S(1)} %bitcast.191), kind=kOutput, calls=%fused_computation.28 | convolution fusion | flops 4841275392 | bytes 14942208 | tf_op jit(solution)/shard_map/qtd,cd->qtc/dot_general | solution.py:920
  243.2 12.5 %gate.1 = (f32[4,512,768]{2,1,0:T(8,128)}, f32[4,8,512]{2,1,0:T(8,128)S(1)}) custom-call(f32[4,512,768]{2,1,0:T(8,128)} %mix_within_block.1.refs_4_.refs_1_.yl_ref, bf16[4,512,256]{2,1,0:T(8,128)(2,1)S(1)} %get-tuple-element.36.refs_1_.bc_ref, f32[4,128,768]{2,1,0:T(8,128)S(1)} %slice_add_fusion.1.inc_ref.refs_3_, f32[4,528,768]{2,1,0:T(8,128)} %fusion.14.z_ref, ...), custom_call_target="tpu_custom_call" | custom-call | flops 25165824 | bytes 1572864 | tf_op jit(solution)/shard_map/gate/pallas_call | solution.py:922
  257.5 9.2 %copy.80 = bf16[1536,2112]{1,0:T(8,128)(2,1)} copy(bf16[1536,2112]{0,1:T(8,128)(2,1)} %bitcast.183) | data formatting | bytes 12976128 | tf_op jit(solution)/shard_map/dot_general | solution.py:1002
  266.8 16.2 %gate_back.1 = (bf16[4,512,768]{2,1,0:T(8,128)(2,1)}, f32[4,512,768]{2,1,0:T(8,128)}, bf16[4,528,1920]{2,1,0:T(8,128)(2,1)}, f32[4,128,768]{2,1,0:T(8,128)S(1)}, f32[4,8,768]{2,1,0:T(8,128)S(1)}) custom-call(f32[4,512,768]{2,1,0:T(8,128)} %get-tuple-element.39.y_ref, f32[4,528,768]{2,1,0:T(8,128)} %fusion.14.z_ref, f32[4,512,768]{2,1,0:T(8,128)} %fusion.17.dn_ref, ...), custom_call_target="tpu_custom_call" | custom-call | flops 402653184 | bytes 31457280 | tf_op jit(solution)/shard_map/gate_back/pallas_call | solution.py:938
  289.0 7.3 %fusion.40.v_ref = f32[4,8,48,768]{3,2,1,0:T(8,128)} fusion(bf16[4,8,48,2112]{3,2,1,0:T(8,128)(2,1)S(1)} %bitcast.190, bf16[2112,768,1,1]{1,0,3,2:T(8,128)(2,1)S(1)} %bitcast.194), kind=kOutput, calls=%fused_computation.115 | convolution fusion | flops 4982833152 | bytes 14450688 | tf_op jit(solution)/shard_map/dot_general | solution.py:1002
  296.3 8.5 %fusion.21 = f32[768,1536,1]{1,0,2:T(8,128)} fusion(bf16[4,512,768]{2,1,0:T(8,128)(2,1)S(1)} %copy-done.65, bf16[1,512,1536]{2,1,0:T(8,128)(2,1)} %bitcast.30, bf16[1,512,1536]{2,1,0:T(8,128)(2,1)} %bitcast.29, bf16[1,512,1536]{2,1,0:T(8,128)(2,1)} %bitcast.28, bf16[1,512,1536]{2,1,0:T(8,128)(2,1)S(1)} %bitcast.192), kind=kOutput, calls=%fused_computation.43 | convolution fusion | flops 4841275392 | bytes 14155776 | tf_op jit(solution)/shard_map/qtc,qtd->cd/dot_general | solution.py:1004
  304.8 6.4 %split_gradients.1 = bf16[8,192,1536]{2,1,0:T(8,128)(2,1)S(1)} custom-call(s32[8]{0:T(128)S(1)} %stack.176.at_ref, f32[4,8,48,768]{3,2,1,0:T(8,128)} %fusion.40.v_ref, f32[1,8,96,1536]{3,2,1,0:T(8,128)} %bitcast.193), custom_call_target="tpu_custom_call" | custom-call | flops 2359296 | bytes 14155776 | tf_op jit(solution)/shard_map/split_gradients/pallas_call | solution.py:981
  318.1 6.4 %convolution_convert_fusion = bf16[2,512,1536]{2,1,0:T(8,128)(2,1)} fusion(bf16[768,1536]{1,0:T(8,128)(2,1)} %in_order.36, bf16[2,2,512,768]{3,2,1,0:T(8,128)(2,1)} %bitcast.208), kind=kOutput, calls=%fused_computation.12 | convolution fusion | flops 2417491968 | bytes 7077888 | tf_op jit(solution)/shard_map/qtc,cd->qtd/dot_general | solution.py:1014
  330.2 25.0 %mix_back.2 = (bf16[4,528,1920]{2,1,0:T(8,128)(2,1)}, f32[4,8,384]{2,1,0:T(8,128)S(1)}, f32[4,8,384]{2,1,0:T(8,128)S(1)}, f32[4,512,512]{2,1,0:T(8,128)}) custom-call(f32[4,512,768]{2,1,0:T(8,128)} %get-tuple-element.35.refs_0_, bf16[4,512,256]{2,1,0:T(8,128)(2,1)S(1)} %get-tuple-element.36.refs_1_.bc_ref, ...), custom_call_target="tpu_custom_call", output_to_operand_aliasing={{0}: (10, {})} | custom-call | flops 40265318400 | bytes 25165824 | tf_op jit(solution)/shard_map/mix_back/pallas_call | solution.py:1065
  356.9 5.9 %fusion.41.v_ref = f32[4,8,48,384]{3,2,1,0:T(8,128)S(1)} fusion(bf16[4,8,48,2112]{3,2,1,0:T(8,128)(2,1)} %bitcast.187, bf16[2112,384,1,1]{1,0,3,2:T(8,128)(2,1)S(1)} %bitcast.197), kind=kOutput, calls=%fused_computation.116 | convolution fusion | flops 2491416576 | bytes 10469376 | tf_op jit(solution)/shard_map/dot_general | solution.py:1002
  374.2 9.0 %all-to-all-start.2 = ((bf16[4,192,1536]{2,1,0:T(8,128)(2,1)}), bf16[4,192,1536]{2,1,0:T(8,128)(2,1)}, u32[]{:S(2)}, u32[]{:S(2)}) async-start(bf16[4,192,1536]{2,1,0:T(8,128)(2,1)} %add_convert_fusion.refs_18_), calls=%async_computation.2 | async-start | bytes 4718592 | tf_op jit(solution)/shard_map/all_to_all | solution.py:44
  383.2 5.7 %convert_add_fusion.1 = f32[2,512,1536]{2,1,0:T(8,128)S(1)} fusion(bf16[2,512,1536]{2,1,0:T(8,128)(2,1)} %collective-permute-done.28, bf16[768,1536]{1,0:T(8,128)(2,1)} %in_order.36, bf16[2,2,512,768]{3,2,1,0:T(8,128)(2,1)} %bitcast.209), kind=kOutput, calls=%fused_computation.2 | convolution fusion | flops 2419064832 | bytes 13369344 | tf_op jit(solution)/shard_map/qtc,cd->qtd/dot_general | solution.py:1014
  392.7 29.5 %mix_back.3 = (bf16[4,528,1920]{2,1,0:T(8,128)(2,1)}, f32[4,8,384]{2,1,0:T(8,128)S(1)}, f32[4,8,384]{2,1,0:T(8,128)S(1)}, f32[4,8,256]{2,1,0:T(8,128)S(1)}, f32[4,8,128]{2,1,0:T(8,128)S(1)}) custom-call(f32[4,512,768]{2,1,0:T(8,128)} %get-tuple-element.35.refs_0_, ...), custom_call_target="tpu_custom_call", output_to_operand_aliasing={{0}: (16, {})} | custom-call | flops 40265318400 | bytes 25165824 | tf_op jit(solution)/shard_map/mix_back/pallas_call | solution.py:1065
  441.2 10.4 %fusion.9 = f32[1536,768,1]{1,0,2:T(8,128)} fusion(bf16[4,528,1536]{2,1,0:T(8,128)(2,1)} %input_norm.1.refs_9_, bf16[4,528,1920]{2,1,0:T(8,128)(2,1)} %in_order.37.refs_0_), kind=kOutput, calls=%fused_computation.17 | convolution fusion | flops 4982833152 | bytes 14450688 | tf_op jit(solution)/shard_map/dot_general | solution.py:1002
  458.6 5.3 split_gradient.3
  477.4 11.5 %fusion.4.refs_0_.refs_1_ = bf16[2,528,1536]{2,1,0:T(8,128)(2,1)} fusion(bf16[1536,1920]{1,0:T(8,128)(2,1)} %place_weights.4, bf16[2,2,528,1920]{3,2,1,0:T(8,128)(2,1)} %bitcast.181), kind=kOutput, calls=%fused_computation.11 | convolution fusion | flops 6230163456 | bytes 13197312 | tf_op jit(solution)/shard_map/qtc,dc->qtd/dot_general | solution.py:1124
  495.8 10.2 %fusion.2.refs_1_ = f32[2,528,1536]{2,1,0:T(8,128)S(1)} fusion(bf16[1536,1920]{1,0:T(8,128)(2,1)} %place_weights.4, bf16[2,2,528,1920]{3,2,1,0:T(8,128)(2,1)} %bitcast.182), kind=kOutput, calls=%fused_computation.5 | convolution fusion | flops 6228541440 | bytes 16441344 | tf_op jit(solution)/shard_map/qtc,dc->qtd/dot_general | solution.py:1124
  512.9 6.1 %all-to-all-start.5 = ((bf16[4,4,48,768]{3,2,1,0:T(8,128)(2,1)}), bf16[4,4,48,768]{3,2,1,0:T(8,128)(2,1)}, u32[]{:S(2)}, u32[]{:S(2)}) async-start(bf16[4,4,48,768]{3,2,1,0:T(8,128)(2,1)} %in_order.42), calls=%async_computation.5 | async-start | bytes 2359296 | tf_op jit(solution)/shard_map/all_to_all | solution.py:44
  534.5 13.7 %all-to-all-done.5 = bf16[4,4,48,768]{3,2,1,0:T(8,128)(2,1)} async-done(((bf16[4,4,48,768]{3,2,1,0:T(8,128)(2,1)}), bf16[4,4,48,768]{3,2,1,0:T(8,128)(2,1)}, u32[]{:S(2)}, u32[]{:S(2)}) %all-to-all-start.5) | async-done | bytes 1179680 | tf_op jit(solution)/shard_map/all_to_all | solution.py:44
  (429 shorter events, 218.9 us)
Async XLA Ops:
  28.9 55.6 %collective-permute-start.7 = (bf16[544,1536]{1,0:T(8,128)(2,1)}, bf16[544,1536]{1,0:T(8,128)(2,1)S(1)}, u32[]{:S(2)}, u32[]{:S(2)}) collective-permute-start(bf16[544,1536]{1,0:T(8,128)(2,1)} %in_order.25.refs_0_), channel_id=1, source_target_pairs={{0,16},{16,0},{1,17},{17,1},{2,18},{18,2},{3,19},{19,3},{4,20},{20... | collective-permute-start | bytes 5013512 | tf_op jit(solution)/shard_map/ppermute | solution.py:34
  33.3 29.5 %collective-permute-start.11 = (bf16[192,1152]{1,0:T(8,128)(2,1)}, bf16[192,1152]{1,0:T(8,128)(2,1)S(1)}, u32[]{:S(2)}, u32[]{:S(2)}) collective-permute-start(bf16[192,1152]{1,0:T(8,128)(2,1)} %in_order.26.refs_1_), channel_id=1, source_target_pairs={{0,4},{2,6},{4,0},{6,2},{1,5},{3,7},{5,1},{7,3},{8,12},{10,14},{12... | collective-permute-start | bytes 1327112 | tf_op jit(solution)/shard_map/ppermute | solution.py:34
  35.8 28.0 %collective-permute-start.13 = (bf16[192,1152]{1,0:T(8,128)(2,1)}, bf16[192,1152]{1,0:T(8,128)(2,1)S(1)}, u32[]{:S(2)}, u32[]{:S(2)}) collective-permute-start(bf16[192,1152]{1,0:T(8,128)(2,1)} %in_order.26.refs_1_), channel_id=1, source_target_pairs={{0,6},{2,0},{4,2},{6,4},{1,7},{3,1},{5,3},{7,5},{8,14},{10,8},{12,... | collective-permute-start | bytes 1327112 | tf_op jit(solution)/shard_map/ppermute | solution.py:34
  38.2 26.6 %collective-permute-start.8 = (bf16[192,1152]{1,0:T(8,128)(2,1)}, bf16[192,1152]{1,0:T(8,128)(2,1)S(1)}, u32[]{:S(2)}, u32[]{:S(2)}) collective-permute-start(bf16[192,1152]{1,0:T(8,128)(2,1)} %in_order.26.refs_1_), channel_id=1, source_target_pairs={{0,1},{1,0},{2,3},{3,2},{4,5},{5,4},{6,7},{7,6},{8,9},{9,8},{10,11... | collective-permute-start | bytes 1327112 | tf_op jit(solution)/shard_map/ppermute | solution.py:34
  63.8 20.0 %collective-permute-start.14 = (bf16[192,1152]{1,0:T(8,128)(2,1)S(1)}, bf16[192,1152]{1,0:T(8,128)(2,1)S(1)}, u32[]{:S(2)}, u32[]{:S(2)}) collective-permute-start(bf16[192,1152]{1,0:T(8,128)(2,1)S(1)} %collective-permute-done.13.refs_7_), channel_id=1, source_target_pairs={{0,1},{1,0},{2,3},{3,2},{4,5},{5,4},{6,7},{7,6},{8,9},{9,8},{10,11... | collective-permute-start | bytes 1327112 | tf_op jit(solution)/shard_map/ppermute | solution.py:34
  64.8 45.9 %collective-permute-start.6 = (bf16[544,1536]{1,0:T(8,128)(2,1)}, bf16[544,1536]{1,0:T(8,128)(2,1)}, u32[]{:S(2)}, u32[]{:S(2)}) collective-permute-start(bf16[544,1536]{1,0:T(8,128)(2,1)} %in_order.25.refs_0_), channel_id=1, source_target_pairs={{0,8},{8,0},{1,9},{9,1},{2,10},{10,2},{3,11},{11,3},{4,12},{12,4},... | collective-permute-start | bytes 5013512 | tf_op jit(solution)/shard_map/ppermute | solution.py:34
  85.8 26.4 %collective-permute-start.15 = (bf16[544,1536]{1,0:T(8,128)(2,1)}, bf16[544,1536]{1,0:T(8,128)(2,1)}, u32[]{:S(2)}, u32[]{:S(2)}) collective-permute-start(bf16[544,1536]{1,0:T(8,128)(2,1)} %in_order.27.refs_2_), channel_id=1, source_target_pairs={{0,8},{8,0},{1,9},{9,1},{2,10},{10,2},{3,11},{11,3},{4,12},{12,4},... | collective-permute-start | bytes 5013512 | tf_op jit(solution)/shard_map/ppermute | solution.py:34
  92.7 52.5 %collective-permute-start.16 = (bf16[192,768]{1,0:T(8,128)(2,1)}, bf16[192,768]{1,0:T(8,128)(2,1)}, u32[]{:S(2)}, u32[]{:S(2)}) collective-permute-start(bf16[192,768]{1,0:T(8,128)(2,1)} %in_order.28), channel_id=1, source_target_pairs={{0,2},{2,4},{4,6},{6,0},{1,3},{3,5},{5,7},{7,1},{8,10},{10,12},{12... | collective-permute-start | bytes 884744 | tf_op jit(solution)/shard_map/ppermute | solution.py:34
  101.9 43.3 %collective-permute-start.17 = (bf16[192,768]{1,0:T(8,128)(2,1)}, bf16[192,768]{1,0:T(8,128)(2,1)}, u32[]{:S(2)}, u32[]{:S(2)}) collective-permute-start(bf16[192,768]{1,0:T(8,128)(2,1)} %in_order.28), channel_id=1, source_target_pairs={{0,4},{2,6},{4,0},{6,2},{1,5},{3,7},{5,1},{7,3},{8,12},{10,14},{12... | collective-permute-start | bytes 884744 | tf_op jit(solution)/shard_map/ppermute | solution.py:34
  101.9 43.3 %collective-permute-start.18 = (bf16[192,768]{1,0:T(8,128)(2,1)}, bf16[192,768]{1,0:T(8,128)(2,1)}, u32[]{:S(2)}, u32[]{:S(2)}) collective-permute-start(bf16[192,768]{1,0:T(8,128)(2,1)} %in_order.28), channel_id=1, source_target_pairs={{0,6},{2,0},{4,2},{6,4},{1,7},{3,1},{5,3},{7,5},{8,14},{10,8},{12,... | collective-permute-start | bytes 884744 | tf_op jit(solution)/shard_map/ppermute | solution.py:34
  106.4 71.2 %all-to-all-start.1 = ((bf16[4,192,768]{2,1,0:T(8,128)(2,1)}), bf16[4,192,768]{2,1,0:T(8,128)(2,1)}, u32[]{:S(2)}, u32[]{:S(2)}) async-start(bf16[4,192,768]{2,1,0:T(8,128)(2,1)} %broadcast_in_dim.84), calls=%async_computation.1 | async-start | bytes 2359296 | tf_op jit(solution)/shard_map/all_to_all | solution.py:44
  148.4 31.5 %collective-permute-start.19 = (bf16[4,192,768]{2,1,0:T(8,128)(2,1)}, bf16[4,192,768]{2,1,0:T(8,128)(2,1)}, u32[]{:S(2)}, u32[]{:S(2)}) collective-permute-start(bf16[4,192,768]{2,1,0:T(8,128)(2,1)} %pad_maximum_fusion.4), channel_id=1, source_target_pairs={{0,1},{1,0},{2,3},{3,2},{4,5},{5,4},{6,7},{7,6},{8,9},{9,8},{10,11... | collective-permute-start | bytes 3538952 | tf_op jit(solution)/shard_map/ppermute | solution.py:34
  148.6 44.5 %collective-permute-start.24 = (bf16[512,1536]{1,0:T(8,128)(2,1)}, bf16[512,1536]{1,0:T(8,128)(2,1)}, u32[]{:S(2)}, u32[]{:S(2)}) collective-permute-start(bf16[512,1536]{1,0:T(8,128)(2,1)} %in_order.34), channel_id=1, source_target_pairs={{0,16},{16,0},{1,17},{17,1},{2,18},{18,2},{3,19},{19,3},{4,20},{20... | collective-permute-start | bytes 4718600 | tf_op jit(solution)/shard_map/ppermute | solution.py:34
  169.5 24.8 %collective-permute-start.20 = (bf16[4,144,768]{2,1,0:T(8,128)(2,1)}, bf16[4,144,768]{2,1,0:T(8,128)(2,1)}, u32[]{:S(2)}, u32[]{:S(2)}) collective-permute-start(bf16[4,144,768]{2,1,0:T(8,128)(2,1)} %pad_maximum_fusion.3), channel_id=1, source_target_pairs={{0,1},{1,2},{2,3},{3,4},{4,5},{5,6},{6,7},{8,9},{9,10},{10,11},{11... | collective-permute-start | bytes 2654216 | tf_op jit(solution)/shard_map/ppermute | solution.py:40
  173.2 23.2 %collective-permute-start.21 = (bf16[4,144,768]{2,1,0:T(8,128)(2,1)}, bf16[4,144,768]{2,1,0:T(8,128)(2,1)}, u32[]{:S(2)}, u32[]{:S(2)}) collective-permute-start(bf16[4,144,768]{2,1,0:T(8,128)(2,1)} %pad_maximum_fusion.3), channel_id=1, source_target_pairs={{0,2},{1,3},{2,4},{3,5},{4,6},{5,7},{8,10},{9,11},{10,12},{11,13},... | collective-permute-start | bytes 2654216 | tf_op jit(solution)/shard_map/ppermute | solution.py:40
  177.6 40.8 %collective-permute-start.22 = (bf16[4,192,768]{2,1,0:T(8,128)(2,1)}, bf16[4,192,768]{2,1,0:T(8,128)(2,1)}, u32[]{:S(2)}, u32[]{:S(2)}) collective-permute-start(bf16[4,192,768]{2,1,0:T(8,128)(2,1)} %in_order.33), channel_id=1, source_target_pairs={{0,1},{1,0},{2,3},{3,2},{4,5},{5,4},{6,7},{7,6},{8,9},{9,8},{10,11... | collective-permute-start | bytes 3538952 | tf_op jit(solution)/shard_map/ppermute | solution.py:34
  179.9 54.7 %collective-permute-start.23 = (bf16[512,1536]{1,0:T(8,128)(2,1)}, bf16[512,1536]{1,0:T(8,128)(2,1)}, u32[]{:S(2)}, u32[]{:S(2)}) collective-permute-start(bf16[512,1536]{1,0:T(8,128)(2,1)} %in_order.34), channel_id=1, source_target_pairs={{0,8},{8,0},{1,9},{9,1},{2,10},{10,2},{3,11},{11,3},{4,12},{12,4},... | collective-permute-start | bytes 4718600 | tf_op jit(solution)/shard_map/ppermute | solution.py:34
  193.0 41.5 %collective-permute-start.25 = (bf16[512,1536]{1,0:T(8,128)(2,1)}, bf16[512,1536]{1,0:T(8,128)(2,1)}, u32[]{:S(2)}, u32[]{:S(2)}) collective-permute-start(bf16[512,1536]{1,0:T(8,128)(2,1)} %in_order.35), channel_id=1, source_target_pairs={{0,8},{8,0},{1,9},{9,1},{2,10},{10,2},{3,11},{11,3},{4,12},{12,4},... | collective-permute-start | bytes 4718600 | tf_op jit(solution)/shard_map/ppermute | solution.py:34
  284.1 40.8 %collective-permute-start.30 = (bf16[4,144,768]{2,1,0:T(8,128)(2,1)}, bf16[4,144,768]{2,1,0:T(8,128)(2,1)S(1)}, u32[]{:S(2)}, u32[]{:S(2)}) collective-permute-start(bf16[4,144,768]{2,1,0:T(8,128)(2,1)} %pad_maximum_fusion.2), channel_id=1, source_target_pairs={{1,0},{2,1},{3,2},{4,3},{5,4},{6,5},{7,6},{9,8},{10,9},{11,10},{12... | collective-permute-start | bytes 2654216 | tf_op jit(solution)/shard_map/ppermute | solution.py:40
  285.4 43.5 %collective-permute-start.31 = (bf16[4,144,768]{2,1,0:T(8,128)(2,1)}, bf16[4,144,768]{2,1,0:T(8,128)(2,1)}, u32[]{:S(2)}, u32[]{:S(2)}) collective-permute-start(bf16[4,144,768]{2,1,0:T(8,128)(2,1)} %pad_maximum_fusion.2), channel_id=1, source_target_pairs={{2,0},{3,1},{4,2},{5,3},{6,4},{7,5},{10,8},{11,9},{12,10},{13,11},... | collective-permute-start | bytes 2654216 | tf_op jit(solution)/shard_map/ppermute | solution.py:40
  315.0 55.5 %collective-permute-start.32 = (bf16[4,192,1536]{2,1,0:T(8,128)(2,1)}, bf16[4,192,1536]{2,1,0:T(8,128)(2,1)}, u32[]{:S(2)}, u32[]{:S(2)}) collective-permute-start(bf16[4,192,1536]{2,1,0:T(8,128)(2,1)} %slice.367), channel_id=1, source_target_pairs={{0,1},{1,0},{2,3},{3,2},{4,5},{5,4},{6,7},{7,6},{8,9},{9,8},{10,11... | collective-permute-start | bytes 7077896 | tf_op jit(solution)/shard_map/ppermute | solution.py:34
  324.5 58.7 %collective-permute-start.28 = (bf16[2,512,1536]{2,1,0:T(8,128)(2,1)}, bf16[2,512,1536]{2,1,0:T(8,128)(2,1)}, u32[]{:S(2)}, u32[]{:S(2)}) collective-permute-start(bf16[2,512,1536]{2,1,0:T(8,128)(2,1)} %convolution_convert_fusion), channel_id=1, source_target_pairs={{0,8},{8,0},{1,9},{9,1},{2,10},{10,2},{3,11},{11,3},{4,12},{12,4},... | collective-permute-start | bytes 9437192 | tf_op jit(solution)/shard_map/ppermute | solution.py:34
  366.0 58.6 %collective-permute-start.34 = (bf16[4,4,48,384]{3,2,1,0:T(8,128)(2,1)}, bf16[4,4,48,384]{3,2,1,0:T(8,128)(2,1)}, u32[]{:S(2)}, u32[]{:S(2)}) collective-permute-start(bf16[4,4,48,384]{3,2,1,0:T(8,128)(2,1)} %get-tuple-element.63), channel_id=1, source_target_pairs={{0,1},{1,0},{2,3},{3,2},{4,5},{5,4},{6,7},{7,6},{8,9},{9,8},{10,11... | collective-permute-start | bytes 1769480 | tf_op jit(solution)/shard_map/ppermute | solution.py:34
  374.2 60.1 %all-to-all-start.2 = ((bf16[4,192,1536]{2,1,0:T(8,128)(2,1)}), bf16[4,192,1536]{2,1,0:T(8,128)(2,1)}, u32[]{:S(2)}, u32[]{:S(2)}) async-start(bf16[4,192,1536]{2,1,0:T(8,128)(2,1)} %add_convert_fusion.refs_18_), calls=%async_computation.2 | async-start | bytes 4718592 | tf_op jit(solution)/shard_map/all_to_all | solution.py:44
  390.3 36.6 %collective-permute-start.29 = (bf16[512,1536]{1,0:T(8,128)(2,1)}, bf16[512,1536]{1,0:T(8,128)(2,1)}, u32[]{:S(2)}, u32[]{:S(2)}) collective-permute-start(bf16[512,1536]{1,0:T(8,128)(2,1)} %fusion.20.refs_19_), channel_id=1, source_target_pairs={{0,16},{16,0},{1,17},{17,1},{2,18},{18,2},{3,19},{19,3},{4,20},{20... | collective-permute-start | bytes 4718600 | tf_op jit(solution)/shard_map/ppermute | solution.py:34
  422.8 28.8 %collective-permute-start.38 = (f32[160,128]{1,0:T(8,128)S(1)}, f32[160,128]{1,0:T(8,128)S(1)}, u32[]{:S(2)}, u32[]{:S(2)}) collective-permute-start(f32[160,128]{1,0:T(8,128)S(1)} %fusion.23.refs_0_), channel_id=1, source_target_pairs={{0,16},{16,0},{1,17},{17,1},{2,18},{18,2},{3,19},{19,3},{4,20},{20... | collective-permute-start | bytes 245768 | tf_op jit(solution)/shard_map/ppermute | solution.py:131
  437.5 33.6 %all-to-all-start.3 = ((bf16[4,4,48,384]{3,2,1,0:T(8,128)(2,1)}), bf16[4,4,48,384]{3,2,1,0:T(8,128)(2,1)S(1)}, u32[]{:S(2)}, u32[]{:S(2)}) async-start(bf16[4,4,48,384]{3,2,1,0:T(8,128)(2,1)} %in_order.39), calls=%async_computation.3 | async-start | bytes 1179648 | tf_op jit(solution)/shard_map/all_to_all | solution.py:44
  465.1 27.3 %collective-permute-start.35 = (bf16[4,4,48,768]{3,2,1,0:T(8,128)(2,1)}, bf16[4,4,48,768]{3,2,1,0:T(8,128)(2,1)}, u32[]{:S(2)}, u32[]{:S(2)}) collective-permute-start(bf16[4,4,48,768]{3,2,1,0:T(8,128)(2,1)} %slice.376), channel_id=1, source_target_pairs={{0,1},{1,0},{2,3},{3,2},{4,5},{5,4},{6,7},{7,6},{8,9},{9,8},{10,11... | collective-permute-start | bytes 3538952 | tf_op jit(solution)/shard_map/ppermute | solution.py:34
  468.7 20.2 %collective-permute-start.40 = (f32[160,128]{1,0:T(8,128)S(1)}, f32[160,128]{1,0:T(8,128)S(1)}, u32[]{:S(2)}, u32[]{:S(2)}) collective-permute-start(f32[160,128]{1,0:T(8,128)S(1)} %add.259.refs_0_), channel_id=1, source_target_pairs={{0,4},{2,6},{4,0},{6,2},{1,5},{3,7},{5,1},{7,3},{8,12},{10,14},{12... | collective-permute-start | bytes 245768 | tf_op jit(solution)/shard_map/ppermute | solution.py:131
  472.0 23.0 %all-to-all-start.4 = ((bf16[4,48,1152]{2,1,0:T(8,128)(2,1)}), bf16[4,48,1152]{2,1,0:T(8,128)(2,1)S(1)}, u32[]{:S(2)}, u32[]{:S(2)}) async-start(bf16[4,48,1152]{2,1,0:T(8,128)(2,1)} %pad_maximum_fusion.8), calls=%async_computation.4 | async-start | bytes 884736 | tf_op jit(solution)/shard_map/all_to_all | solution.py:44
  512.9 35.4 %all-to-all-start.5 = ((bf16[4,4,48,768]{3,2,1,0:T(8,128)(2,1)}), bf16[4,4,48,768]{3,2,1,0:T(8,128)(2,1)}, u32[]{:S(2)}, u32[]{:S(2)}) async-start(bf16[4,4,48,768]{3,2,1,0:T(8,128)(2,1)} %in_order.42), calls=%async_computation.5 | async-start | bytes 2359296 | tf_op jit(solution)/shard_map/all_to_all | solution.py:44
  519.0 37.9 %collective-permute-start.37 = (bf16[528,1536]{1,0:T(8,128)(2,1)}, bf16[528,1536]{1,0:T(8,128)(2,1)}, u32[]{:S(2)}, u32[]{:S(2)}) collective-permute-start(bf16[528,1536]{1,0:T(8,128)(2,1)} %fusion.19.refs_2_), channel_id=1, source_target_pairs={{0,16},{16,0},{1,17},{17,1},{2,18},{18,2},{3,19},{19,3},{4,20},{20... | collective-permute-start | bytes 4866056 | tf_op jit(solution)/shard_map/ppermute | solution.py:34
  (90 other events, 890.0 us)
